TPU v7x, 256 devices: a whole 4x4x8 slice. The times are simulated.
256 devices in a mesh: dp: 4 (over y), fsdp: 64 (over x, z, core).
Axes of the slice: x: 4, y: 4, z: 8, core: 2. Of those that a mesh axis runs over, the one named last changes fastest.
Arguments:
- grads: bfloat16 [4, 256, 512, 512], P('dp', None, 'fsdp'), may hold values from -6 to 6
- left_factor: float32 [256, 512, 512], P(('dp', 'fsdp')), as said below
- right_factor: float32 [256, 512, 512], P(('dp', 'fsdp')), as said below
- left_root: float32 [256, 512, 512], P(('dp', 'fsdp')), as said below
- right_root: float32 [256, 512, 512], P(('dp', 'fsdp')), as said below
- block_of_slot: int32 [256], replicated, may hold values from 0 to 255, as said below
- refresh: int32 [1], replicated, may hold values from 0 to 15
Outputs:
- new_left_factor: float32 [256, 512, 512], P(('dp', 'fsdp'))
- new_right_factor: float32 [256, 512, 512], P(('dp', 'fsdp'))
- new_left_root: float32 [256, 512, 512], P(('dp', 'fsdp'))
- new_right_root: float32 [256, 512, 512], P(('dp', 'fsdp'))
- update: bfloat16 [256, 512, 512], P(None, 'fsdp')
Inputs may be any that keep to these rules, and one draw needn't show every extreme that they name: A permutation of the block numbers with block_of_slot[s] mod 16 equal to s mod 16 for every slot s. `left_factor`: every block is symmetric positive definite. `right_factor`: every block is symmetric positive definite. `left_root`: every block is symmetric. `right_root`: every block is symmetric.
All inputs are finite; a program needn't handle non-finite values.
Results may differ from a plain program's by a relative error of at most 0.015.
Values may be sent and summed in bfloat16 or wider, within the bound.
No kernel may reach another device: no remote copies, remote signals or barrier semaphores. Data moves between devices by JAX's collectives and lax.ppermute only.
A program may use at most 64 MiB of HBM per device.

v0:
```python
import jax
import jax.numpy as jnp
from jax import lax
from jax.sharding import PartitionSpec as P

ITERS = 2


root_power = 4.0
refresh_period = 16
exact = lax.Precision.HIGHEST


def product(first_matrix, second_matrix):
    return jnp.dot(first_matrix, second_matrix, precision=exact, preferred_element_type=jnp.float32)


def inverse_root(factor):
    block_order = factor.shape[0]
    identity = jnp.eye(block_order, dtype=jnp.float32)
    scaling = (1.0 + root_power) / (2.0 * jnp.sqrt(jnp.sum(factor * factor)))
    approx = identity * scaling ** (1.0 / root_power)
    coupled = factor * scaling
    for iteration in range(ITERS):
        middle = ((root_power + 1.0) * identity - coupled) / root_power
        approx = product(approx, middle)
        square = product(middle, middle)
        coupled = product(product(square, square), coupled)
    return approx


def refreshed(factor, previous):
    return inverse_root(factor)


def kept(factor, previous):
    return previous


def batched(pattern, first_stack, second_stack):
    return jnp.einsum(
        pattern, first_stack, second_stack, precision=exact, preferred_element_type=jnp.float32
    )


def per_device(grads, left_factor, right_factor, left_root, right_root, block_of_slot, refresh):
    data_count = lax.axis_size("dp")
    shard_count = lax.axis_size("fsdp")
    local = grads[0]
    blocks_dev = left_factor.shape[0]
    piece_rows = local.shape[1]
    block_order = local.shape[2]
    ordered = jnp.take(local, block_of_slot, axis=0).reshape(
        data_count, shard_count, blocks_dev, piece_rows, block_order
    )
    moved = lax.all_to_all(ordered, "fsdp", split_axis=1, concat_axis=3, tiled=True)
    owned = lax.psum_scatter(
        moved.astype(jnp.float32).astype(jnp.bfloat16), "dp", scatter_dimension=0, tiled=True
    ).astype(jnp.float32)
    grad_blocks = owned.reshape(blocks_dev, block_order, block_order)
    device_index = lax.axis_index("dp") * shard_count + lax.axis_index("fsdp")
    own_blocks = lax.dynamic_slice_in_dim(block_of_slot, device_index * blocks_dev, blocks_dev)
    own_flags = own_blocks % refresh_period == refresh[0]
    left_new = left_factor + batched("kij,klj->kil", grad_blocks, grad_blocks) / block_order
    right_new = right_factor + batched("kji,kjl->kil", grad_blocks, grad_blocks) / block_order
    left_now = jnp.stack([lax.cond(own_flags[0], refreshed, kept, left_new[0], left_root[0])])
    right_now = jnp.stack([lax.cond(own_flags[0], refreshed, kept, right_new[0], right_root[0])])
    mixed = batched("kij,kjl->kil", left_now, grad_blocks)
    update_own = batched("kij,kjl->kil", mixed, right_now).astype(jnp.bfloat16)
    spread_rows = lax.all_to_all(
        update_own.reshape(1, blocks_dev, block_order, block_order),
        "fsdp",
        split_axis=2,
        concat_axis=0,
        tiled=True,
    )
    every_slot = lax.all_gather(spread_rows, "dp", axis=0, tiled=True).reshape(
        -1, piece_rows, block_order
    )
    updates = jnp.zeros_like(every_slot).at[block_of_slot].set(every_slot)
    return (left_new, right_new, left_now, right_now, updates)


def solution(mesh):
    in_specs = (
        P("dp", None, "fsdp", None),
        P(("dp", "fsdp"), None, None),
        P(("dp", "fsdp"), None, None),
        P(("dp", "fsdp"), None, None),
        P(("dp", "fsdp"), None, None),
        P(),
        P(),
    )
    out_specs = (
        P(("dp", "fsdp"), None, None),
        P(("dp", "fsdp"), None, None),
        P(("dp", "fsdp"), None, None),
        P(("dp", "fsdp"), None, None),
        P(None, "fsdp", None),
    )
    return jax.shard_map(
        per_device, mesh=mesh, in_specs=in_specs, out_specs=out_specs, check_vma=False
    )
```

profile of v0, /device:TPU:1, one launch (start us, length us, event | category | flops | bytes accessed | tf_op | source)
XLA Modules:
  0.0 262.7 jit_solution(2366613124541961632)
XLA Ops:
  7.2 0.0 copy-start
  7.2 0.0 copy-start.2
  7.2 0.0 copy-start.6
  7.2 0.0 reduce-scatter.2.cloned.1.call-start
  7.2 2.4 copy.41
  9.7 0.0 copy-done.2
  9.7 1.0 copy.42
  10.7 0.0 copy-done.6
  10.7 0.1 broadcast_in_dim.18
  10.8 0.0 copy-done
  10.8 2.1 gather_fusion
  12.9 1.8 broadcast_select_fusion
  14.6 0.3 copy.16
  14.9 64.0 %all_to_all.24 = bf16[4,64,1,8,512]{4,3,0,2,1:T(8,128)(2,1)S(1)} all-to-all(bf16[4,64,1,8,512]{4,3,0,2,1:T(8,128)(2,1)S(1)} %copy.16), channel_id=1, replica_groups=mesh['dp'=4,'fsdp'=64] {'fsdp'}, dimensions={1} | all-to-all | bytes 4194304 | tf_op jit(solution)/shard_map/all_to_all | solution.py:56
  79.0 1.5 copy.24
  80.5 0.0 copy-start.3
  80.5 0.0 reduce-scatter.2.cloned.1.call-update
  80.5 0.0 all-gather.2.cloned.1.call-start
  80.6 0.6 dynamic_slice.3
  83.8 25.8 %reduce-scatter.2.cloned.1.call-done = bf16[1,1,1,512,512]{4,3,0,2,1:T(8,128)(2,1)} async-done(((bf16[4,1,1,512,512]{4,3,0,2,1:T(8,128)(2,1)}), bf16[1,1,1,512,512]{4,3,0,2,1:T(8,128)(2,1)}) %reduce-scatter.2.cloned.1.call-update) | async-done | bytes 524304 | tf_op jit(solution)/shard_map/reduce_scatter | solution.py:57
  109.6 0.0 copy-done.3
  109.6 2.6 %fusion.65 = f32[1,512,512]{2,1,0:T(8,128)} fusion(f32[1,512,512]{2,1,0:T(8,128)S(1)} %copy-done.3, bf16[1,1,1,512,512]{4,3,0,2,1:T(8,128)(2,1)} %reduce-scatter.2.cloned.1.call-done), kind=kOutput, calls=%fused_computation.79 | convolution fusion | flops 268959744 | bytes 2621440 | tf_op jit(solution)/shard_map/kji,kjl->kil/dot_general | solution.py:41
  112.2 0.0 copy-start.1
  112.2 1.3 conditional.3
  112.2 1.3 copy.32
  113.5 0.1 copy-done.1
  113.6 0.0 copy-start.4
  113.6 3.0 %fusion.64 = f32[1,512,512]{2,1,0:T(8,128)} fusion(f32[1,512,512]{2,1,0:T(8,128)} %param.12, bf16[1,1,1,512,512]{4,3,0,2,1:T(8,128)(2,1)S(1)} %copy-done.1), kind=kOutput, calls=%fused_computation.78 | convolution fusion | flops 268959744 | bytes 2621440 | tf_op jit(solution)/shard_map/kij,klj->kil/dot_general | solution.py:41
  116.6 0.0 copy-done.4
  116.7 1.2 conditional.2
  116.7 1.2 copy.28
  117.9 0.0 copy-start.5
  117.9 1.0 copy-done.5
  118.8 2.2 fusion.67
  121.1 3.1 %fusion.66 = bf16[1,1,512,512]{3,2,1,0:T(8,128)(2,1)S(1)} fusion(f32[512,512]{1,0:T(8,128)S(1)} %fusion.67, f32[512,512]{1,0:T(8,128)} %get-tuple-element.26), kind=kOutput, calls=%fused_computation.81 | convolution fusion | flops 1610874880 | bytes 2621440 | tf_op jit(solution)/shard_map/kij,kjl->kil/dot_general | solution.py:41
  124.1 0.8 copy.26
  125.0 0.5 broadcast.162
  125.5 4.6 %reduce.2 = bf16[512,512]{1,0:T(8,128)(2,1)} reduce(bf16[512,1,1,512]{3,2,1,0:T(2,128)(2,1)S(1)} %bitcast.75, bf16[]{:T(256)} %broadcast.162), dimensions={1,2}, to_apply=%bitcast.69.reduce_sub_computation | reduce | bytes 1048578
  130.1 1.2 reshape.129
  131.3 59.6 %all_to_all.25 = bf16[64,2,2048]{2,1,0:T(2,128)(2,1)} all-to-all(bf16[64,2,2048]{2,1,0:T(2,128)(2,1)S(1)} %reshape.129), channel_id=1, replica_groups=mesh['dp'=4,'fsdp'=64] {'fsdp'}, dimensions={0} | all-to-all | bytes 1048576 | tf_op jit(solution)/shard_map/all_to_all | solution.py:70
  190.9 3.6 %reshape.130 = bf16[512,1,1,512]{3,2,1,0:T(2,128)(2,1)S(1)} reshape(bf16[64,2,2048]{2,1,0:T(2,128)(2,1)} %all_to_all.25) | data formatting | bytes 1048576
  194.6 0.9 copy.25
  195.5 0.0 all-gather.2.cloned.1.call-update
  195.5 28.9 %all-gather.2.cloned.1.call-done = bf16[256,1,8,512]{3,2,1,0:T(8,128)(2,1)} async-done(((bf16[64,1,8,512]{3,2,1,0:T(8,128)(2,1)}), bf16[256,1,8,512]{3,2,1,0:T(8,128)(2,1)}) %all-gather.2.cloned.1.call-update) | async-done | bytes 2097168 | tf_op jit(solution)/shard_map/all_gather | solution.py:77
  224.4 1.5 broadcast_in_dim.22
  225.9 29.9 %scatter_fusion = bf16[256,8,512]{2,1,0:T(8,128)(2,1)} fusion(bf16[256,8,512]{2,1,0:T(8,128)(2,1)} %broadcast_in_dim.22, s32[256]{0:T(256)S(1)} %compare_select_fusion, bf16[256,8,512]{2,1,0:T(8,128)(2,1)} %bitcast.77), kind=kCustom, calls=%fused_computation.1 | custom fusion | bytes 6292480 | tf_op jit(solution)/shard_map/scatter | solution.py:80
  (3 shorter events, 0.0 us)
Async XLA Ops:
  7.2 3.6 %copy-start = (bf16[1,256,8,512]{3,2,1,0:T(8,128)(2,1)S(1)}, bf16[1,256,8,512]{3,2,1,0:T(8,128)(2,1)}, u32[]{:S(2)}) copy-start(bf16[1,256,8,512]{3,2,1,0:T(8,128)(2,1)} %param.11) | copy-start | bytes 6291460
  7.2 2.5 copy-start.2
  7.2 3.5 %copy-start.6 = (s32[256]{0:T(256)S(1)}, s32[256]{0:T(256)}, u32[]{:S(2)}) copy-start(s32[256]{0:T(256)} %param.16) | copy-start | bytes 3076
  7.2 102.4 %reduce-scatter.2.cloned.1.call-start = ((), (), s32[]{:S(2)}) async-start(), calls=%async_computation.3 | async-start | bytes 2621440 | tf_op jit(solution)/shard_map/reduce_scatter | solution.py:57
  80.5 29.1 %copy-start.3 = (f32[1,512,512]{2,1,0:T(8,128)S(1)}, f32[1,512,512]{2,1,0:T(8,128)}, u32[]{:S(2)}) copy-start(f32[1,512,512]{2,1,0:T(8,128)} %param.13) | copy-start | bytes 3145732
  80.5 143.9 %all-gather.2.cloned.1.call-start = ((), (), s32[]{:S(2)}) async-start(), calls=%async_computation.4 | async-start | bytes 2621440 | tf_op jit(solution)/shard_map/all_gather | solution.py:77
  112.2 1.4 copy-start.1
  113.6 3.1 %copy-start.4 = (f32[1,512,512]{2,1,0:T(8,128)}, f32[1,512,512]{2,1,0:T(8,128)S(1)}, u32[]{:S(2)}) copy-start(f32[1,512,512]{2,1,0:T(8,128)S(1)} %get-tuple-element.21) | copy-start | bytes 3145732
  117.9 1.0 copy-start.5
Sparse Core Ops, SparseCore 0:
  80.6 28.9 reduce-scatter.1
  195.6 28.7 all-gather.1
where the time goes:
time: 264 us; the launch traced here: 263 us
  blocking collectives  124 us (47%)
  waiting for transfers between devices  54.8 us (21%)
  local copies, waits for them, and re-layouts  50.1 us (19%)
  between operations  16.7 us (6%)
  matrix products  11 us (4%)
  other arithmetic  6.36 us (2%)
    all_to_all x1, blocking collectives, per_device(): lax.all_to_all(ordered, 'fsdp', split_axis=1, concat_axis=3, tiled=True)  64 us
    all_to_all x1, blocking collectives, per_device(): lax.all_to_all(update_own.reshape(1, blocks_dev, block_order, block_order...  59.6 us
    scatter x1, local copies, waits for them, and re-layouts, per_device(): updates = jnp.zeros_like(every_slot).at[block_of_slot].set(every_slot)  29.9 us
    all_gather x1, waiting for transfers between devices, per_device(): lax.all_gather(spread_rows, 'dp', axis=0, tiled=True)  28.9 us
    reduce_scatter x1, waiting for transfers between devices, per_device(): lax.psum_scatter(moved.astype(jnp.float32).astype(jnp.bfloat16), 'dp', sc...  25.8 us
    dot_general x4, matrix products, batched(): jnp.einsum(pattern, first_stack, second_stack, precision=exact, preferred...  11 us
    unnamed x20, local copies, waits for them, and re-layouts  10.8 us
  transfers between devices with their start and end apart: 2, of which 2 were waited for; matrix products, arithmetic and copies ran while one was open for 0% of the time, Pallas kernels for 0%

commit v1 on v0

v1 whole, which is shorter than its diff:
```python
import functools

import jax
import jax.numpy as jnp
from jax import lax
from jax.experimental import pallas as pl
from jax.experimental.pallas import tpu as pltpu
from jax.sharding import PartitionSpec as P

ITERS = 2
REFRESH_PERIOD = 16
N_DP = 4

VMEM = pltpu.VMEM
SMEM = pltpu.SMEM


def bf16_dot(a, b, dims=((1,), (0,))):
    return lax.dot_general(
        a.astype(jnp.bfloat16),
        b.astype(jnp.bfloat16),
        (dims, ((), ())),
        preferred_element_type=jnp.float32,
    )


def take_kernel(index_ref, source_ref, out_ref):
    def body(slot, carry):
        out_ref[slot] = source_ref[index_ref[slot]]
        return carry

    lax.fori_loop(0, out_ref.shape[0], body, 0, unroll=8)


def take_blocks(index, source):
    return pl.pallas_call(
        take_kernel,
        out_shape=jax.ShapeDtypeStruct(source.shape, source.dtype),
        in_specs=[pl.BlockSpec(memory_space=SMEM), pl.BlockSpec(memory_space=VMEM)],
        out_specs=pl.BlockSpec(memory_space=VMEM),
        compiler_params=pltpu.CompilerParams(vmem_limit_bytes=16 * 2**20),
        name="order_blocks",
    )(index, source)


def spread_kernel(index_ref, start_ref, *refs):
    out_ref = refs[-1]
    for part, source_ref in enumerate(refs[:-1]):
        start = start_ref[part]

        def body(slot, carry):
            out_ref[index_ref[start + slot]] = source_ref[slot]
            return carry

        lax.fori_loop(0, source_ref.shape[0], body, 0, unroll=8)


def spread_blocks(index, starts, sources):
    rows, columns = sources[0].shape[1:]
    return pl.pallas_call(
        spread_kernel,
        out_shape=jax.ShapeDtypeStruct((index.shape[0], rows, columns), sources[0].dtype),
        in_specs=[pl.BlockSpec(memory_space=SMEM)] * 2
        + [pl.BlockSpec(memory_space=VMEM)] * len(sources),
        out_specs=pl.BlockSpec(memory_space=VMEM),
        compiler_params=pltpu.CompilerParams(vmem_limit_bytes=16 * 2**20),
        name="place_blocks",
    )(index, starts, *sources)


def inverse_root(factor):
    order = factor.shape[0]
    rows = lax.broadcasted_iota(jnp.int32, (order, order), 0)
    cols = lax.broadcasted_iota(jnp.int32, (order, order), 1)
    scaling = 2.5 / jnp.sqrt(jnp.sum(factor * factor, keepdims=True))
    root_scale = jnp.sqrt(jnp.sqrt(scaling))
    coupled = factor * scaling
    first = coupled * 0.25
    f_part = 2.5 * first - bf16_dot(first, first)
    h_part = 3.125 * f_part - bf16_dot(f_part, f_part)
    coupled = (1.5625 * 1.5625) * coupled - bf16_dot(h_part, coupled)
    second = coupled * 0.25
    total = bf16_dot(first, second) - 1.25 * (first + second)
    total = jnp.where(rows == cols, total + 1.5625, total)
    return total * root_scale


def owner_kernel(
    flag_ref, grad_ref, left_ref, right_ref, lroot_ref, rroot_ref,
    new_left_ref, new_right_ref, new_lroot_ref, new_rroot_ref, update_ref,
):
    order = grad_ref.shape[0]
    grad = grad_ref[...]
    new_left_ref[...] = left_ref[...] + bf16_dot(grad, grad, ((1,), (1,))) * (1.0 / order)
    new_right_ref[...] = right_ref[...] + bf16_dot(grad, grad, ((0,), (0,))) * (1.0 / order)

    @pl.when(flag_ref[0] != 0)
    def _():
        new_lroot_ref[...] = inverse_root(new_left_ref[...])
        new_rroot_ref[...] = inverse_root(new_right_ref[...])

    @pl.when(flag_ref[0] == 0)
    def _():
        new_lroot_ref[...] = lroot_ref[...]
        new_rroot_ref[...] = rroot_ref[...]

    mixed = bf16_dot(new_lroot_ref[...], grad)
    update_ref[...] = bf16_dot(mixed, new_rroot_ref[...]).astype(update_ref.dtype)


def owner_step(flag, grad, left, right, lroot, rroot):
    order = grad.shape[0]
    matrix = jax.ShapeDtypeStruct((order, order), jnp.float32)
    return pl.pallas_call(
        owner_kernel,
        out_shape=(matrix,) * 4 + (jax.ShapeDtypeStruct((order, order), jnp.bfloat16),),
        in_specs=[pl.BlockSpec(memory_space=SMEM)] + [pl.BlockSpec(memory_space=VMEM)] * 5,
        out_specs=(pl.BlockSpec(memory_space=VMEM),) * 5,
        compiler_params=pltpu.CompilerParams(vmem_limit_bytes=40 * 2**20),
        name="owner_step",
    )(flag, grad, left, right, lroot, rroot)


def per_device(grads, left_factor, right_factor, left_root, right_root, block_of_slot, refresh):
    shard_count = lax.axis_size("fsdp")
    data_count = lax.axis_size("dp")
    local = grads[0]
    blocks, piece_rows, order = local.shape
    me_dp, me_fsdp = lax.axis_index("dp"), lax.axis_index("fsdp")

    ordered = take_blocks(block_of_slot, local)
    ordered = ordered.reshape(data_count, blocks // data_count, piece_rows, order)
    replicas = lax.all_to_all(ordered, "dp", split_axis=0, concat_axis=0, tiled=True)
    summed = jnp.sum(replicas.astype(jnp.float32), axis=0).astype(jnp.bfloat16)
    grad = lax.all_to_all(summed, "fsdp", split_axis=0, concat_axis=0, tiled=True)
    grad = grad.reshape(order, order)

    own = lax.dynamic_slice_in_dim(block_of_slot, me_dp * shard_count + me_fsdp, 1)
    flag = (own % REFRESH_PERIOD == refresh).astype(jnp.int32)
    new_left, new_right, new_lroot, new_rroot, update = owner_step(
        flag, grad, left_factor[0], right_factor[0], left_root[0], right_root[0]
    )

    rows = update.reshape(shard_count, piece_rows, order)
    rows = lax.all_to_all(rows, "fsdp", split_axis=0, concat_axis=0, tiled=True)
    parts, starts = [rows], [me_dp * shard_count]
    for step in range(1, data_count):
        pairs = [(i, (i + step) % data_count) for i in range(data_count)]
        parts.append(lax.ppermute(rows, "dp", pairs))
        starts.append((me_dp + data_count - step) % data_count * shard_count)
    updates = spread_blocks(block_of_slot, jnp.stack(starts).astype(jnp.int32), parts)
    return new_left[None], new_right[None], new_lroot[None], new_rroot[None], updates


def solution(mesh):
    owned = P(("dp", "fsdp"), None, None)
    return jax.shard_map(
        per_device,
        mesh=mesh,
        in_specs=(P("dp", None, "fsdp", None), owned, owned, owned, owned, P(), P()),
        out_specs=(owned, owned, owned, owned, P(None, "fsdp", None)),
        check_vma=False,
    )
```

time: 264 us -> 130 us (0.49)
  blocking collectives: 124 us -> 51.8 us
  local copies, waits for them, and re-layouts: 50.1 us -> 5.31 us
  starting transfers between devices: 0.08 us -> 16.1 us
  waiting for transfers between devices: 54.8 us -> 39.4 us
  between operations: 16.7 us -> 3.28 us
  matrix products: 11 us -> 0 us
  Pallas kernels: 0 us -> 9.62 us
  other arithmetic: 6.36 us -> 3.07 us
    all_to_all x2, blocking collectives: 124 us -> 51.8 us  [the longest x1 29.7 us: per_device(): lax.all_to_all(ordered, 'dp', split_axis=0, concat_axis=0, tiled=True)]
    scatter x1 -> x0, local copies, waits for them, and re-layouts: 29.9 us -> none  [per_device(): updates = jnp.zeros_like(every_slot).at[block_of_slot].set(every_slot)]
    all_gather x1 -> x0, waiting for transfers between devices: 28.9 us -> none  [per_device(): lax.all_gather(spread_rows, 'dp', axis=0, tiled=True)]
    reduce_scatter x1 -> x0, waiting for transfers between devices: 25.8 us -> none  [per_device(): lax.psum_scatter(moved.astype(jnp.float32).astype(jnp.bfloat16), 'dp', sc...]
    ppermute x0 -> x3, waiting for transfers between devices: none -> 25.3 us  [per_device(): parts.append(lax.ppermute(rows, 'dp', pairs))]
    all_to_all x0 -> x1, waiting for transfers between devices: none -> 14.1 us  [per_device(): lax.all_to_all(summed, 'fsdp', split_axis=0, concat_axis=0, tiled=True)]
    all_to_all x0 -> x1, starting transfers between devices: none -> 14 us  [per_device(): lax.all_to_all(summed, 'fsdp', split_axis=0, concat_axis=0, tiled=True)]
    dot_general x4 -> x0, matrix products: 11 us -> none  [batched(): jnp.einsum(pattern, first_stack, second_stack, precision=exact, preferred...]
  transfers between devices with their start and end apart: 2 -> 4, of which waited for: 2 -> 4; matrix products, arithmetic and copies ran while one was open for 0% -> 1% of each run, Pallas kernels for 0% -> 0%
where the time goes in v1:
time: 130 us; the launch traced here: 129 us
  blocking collectives  51.8 us (40%)
  waiting for transfers between devices  39.4 us (30%)
  starting transfers between devices  16.1 us (12%)
  Pallas kernels  9.62 us (7%)
  local copies, waits for them, and re-layouts  5.31 us (4%)
  between operations  3.28 us (3%)
  other arithmetic  3.07 us (2%)
    all_to_all x1, blocking collectives, per_device(): lax.all_to_all(ordered, 'dp', split_axis=0, concat_axis=0, tiled=True)  29.7 us
    ppermute x3, waiting for transfers between devices, per_device(): parts.append(lax.ppermute(rows, 'dp', pairs))  25.3 us
    all_to_all x1, blocking collectives, per_device(): rows = lax.all_to_all(rows, 'fsdp', split_axis=0, concat_axis=0, tiled=True)  22.2 us
    all_to_all x1, waiting for transfers between devices, per_device(): lax.all_to_all(summed, 'fsdp', split_axis=0, concat_axis=0, tiled=True)  14.1 us
    all_to_all x1, starting transfers between devices, per_device(): lax.all_to_all(summed, 'fsdp', split_axis=0, concat_axis=0, tiled=True)  14 us
    pallas_call x1, Pallas kernels, owner_step(): pl.pallas_call(owner_kernel, out_shape=(matrix,) * 4 + (jax.ShapeDtypeStr...  6.28 us
    unnamed x14, local copies, waits for them, and re-layouts  4.72 us
    reduce_sum x1, other arithmetic, per_device(): summed = jnp.sum(replicas.astype(jnp.float32), axis=0).astype(jnp.bfloat16)  2.99 us
  transfers between devices with their start and end apart: 4, of which 4 were waited for; matrix products, arithmetic and copies ran while one was open for 1% of the time, Pallas kernels for 0%

profile of v1, /device:TPU:1, one launch (start us, length us, event | category | flops | bytes accessed | tf_op | source)
XLA Modules:
  0.0 128.7 jit_solution(814889319261302328)
XLA Ops:
  0.6 0.0 copy-start
  0.6 1.6 %copy-done = bf16[1,256,8,512]{3,2,1,0:T(8,128)(2,1)S(1)} copy-done((bf16[1,256,8,512]{3,2,1,0:T(8,128)(2,1)S(1)}, bf16[1,256,8,512]{3,2,1,0:T(8,128)(2,1)}, u32[]{:S(2)}) %copy-start) | copy-done | bytes 2097176
  2.2 0.0 copy-start.5
  2.2 0.7 copy-done.5
  2.9 1.0 order_blocks.1
  3.9 29.7 %all_to_all.15 = bf16[4,64,8,512]{3,2,1,0:T(8,128)(2,1)} all-to-all(bf16[4,64,8,512]{3,2,1,0:T(8,128)(2,1)S(1)} %bitcast.16), channel_id=1, replica_groups=mesh['dp'=4,'fsdp'=64] {'dp'}, dimensions={0} | all-to-all | bytes 4194304 | tf_op jit(solution)/shard_map/all_to_all | solution.py:133
  33.5 0.0 copy-start.6
  33.6 0.0 copy-start.1
  33.6 0.0 copy-start.2
  33.6 3.0 %reduce_sum.12 = bf16[64,8,512]{2,1,0:T(8,128)(2,1)} reduce(bf16[4,64,8,512]{3,2,1,0:T(8,128)(2,1)} %all_to_all.15, bf16[]{:T(256)} %constant.63.clone.1), dimensions={0}, to_apply=%region_0.0 | reduce | flops 786432 | bytes 2621442 | tf_op jit(solution)/shard_map/reduce_sum | solution.py:134
  36.5 14.0 %all-to-all-start.1 = ((bf16[64,8,512]{2,1,0:T(8,128)(2,1)}), bf16[64,8,512]{2,1,0:T(8,128)(2,1)S(1)}, u32[]{:S(2)}, u32[]{:S(2)}) async-start(bf16[64,8,512]{2,1,0:T(8,128)(2,1)} %reduce_sum.12), calls=%async_computation.1 | async-start | bytes 1048576 | tf_op jit(solution)/shard_map/all_to_all | solution.py:135
  50.6 0.0 copy-done.6
  50.6 0.6 dynamic_slice.3
  53.8 14.1 %all-to-all-done.1 = bf16[64,8,512]{2,1,0:T(8,128)(2,1)S(1)} async-done(((bf16[64,8,512]{2,1,0:T(8,128)(2,1)}), bf16[64,8,512]{2,1,0:T(8,128)(2,1)S(1)}, u32[]{:S(2)}, u32[]{:S(2)}) %all-to-all-start.1) | async-done | bytes 524320 | tf_op jit(solution)/shard_map/all_to_all | solution.py:135
  67.9 0.0 copy-done.1
  67.9 0.0 copy-done.2
  67.9 0.0 copy-start.3
  67.9 1.2 copy-done.3
  69.1 0.0 copy-start.4
  69.1 1.2 copy-done.4
  70.3 6.3 %owner_step.1 = (f32[512,512]{1,0:T(8,128)}, f32[512,512]{1,0:T(8,128)}, f32[512,512]{1,0:T(8,128)}, f32[512,512]{1,0:T(8,128)}, bf16[512,512]{1,0:T(8,128)(2,1)S(1)}) custom-call(s32[1]{0:T(128)S(6)} %convert_element_type.2.flag_ref, bf16[512,512]{1,0:T(8,128)(2,1)S(1)} %bitcast.18, f32[512,512]{1,0:T(8,128)S(1)} %bitcast.19, f32[512,512]{1,0:T(8,128)S(1)} %bitcast.20, ...), custom_call_target="tpu_custom_call" | custom-call | tf_op jit(solution)/shard_map/owner_step/pallas_call | solution.py:114
  76.6 22.2 %all_to_all.16.refs_0_ = bf16[64,8,512]{2,1,0:T(8,128)(2,1)S(1)} all-to-all(bf16[64,8,512]{2,1,0:T(8,128)(2,1)S(1)} %bitcast.23), channel_id=1, replica_groups=mesh['dp'=4,'fsdp'=64] {'fsdp'}, dimensions={0} | all-to-all | bytes 1048576 | tf_op jit(solution)/shard_map/all_to_all | solution.py:145
  98.8 0.9 collective-permute-start.2
  99.7 1.2 collective-permute-start.1
  100.9 0.0 collective-permute-start
  100.9 0.1 pad_add_fusion.start_ref
  101.0 11.0 %collective-permute-done.2.refs_3_ = bf16[64,8,512]{2,1,0:T(8,128)(2,1)S(1)} collective-permute-done((bf16[64,8,512]{2,1,0:T(8,128)(2,1)S(1)}, bf16[64,8,512]{2,1,0:T(8,128)(2,1)S(1)}, u32[]{:S(2)}, u32[]{:S(2)}) %collective-permute-start.2) | collective-permute-done | bytes 524320 | tf_op jit(solution)/shard_map/ppermute | solution.py:149
  112.0 2.1 %collective-permute-done.1.refs_2_ = bf16[64,8,512]{2,1,0:T(8,128)(2,1)S(1)} collective-permute-done((bf16[64,8,512]{2,1,0:T(8,128)(2,1)S(1)}, bf16[64,8,512]{2,1,0:T(8,128)(2,1)S(1)}, u32[]{:S(2)}, u32[]{:S(2)}) %collective-permute-start.1) | collective-permute-done | bytes 524320 | tf_op jit(solution)/shard_map/ppermute | solution.py:149
  114.1 12.2 %collective-permute-done.refs_1_ = bf16[64,8,512]{2,1,0:T(8,128)(2,1)S(1)} collective-permute-done((bf16[64,8,512]{2,1,0:T(8,128)(2,1)S(1)}, bf16[64,8,512]{2,1,0:T(8,128)(2,1)S(1)}, u32[]{:S(2)}, u32[]{:S(2)}) %collective-permute-start) | collective-permute-done | bytes 524320 | tf_op jit(solution)/shard_map/ppermute | solution.py:149
  126.3 2.4 %place_blocks.1 = bf16[256,8,512]{2,1,0:T(8,128)(2,1)} custom-call(s32[256]{0:T(256)S(1)} %copy-done.6, s32[4]{0:T(128)S(1)} %pad_add_fusion.start_ref, bf16[64,8,512]{2,1,0:T(8,128)(2,1)S(1)} %all_to_all.16.refs_0_, bf16[64,8,512]{2,1,0:T(8,128)(2,1)S(1)} %collective-permute-done.refs_1_, bf16[64,8,512]{2,1,0:T(8,128)(2,1)S(1)} %collective-permute-done.1.refs_2_, ...), custom_call_target="tpu_custom_call" | custom-call | tf_op jit(solution)/shard_map/place_blocks/pallas_call | solution.py:60
Async XLA Ops:
  0.6 1.6 %copy-start = (bf16[1,256,8,512]{3,2,1,0:T(8,128)(2,1)S(1)}, bf16[1,256,8,512]{3,2,1,0:T(8,128)(2,1)}, u32[]{:S(2)}) copy-start(bf16[1,256,8,512]{3,2,1,0:T(8,128)(2,1)} %param.7) | copy-start | bytes 6291460
  2.2 0.7 copy-start.5
  33.5 17.0 %copy-start.6 = (s32[256]{0:T(256)S(1)}, s32[256]{0:T(256)}, u32[]{:S(2)}) copy-start(s32[256]{0:T(256)} %index_ref.3) | copy-start | bytes 3076
  33.6 34.3 %copy-start.1 = (f32[1,512,512]{2,1,0:T(8,128)S(1)}, f32[1,512,512]{2,1,0:T(8,128)}, u32[]{:S(2)}) copy-start(f32[1,512,512]{2,1,0:T(8,128)} %param.8) | copy-start | bytes 3145732
  33.6 34.3 %copy-start.2 = (f32[1,512,512]{2,1,0:T(8,128)S(1)}, f32[1,512,512]{2,1,0:T(8,128)}, u32[]{:S(2)}) copy-start(f32[1,512,512]{2,1,0:T(8,128)} %param.9) | copy-start | bytes 3145732
  36.5 31.3 %all-to-all-start.1 = ((bf16[64,8,512]{2,1,0:T(8,128)(2,1)}), bf16[64,8,512]{2,1,0:T(8,128)(2,1)S(1)}, u32[]{:S(2)}, u32[]{:S(2)}) async-start(bf16[64,8,512]{2,1,0:T(8,128)(2,1)} %reduce_sum.12), calls=%async_computation.1 | async-start | bytes 1048576 | tf_op jit(solution)/shard_map/all_to_all | solution.py:135
  67.9 1.2 copy-start.3
  69.1 1.2 copy-start.4
  98.8 13.2 %collective-permute-start.2 = (bf16[64,8,512]{2,1,0:T(8,128)(2,1)S(1)}, bf16[64,8,512]{2,1,0:T(8,128)(2,1)S(1)}, u32[]{:S(2)}, u32[]{:S(2)}) collective-permute-start(bf16[64,8,512]{2,1,0:T(8,128)(2,1)S(1)} %all_to_all.16.refs_0_), channel_id=1, source_target_pairs={{0,192},{64,0},{128,64},{192,128},{1,193},{65,1},{129,65},{193,129... | collective-permute-start | bytes 1572872 | tf_op jit(solution)/shard_map/ppermute | solution.py:149
  99.7 14.4 %collective-permute-start.1 = (bf16[64,8,512]{2,1,0:T(8,128)(2,1)S(1)}, bf16[64,8,512]{2,1,0:T(8,128)(2,1)S(1)}, u32[]{:S(2)}, u32[]{:S(2)}) collective-permute-start(bf16[64,8,512]{2,1,0:T(8,128)(2,1)S(1)} %all_to_all.16.refs_0_), channel_id=1, source_target_pairs={{0,128},{64,192},{128,0},{192,64},{1,129},{65,193},{129,1},{193,65... | collective-permute-start | bytes 1572872 | tf_op jit(solution)/shard_map/ppermute | solution.py:149
  100.9 25.4 %collective-permute-start = (bf16[64,8,512]{2,1,0:T(8,128)(2,1)S(1)}, bf16[64,8,512]{2,1,0:T(8,128)(2,1)S(1)}, u32[]{:S(2)}, u32[]{:S(2)}) collective-permute-start(bf16[64,8,512]{2,1,0:T(8,128)(2,1)S(1)} %all_to_all.16.refs_0_), channel_id=1, source_target_pairs={{0,64},{64,128},{128,192},{192,0},{1,65},{65,129},{129,193},{193,1... | collective-permute-start | bytes 1572872 | tf_op jit(solution)/shard_map/ppermute | solution.py:149

commit v2 on v1

--- a/solution.py
+++ b/solution.py
@@ -13,6 +13,7 @@
 
 VMEM = pltpu.VMEM
 SMEM = pltpu.SMEM
+HBM = pltpu.HBM
 
 
 def bf16_dot(a, b, dims=((1,), (0,))):
@@ -24,48 +25,103 @@
     )
 
 
-def take_kernel(index_ref, source_ref, out_ref):
-    def body(slot, carry):
-        out_ref[slot] = source_ref[index_ref[slot]]
-        return carry
-
-    lax.fori_loop(0, out_ref.shape[0], body, 0, unroll=8)
-
-
-def take_blocks(index, source):
-    return pl.pallas_call(
-        take_kernel,
-        out_shape=jax.ShapeDtypeStruct(source.shape, source.dtype),
-        in_specs=[pl.BlockSpec(memory_space=SMEM), pl.BlockSpec(memory_space=VMEM)],
-        out_specs=pl.BlockSpec(memory_space=VMEM),
-        compiler_params=pltpu.CompilerParams(vmem_limit_bytes=16 * 2**20),
-        name="order_blocks",
+def order_kernel(pieces, index_ref, source_ref, *refs):
+    outs, (index_smem, index_sem, sems) = refs[: len(pieces)], refs[len(pieces) :]
+    fetch = pltpu.make_async_copy(index_ref, index_smem, index_sem)
+    fetch.start()
+    me = lax.axis_index("dp")
+    fetch.wait()
+    for number, ((quarter, first), out_ref) in enumerate(zip(pieces, outs, strict=True)):
+        start = lax.rem(me + quarter, N_DP) * (index_ref.shape[0] // N_DP) + first
+
+        def body(slot, carry, out_ref=out_ref, number=number, start=start):
+            pltpu.make_async_copy(
+                source_ref.at[index_smem[start + slot]], out_ref.at[slot], sems.at[number]
+            ).start()
+            return carry
+
+        lax.fori_loop(0, out_ref.shape[0], body, 0, unroll=8)
+    for number, out_ref in enumerate(outs):
+        pltpu.make_async_copy(out_ref, out_ref, sems.at[number]).wait()
+
+
+def order_blocks(index, source, pieces, counts, name):
+    return pl.pallas_call(
+        functools.partial(order_kernel, pieces),
+        out_shape=[
+            jax.ShapeDtypeStruct((count, *source.shape[1:]), source.dtype) for count in counts
+        ],
+        in_specs=[pl.BlockSpec(memory_space=HBM)] * 2,
+        out_specs=[pl.BlockSpec(memory_space=pl.ANY)] * len(pieces),
+        scratch_shapes=[
+            pltpu.SMEM(index.shape, index.dtype),
+            pltpu.SemaphoreType.DMA,
+            pltpu.SemaphoreType.DMA((len(pieces),)),
+        ],
+        compiler_params=pltpu.CompilerParams(vmem_limit_bytes=4 * 2**20),
+        name=name,
     )(index, source)
 
 
-def spread_kernel(index_ref, start_ref, *refs):
+def place_kernel(pieces, index_ref, *refs):
     out_ref = refs[-1]
-    for part, source_ref in enumerate(refs[:-1]):
-        start = start_ref[part]
-
-        def body(slot, carry):
+    me = lax.axis_index("dp")
+    for (quarter, first), source_ref in zip(pieces, refs[:-1], strict=True):
+        start = lax.rem(me + quarter, N_DP) * (index_ref.shape[0] // N_DP) + first
+
+        def body(slot, carry, source_ref=source_ref, start=start):
             out_ref[index_ref[start + slot]] = source_ref[slot]
             return carry
 
         lax.fori_loop(0, source_ref.shape[0], body, 0, unroll=8)
 
 
-def spread_blocks(index, starts, sources):
+def place_blocks(index, sources, pieces):
     rows, columns = sources[0].shape[1:]
     return pl.pallas_call(
-        spread_kernel,
+        functools.partial(place_kernel, pieces),
         out_shape=jax.ShapeDtypeStruct((index.shape[0], rows, columns), sources[0].dtype),
-        in_specs=[pl.BlockSpec(memory_space=SMEM)] * 2
+        in_specs=[pl.BlockSpec(memory_space=SMEM)]
         + [pl.BlockSpec(memory_space=VMEM)] * len(sources),
         out_specs=pl.BlockSpec(memory_space=VMEM),
-        compiler_params=pltpu.CompilerParams(vmem_limit_bytes=16 * 2**20),
+        compiler_params=pltpu.CompilerParams(vmem_limit_bytes=8 * 2**20),
         name="place_blocks",
-    )(index, starts, *sources)
+    )(index, *sources)
+
+
+def add_kernel(first_ref, second_ref, out_ref):
+    total = first_ref[...].astype(jnp.float32) + second_ref[...].astype(jnp.float32)
+    out_ref[...] = total.astype(out_ref.dtype)
+
+
+def add_pieces(first, second):
+    return pl.pallas_call(
+        add_kernel,
+        out_shape=jax.ShapeDtypeStruct(first.shape, first.dtype),
+        in_specs=[pl.BlockSpec(memory_space=VMEM)] * 2,
+        out_specs=pl.BlockSpec(memory_space=VMEM),
+        compiler_params=pltpu.CompilerParams(vmem_limit_bytes=4 * 2**20),
+        name="add_pieces",
+    )(first, second)
+
+
+def total_kernel(mine_ref, comb_a_ref, raw_a_ref, comb_b_ref, raw_b_ref, out_ref):
+    half = comb_a_ref.shape[0]
+    for start, comb_ref, raw_ref in ((0, comb_a_ref, raw_a_ref), (half, comb_b_ref, raw_b_ref)):
+        part = pl.ds(start, half)
+        total = mine_ref[part].astype(jnp.float32) + comb_ref[...].astype(jnp.float32)
+        out_ref[part] = (total + raw_ref[...].astype(jnp.float32)).astype(out_ref.dtype)
+
+
+def total_pieces(*pieces):
+    return pl.pallas_call(
+        total_kernel,
+        out_shape=jax.ShapeDtypeStruct(pieces[0].shape, pieces[0].dtype),
+        in_specs=[pl.BlockSpec(memory_space=VMEM)] * 5,
+        out_specs=pl.BlockSpec(memory_space=VMEM),
+        compiler_params=pltpu.CompilerParams(vmem_limit_bytes=6 * 2**20),
+        name="total_pieces",
+    )(*pieces)
 
 
 def inverse_root(factor):
@@ -116,26 +172,44 @@
         out_shape=(matrix,) * 4 + (jax.ShapeDtypeStruct((order, order), jnp.bfloat16),),
         in_specs=[pl.BlockSpec(memory_space=SMEM)] + [pl.BlockSpec(memory_space=VMEM)] * 5,
         out_specs=(pl.BlockSpec(memory_space=VMEM),) * 5,
-        compiler_params=pltpu.CompilerParams(vmem_limit_bytes=40 * 2**20),
+        compiler_params=pltpu.CompilerParams(vmem_limit_bytes=24 * 2**20),
         name="owner_step",
     )(flag, grad, left, right, lroot, rroot)
 
 
 def per_device(grads, left_factor, right_factor, left_root, right_root, block_of_slot, refresh):
     shard_count = lax.axis_size("fsdp")
-    data_count = lax.axis_size("dp")
     local = grads[0]
     blocks, piece_rows, order = local.shape
-    me_dp, me_fsdp = lax.axis_index("dp"), lax.axis_index("fsdp")
-
-    ordered = take_blocks(block_of_slot, local)
-    ordered = ordered.reshape(data_count, blocks // data_count, piece_rows, order)
-    replicas = lax.all_to_all(ordered, "dp", split_axis=0, concat_axis=0, tiled=True)
-    summed = jnp.sum(replicas.astype(jnp.float32), axis=0).astype(jnp.bfloat16)
+    quarter, half = blocks // N_DP, blocks // N_DP // 2
+
+    def to_next(piece):
+        return lax.ppermute(piece, "dp", [(i, (i + 1) % N_DP) for i in range(N_DP)])
+
+    def to_prev(piece):
+        return lax.ppermute(piece, "dp", [(i, (i - 1) % N_DP) for i in range(N_DP)])
+
+    relay_a, relay_b = order_blocks(
+        block_of_slot, local, ((2, 0), (2, half)), (half, half), "order_relays"
+    )
+    own_a, own_b, raw_b, raw_a, mine = order_blocks(
+        block_of_slot,
+        local,
+        ((1, 0), (3, half), (1, half), (3, 0), (0, 0)),
+        (half, half, half, half, quarter),
+        "order_rest",
+    )
+    relayed_a, relayed_b = to_next(relay_a), to_prev(relay_b)
+    raw_a, raw_b = to_prev(raw_a), to_next(raw_b)
+    comb_a, comb_b = to_next(add_pieces(own_a, relayed_a)), to_prev(add_pieces(own_b, relayed_b))
+    summed = total_pieces(mine, comb_a, raw_a, comb_b, raw_b)
+
     grad = lax.all_to_all(summed, "fsdp", split_axis=0, concat_axis=0, tiled=True)
     grad = grad.reshape(order, order)
 
-    own = lax.dynamic_slice_in_dim(block_of_slot, me_dp * shard_count + me_fsdp, 1)
+    own = lax.dynamic_slice_in_dim(
+        block_of_slot, lax.axis_index("dp") * shard_count + lax.axis_index("fsdp"), 1
+    )
     flag = (own % REFRESH_PERIOD == refresh).astype(jnp.int32)
     new_left, new_right, new_lroot, new_rroot, update = owner_step(
         flag, grad, left_factor[0], right_factor[0], left_root[0], right_root[0]
@@ -143,12 +217,15 @@
 
     rows = update.reshape(shard_count, piece_rows, order)
     rows = lax.all_to_all(rows, "fsdp", split_axis=0, concat_axis=0, tiled=True)
-    parts, starts = [rows], [me_dp * shard_count]
-    for step in range(1, data_count):
-        pairs = [(i, (i + step) % data_count) for i in range(data_count)]
-        parts.append(lax.ppermute(rows, "dp", pairs))
-        starts.append((me_dp + data_count - step) % data_count * shard_count)
-    updates = spread_blocks(block_of_slot, jnp.stack(starts).astype(jnp.int32), parts)
+    rows_a, rows_b = rows[:half], rows[half:]
+    prev_a, next_b = to_next(rows_a), to_prev(rows_b)
+    prev_b, next_a = to_next(rows_b), to_prev(rows_a)
+    over_a, over_b = to_next(prev_a), to_prev(next_b)
+    updates = place_blocks(
+        block_of_slot,
+        (rows, prev_a, prev_b, next_a, next_b, over_a, over_b),
+        ((0, 0), (3, 0), (3, half), (1, 0), (1, half), (2, 0), (2, half)),
+    )
     return new_left[None], new_right[None], new_lroot[None], new_rroot[None], updates
 
 

time: 130 us -> 114 us (0.88)
  blocking collectives: 51.8 us -> 26.7 us
  starting transfers between devices: 16.1 us -> 28.2 us
  other arithmetic: 3.07 us -> 0 us
  Pallas kernels: 9.62 us -> 11.6 us
    all_to_all x1 -> x0, blocking collectives: 29.7 us -> none  [per_device(): lax.all_to_all(ordered, 'dp', split_axis=0, concat_axis=0, tiled=True)]
    ppermute x3 -> x12, starting transfers between devices: 2.07 us -> 14.2 us  [the longest x6 10.6 us: to_prev(): return lax.ppermute(piece, 'dp', [(i, (i - 1) % N_DP) for i in range(N_DP)])]
    pallas_call x2 -> x6, Pallas kernels: 3.34 us -> 8.72 us  [the longest x2 5.23 us: order_blocks(): pl.pallas_call(functools.partial(order_kernel, pieces), out_shape=[jax.Sh...]
    all_to_all x1, blocking collectives: 22.2 us -> 26.7 us  [per_device(): rows = lax.all_to_all(rows, 'fsdp', split_axis=0, concat_axis=0, tiled=True)]
    pallas_call x1, Pallas kernels: 6.28 us -> 2.89 us  [owner_step(): pl.pallas_call(owner_kernel, out_shape=(matrix,) * 4 + (jax.ShapeDtypeStr...]
    reduce_sum x1 -> x0, other arithmetic: 2.99 us -> none  [per_device(): summed = jnp.sum(replicas.astype(jnp.float32), axis=0).astype(jnp.bfloat16)]
    ppermute x3 -> x12, waiting for transfers between devices: 25.3 us -> 24.3 us  [the longest x6 14 us: to_next(): return lax.ppermute(piece, 'dp', [(i, (i + 1) % N_DP) for i in range(N_DP)])]
  transfers between devices with their start and end apart: 4 -> 13, of which waited for: 4 -> 8; matrix products, arithmetic and copies ran while one was open for 1% -> 1% of each run, Pallas kernels for 0% -> 3%
where the time goes in v2:
time: 114 us
  waiting for transfers between devices  38.5 us (34%)
  starting transfers between devices  28.2 us (25%)
  blocking collectives  26.7 us (23%)
  Pallas kernels  11.6 us (10%)
  local copies, waits for them, and re-layouts  5.35 us (5%)
  between operations  3.33 us (3%)
    all_to_all x1, blocking collectives, per_device(): rows = lax.all_to_all(rows, 'fsdp', split_axis=0, concat_axis=0, tiled=True)  26.7 us
    all_to_all x1, waiting for transfers between devices, per_device(): lax.all_to_all(summed, 'fsdp', split_axis=0, concat_axis=0, tiled=True)  14.1 us
    ppermute x6, waiting for transfers between devices, to_next(): return lax.ppermute(piece, 'dp', [(i, (i + 1) % N_DP) for i in range(N_DP)])  14 us
    all_to_all x1, starting transfers between devices, per_device(): lax.all_to_all(summed, 'fsdp', split_axis=0, concat_axis=0, tiled=True)  13.9 us
    ppermute x6, starting transfers between devices, to_prev(): return lax.ppermute(piece, 'dp', [(i, (i - 1) % N_DP) for i in range(N_DP)])  10.6 us
    ppermute x6, waiting for transfers between devices, to_prev(): return lax.ppermute(piece, 'dp', [(i, (i - 1) % N_DP) for i in range(N_DP)])  10.3 us
    pallas_call x2, Pallas kernels, order_blocks(): pl.pallas_call(functools.partial(order_kernel, pieces), out_shape=[jax.Sh...  5.23 us
    unnamed x14, local copies, waits for them, and re-layouts  4.73 us
  transfers between devices with their start and end apart: 13, of which 8 were waited for; matrix products, arithmetic and copies ran while one was open for 1% of the time, Pallas kernels for 3%

profile of v2, /device:TPU:1, one launch (start us, length us, event | category | flops | bytes accessed | tf_op | source)
XLA Modules:
  0.0 113.6 jit_solution(1708886763538883241)
XLA Ops:
  0.6 0.0 copy-start
  0.6 1.6 %copy-done = bf16[1,256,8,512]{3,2,1,0:T(8,128)(2,1)S(1)} copy-done((bf16[1,256,8,512]{3,2,1,0:T(8,128)(2,1)S(1)}, bf16[1,256,8,512]{3,2,1,0:T(8,128)(2,1)}, u32[]{:S(2)}) %copy-start) | copy-done | bytes 2097176
  2.2 0.0 copy-start.5
  2.2 0.7 copy-done.5
  2.9 1.6 %order_relays.1 = (bf16[32,8,512]{2,1,0:T(8,128)(2,1)S(1)}, bf16[32,8,512]{2,1,0:T(8,128)(2,1)S(1)}) custom-call(s32[256]{0:T(256)S(1)} %copy-done.5, bf16[256,8,512]{2,1,0:T(8,128)(2,1)S(1)} %bitcast.11), custom_call_target="tpu_custom_call" | custom-call | tf_op jit(solution)/shard_map/order_relays/pallas_call | solution.py:49
  4.5 2.2 %collective-permute-start = (bf16[32,8,512]{2,1,0:T(8,128)(2,1)S(1)}, bf16[32,8,512]{2,1,0:T(8,128)(2,1)S(1)}, u32[]{:S(2)}, u32[]{:S(2)}) collective-permute-start(bf16[32,8,512]{2,1,0:T(8,128)(2,1)S(1)} %get-tuple-element.19), channel_id=1, source_target_pairs={{0,64},{64,128},{128,192},{192,0},{1,65},{65,129},{129,193},{193,1... | collective-permute-start | bytes 786440 | tf_op jit(solution)/shard_map/ppermute | solution.py:187
  6.7 1.5 %collective-permute-start.3 = (bf16[32,8,512]{2,1,0:T(8,128)(2,1)S(1)}, bf16[32,8,512]{2,1,0:T(8,128)(2,1)S(1)}, u32[]{:S(2)}, u32[]{:S(2)}) collective-permute-start(bf16[32,8,512]{2,1,0:T(8,128)(2,1)S(1)} %get-tuple-element.22), channel_id=1, source_target_pairs={{0,192},{64,0},{128,64},{192,128},{1,193},{65,1},{129,65},{193,129... | collective-permute-start | bytes 786440 | tf_op jit(solution)/shard_map/ppermute | solution.py:190
  8.2 3.6 %order_rest.1 = (bf16[32,8,512]{2,1,0:T(8,128)(2,1)S(1)}, bf16[32,8,512]{2,1,0:T(8,128)(2,1)S(1)}, bf16[32,8,512]{2,1,0:T(8,128)(2,1)S(1)}, bf16[32,8,512]{2,1,0:T(8,128)(2,1)S(1)}, bf16[64,8,512]{2,1,0:T(8,128)(2,1)S(1)}) custom-call(s32[256]{0:T(256)S(1)} %copy-done.5, bf16[256,8,512]{2,1,0:T(8,128)(2,1)S(1)} %bitcast.12), custom_call_target="tpu_custom_call" | custom-call | tf_op jit(solution)/shard_map/order_rest/pallas_call | solution.py:49
  11.9 1.5 %collective-permute-start.2 = (bf16[32,8,512]{2,1,0:T(8,128)(2,1)S(1)}, bf16[32,8,512]{2,1,0:T(8,128)(2,1)S(1)}, u32[]{:S(2)}, u32[]{:S(2)}) collective-permute-start(bf16[32,8,512]{2,1,0:T(8,128)(2,1)S(1)} %get-tuple-element.20), channel_id=1, source_target_pairs={{0,192},{64,0},{128,64},{192,128},{1,193},{65,1},{129,65},{193,129... | collective-permute-start | bytes 786440 | tf_op jit(solution)/shard_map/ppermute | solution.py:190
  13.3 0.1 collective-permute-start.5
  13.4 0.0 collective-permute-done.second_ref
  13.4 0.1 add_pieces.2
  13.5 0.0 copy-start.6
  13.5 0.0 copy-start.1
  13.5 0.0 copy-start.2
  13.5 0.3 collective-permute-start.1
  13.9 0.0 collective-permute-done.3.second_ref
  13.9 0.1 add_pieces.3
  13.9 2.5 %collective-permute-start.4 = (bf16[32,8,512]{2,1,0:T(8,128)(2,1)S(1)}, bf16[32,8,512]{2,1,0:T(8,128)(2,1)S(1)}, u32[]{:S(2)}, u32[]{:S(2)}) collective-permute-start(bf16[32,8,512]{2,1,0:T(8,128)(2,1)S(1)} %add_pieces.3), channel_id=1, source_target_pairs={{0,192},{64,0},{128,64},{192,128},{1,193},{65,1},{129,65},{193,129... | collective-permute-start | bytes 786440 | tf_op jit(solution)/shard_map/ppermute | solution.py:190
  16.4 2.7 %collective-permute-done.2.raw_a_ref = bf16[32,8,512]{2,1,0:T(8,128)(2,1)S(1)} collective-permute-done((bf16[32,8,512]{2,1,0:T(8,128)(2,1)S(1)}, bf16[32,8,512]{2,1,0:T(8,128)(2,1)S(1)}, u32[]{:S(2)}, u32[]{:S(2)}) %collective-permute-start.2) | collective-permute-done | bytes 262176 | tf_op jit(solution)/shard_map/ppermute | solution.py:190
  19.1 1.7 %collective-permute-done.5.raw_b_ref = bf16[32,8,512]{2,1,0:T(8,128)(2,1)S(1)} collective-permute-done((bf16[32,8,512]{2,1,0:T(8,128)(2,1)S(1)}, bf16[32,8,512]{2,1,0:T(8,128)(2,1)S(1)}, u32[]{:S(2)}, u32[]{:S(2)}) %collective-permute-start.5) | collective-permute-done | bytes 262176 | tf_op jit(solution)/shard_map/ppermute | solution.py:187
  20.8 5.6 %collective-permute-done.1.comb_a_ref = bf16[32,8,512]{2,1,0:T(8,128)(2,1)S(1)} collective-permute-done((bf16[32,8,512]{2,1,0:T(8,128)(2,1)S(1)}, bf16[32,8,512]{2,1,0:T(8,128)(2,1)S(1)}, u32[]{:S(2)}, u32[]{:S(2)}) %collective-permute-start.1) | collective-permute-done | bytes 262176 | tf_op jit(solution)/shard_map/ppermute | solution.py:187
  26.4 0.0 collective-permute-done.4.comb_b_ref
  26.4 1.0 total_pieces.1
  27.4 13.9 %all-to-all-start = ((bf16[64,8,512]{2,1,0:T(8,128)(2,1)}), bf16[64,8,512]{2,1,0:T(8,128)(2,1)S(1)}, u32[]{:S(2)}, u32[]{:S(2)}) async-start(bf16[64,8,512]{2,1,0:T(8,128)(2,1)} %total_pieces.1), calls=%async_computation | async-start | bytes 1048576 | tf_op jit(solution)/shard_map/all_to_all | solution.py:207
  41.4 0.0 copy-done.6
  41.4 0.6 dynamic_slice.3
  44.6 14.1 %all-to-all-done = bf16[64,8,512]{2,1,0:T(8,128)(2,1)S(1)} async-done(((bf16[64,8,512]{2,1,0:T(8,128)(2,1)}), bf16[64,8,512]{2,1,0:T(8,128)(2,1)S(1)}, u32[]{:S(2)}, u32[]{:S(2)}) %all-to-all-start) | async-done | bytes 524320 | tf_op jit(solution)/shard_map/all_to_all | solution.py:207
  58.7 0.0 copy-done.1
  58.7 0.0 copy-done.2
  58.7 0.0 copy-start.3
  58.7 1.2 %copy-done.3 = f32[1,512,512]{2,1,0:T(8,128)S(1)} copy-done((f32[1,512,512]{2,1,0:T(8,128)S(1)}, f32[1,512,512]{2,1,0:T(8,128)}, u32[]{:S(2)}) %copy-start.3) | copy-done | bytes 1048600
  59.9 1.2 %copy-done.4 = f32[1,512,512]{2,1,0:T(8,128)S(1)} copy-done((f32[1,512,512]{2,1,0:T(8,128)S(1)}, f32[1,512,512]{2,1,0:T(8,128)}, u32[]{:S(2)}) %copy-start.4) | copy-done | bytes 1048600
  61.1 2.9 %owner_step.1 = (f32[512,512]{1,0:T(8,128)}, f32[512,512]{1,0:T(8,128)}, f32[512,512]{1,0:T(8,128)}, f32[512,512]{1,0:T(8,128)}, bf16[512,512]{1,0:T(8,128)(2,1)S(1)}) custom-call(s32[1]{0:T(128)S(6)} %convert_element_type.3.flag_ref, bf16[512,512]{1,0:T(8,128)(2,1)S(1)} %bitcast.13, f32[512,512]{1,0:T(8,128)S(1)} %bitcast.14, f32[512,512]{1,0:T(8,128)S(1)} %bitcast.15, ...), custom_call_target="tpu_custom_call" | custom-call | tf_op jit(solution)/shard_map/owner_step/pallas_call | solution.py:170
  64.0 26.7 %all_to_all.10.refs_0_ = bf16[64,8,512]{2,1,0:T(8,128)(2,1)S(1)} all-to-all(bf16[64,8,512]{2,1,0:T(8,128)(2,1)S(1)} %bitcast.18), channel_id=1, replica_groups=mesh['dp'=4,'fsdp'=64] {'fsdp'}, dimensions={0} | all-to-all | bytes 1048576 | tf_op jit(solution)/shard_map/all_to_all | solution.py:219
  90.8 0.8 collective-permute-start.9
  91.5 1.0 collective-permute-start.6
  92.5 0.0 collective-permute-start.7
  92.5 2.6 %collective-permute-start.8 = (bf16[32,8,512]{2,1,0:T(8,128)(2,1)S(1)}, bf16[32,8,512]{2,1,0:T(8,128)(2,1)S(1)}, u32[]{:S(2)}, u32[]{:S(2)}) collective-permute-start(bf16[32,8,512]{2,1,0:T(8,128)(2,1)S(1)} %get-tuple-element.30), channel_id=1, source_target_pairs={{0,192},{64,0},{128,64},{192,128},{1,193},{65,1},{129,65},{193,129... | collective-permute-start | bytes 786440 | tf_op jit(solution)/shard_map/ppermute | solution.py:190
  95.2 3.4 %collective-permute-done.9.refs_4_ = bf16[32,8,512]{2,1,0:T(8,128)(2,1)S(1)} collective-permute-done((bf16[32,8,512]{2,1,0:T(8,128)(2,1)S(1)}, bf16[32,8,512]{2,1,0:T(8,128)(2,1)S(1)}, u32[]{:S(2)}, u32[]{:S(2)}) %collective-permute-start.9) | collective-permute-done | bytes 262176 | tf_op jit(solution)/shard_map/ppermute | solution.py:190
  98.6 1.7 %collective-permute-start.11 = (bf16[32,8,512]{2,1,0:T(8,128)(2,1)S(1)}, bf16[32,8,512]{2,1,0:T(8,128)(2,1)S(1)}, u32[]{:S(2)}, u32[]{:S(2)}) collective-permute-start(bf16[32,8,512]{2,1,0:T(8,128)(2,1)S(1)} %collective-permute-done.9.refs_4_), channel_id=1, source_target_pairs={{0,192},{64,0},{128,64},{192,128},{1,193},{65,1},{129,65},{193,129... | collective-permute-start | bytes 786440 | tf_op jit(solution)/shard_map/ppermute | solution.py:190
  100.3 0.0 collective-permute-done.6.refs_1_
  100.3 0.0 collective-permute-start.10
  100.3 5.3 %collective-permute-done.7.refs_2_ = bf16[32,8,512]{2,1,0:T(8,128)(2,1)S(1)} collective-permute-done((bf16[32,8,512]{2,1,0:T(8,128)(2,1)S(1)}, bf16[32,8,512]{2,1,0:T(8,128)(2,1)S(1)}, u32[]{:S(2)}, u32[]{:S(2)}) %collective-permute-start.7) | collective-permute-done | bytes 262176 | tf_op jit(solution)/shard_map/ppermute | solution.py:187
  105.6 0.0 collective-permute-done.8.refs_3_
  105.6 4.2 %collective-permute-done.11.refs_6_ = bf16[32,8,512]{2,1,0:T(8,128)(2,1)S(1)} collective-permute-done((bf16[32,8,512]{2,1,0:T(8,128)(2,1)S(1)}, bf16[32,8,512]{2,1,0:T(8,128)(2,1)S(1)}, u32[]{:S(2)}, u32[]{:S(2)}) %collective-permute-start.11) | collective-permute-done | bytes 262176 | tf_op jit(solution)/shard_map/ppermute | solution.py:190
  109.9 1.4 %collective-permute-done.10.refs_5_ = bf16[32,8,512]{2,1,0:T(8,128)(2,1)S(1)} collective-permute-done((bf16[32,8,512]{2,1,0:T(8,128)(2,1)S(1)}, bf16[32,8,512]{2,1,0:T(8,128)(2,1)S(1)}, u32[]{:S(2)}, u32[]{:S(2)}) %collective-permute-start.10) | collective-permute-done | bytes 262176 | tf_op jit(solution)/shard_map/ppermute | solution.py:187
  111.2 2.4 %place_blocks.1 = bf16[256,8,512]{2,1,0:T(8,128)(2,1)} custom-call(s32[256]{0:T(256)S(1)} %copy-done.6, bf16[64,8,512]{2,1,0:T(8,128)(2,1)S(1)} %all_to_all.10.refs_0_, bf16[32,8,512]{2,1,0:T(8,128)(2,1)S(1)} %collective-permute-done.6.refs_1_, bf16[32,8,512]{2,1,0:T(8,128)(2,1)S(1)} %collective-permute-done.7.refs_2_, ...), custom_call_target="tpu_custom_call" | custom-call | tf_op jit(solution)/shard_map/place_blocks/pallas_call | solution.py:81
  (2 shorter events, 0.0 us)
Async XLA Ops:
  0.6 1.6 %copy-start = (bf16[1,256,8,512]{3,2,1,0:T(8,128)(2,1)S(1)}, bf16[1,256,8,512]{3,2,1,0:T(8,128)(2,1)}, u32[]{:S(2)}) copy-start(bf16[1,256,8,512]{3,2,1,0:T(8,128)(2,1)} %param.7) | copy-start | bytes 6291460
  2.2 0.7 copy-start.5
  4.5 8.9 %collective-permute-start = (bf16[32,8,512]{2,1,0:T(8,128)(2,1)S(1)}, bf16[32,8,512]{2,1,0:T(8,128)(2,1)S(1)}, u32[]{:S(2)}, u32[]{:S(2)}) collective-permute-start(bf16[32,8,512]{2,1,0:T(8,128)(2,1)S(1)} %get-tuple-element.19), channel_id=1, source_target_pairs={{0,64},{64,128},{128,192},{192,0},{1,65},{65,129},{129,193},{193,1... | collective-permute-start | bytes 786440 | tf_op jit(solution)/shard_map/ppermute | solution.py:187
  6.7 7.2 %collective-permute-start.3 = (bf16[32,8,512]{2,1,0:T(8,128)(2,1)S(1)}, bf16[32,8,512]{2,1,0:T(8,128)(2,1)S(1)}, u32[]{:S(2)}, u32[]{:S(2)}) collective-permute-start(bf16[32,8,512]{2,1,0:T(8,128)(2,1)S(1)} %get-tuple-element.22), channel_id=1, source_target_pairs={{0,192},{64,0},{128,64},{192,128},{1,193},{65,1},{129,65},{193,129... | collective-permute-start | bytes 786440 | tf_op jit(solution)/shard_map/ppermute | solution.py:190
  11.9 7.2 %collective-permute-start.2 = (bf16[32,8,512]{2,1,0:T(8,128)(2,1)S(1)}, bf16[32,8,512]{2,1,0:T(8,128)(2,1)S(1)}, u32[]{:S(2)}, u32[]{:S(2)}) collective-permute-start(bf16[32,8,512]{2,1,0:T(8,128)(2,1)S(1)} %get-tuple-element.20), channel_id=1, source_target_pairs={{0,192},{64,0},{128,64},{192,128},{1,193},{65,1},{129,65},{193,129... | collective-permute-start | bytes 786440 | tf_op jit(solution)/shard_map/ppermute | solution.py:190
  13.3 7.5 %collective-permute-start.5 = (bf16[32,8,512]{2,1,0:T(8,128)(2,1)S(1)}, bf16[32,8,512]{2,1,0:T(8,128)(2,1)S(1)}, u32[]{:S(2)}, u32[]{:S(2)}) collective-permute-start(bf16[32,8,512]{2,1,0:T(8,128)(2,1)S(1)} %get-tuple-element.23), channel_id=1, source_target_pairs={{0,64},{64,128},{128,192},{192,0},{1,65},{65,129},{129,193},{193,1... | collective-permute-start | bytes 786440 | tf_op jit(solution)/shard_map/ppermute | solution.py:187
  13.5 27.9 %copy-start.6 = (s32[256]{0:T(256)S(1)}, s32[256]{0:T(256)}, u32[]{:S(2)}) copy-start(s32[256]{0:T(256)} %index_ref.5) | copy-start | bytes 3076
  13.5 45.2 %copy-start.1 = (f32[1,512,512]{2,1,0:T(8,128)S(1)}, f32[1,512,512]{2,1,0:T(8,128)}, u32[]{:S(2)}) copy-start(f32[1,512,512]{2,1,0:T(8,128)} %param.8) | copy-start | bytes 3145732
  13.5 45.2 %copy-start.2 = (f32[1,512,512]{2,1,0:T(8,128)S(1)}, f32[1,512,512]{2,1,0:T(8,128)}, u32[]{:S(2)}) copy-start(f32[1,512,512]{2,1,0:T(8,128)} %param.9) | copy-start | bytes 3145732
  13.5 12.9 %collective-permute-start.1 = (bf16[32,8,512]{2,1,0:T(8,128)(2,1)S(1)}, bf16[32,8,512]{2,1,0:T(8,128)(2,1)S(1)}, u32[]{:S(2)}, u32[]{:S(2)}) collective-permute-start(bf16[32,8,512]{2,1,0:T(8,128)(2,1)S(1)} %add_pieces.2), channel_id=1, source_target_pairs={{0,64},{64,128},{128,192},{192,0},{1,65},{65,129},{129,193},{193,1... | collective-permute-start | bytes 786440 | tf_op jit(solution)/shard_map/ppermute | solution.py:187
  13.9 12.5 %collective-permute-start.4 = (bf16[32,8,512]{2,1,0:T(8,128)(2,1)S(1)}, bf16[32,8,512]{2,1,0:T(8,128)(2,1)S(1)}, u32[]{:S(2)}, u32[]{:S(2)}) collective-permute-start(bf16[32,8,512]{2,1,0:T(8,128)(2,1)S(1)} %add_pieces.3), channel_id=1, source_target_pairs={{0,192},{64,0},{128,64},{192,128},{1,193},{65,1},{129,65},{193,129... | collective-permute-start | bytes 786440 | tf_op jit(solution)/shard_map/ppermute | solution.py:190
  27.4 31.3 %all-to-all-start = ((bf16[64,8,512]{2,1,0:T(8,128)(2,1)}), bf16[64,8,512]{2,1,0:T(8,128)(2,1)S(1)}, u32[]{:S(2)}, u32[]{:S(2)}) async-start(bf16[64,8,512]{2,1,0:T(8,128)(2,1)} %total_pieces.1), calls=%async_computation | async-start | bytes 1048576 | tf_op jit(solution)/shard_map/all_to_all | solution.py:207
  58.7 1.2 %copy-start.3 = (f32[1,512,512]{2,1,0:T(8,128)S(1)}, f32[1,512,512]{2,1,0:T(8,128)}, u32[]{:S(2)}) copy-start(f32[1,512,512]{2,1,0:T(8,128)} %param.10) | copy-start | bytes 3145732
  59.9 1.2 %copy-start.4 = (f32[1,512,512]{2,1,0:T(8,128)S(1)}, f32[1,512,512]{2,1,0:T(8,128)}, u32[]{:S(2)}) copy-start(f32[1,512,512]{2,1,0:T(8,128)} %param.11) | copy-start | bytes 3145732
  90.8 7.8 %collective-permute-start.9 = (bf16[32,8,512]{2,1,0:T(8,128)(2,1)S(1)}, bf16[32,8,512]{2,1,0:T(8,128)(2,1)S(1)}, u32[]{:S(2)}, u32[]{:S(2)}) collective-permute-start(bf16[32,8,512]{2,1,0:T(8,128)(2,1)S(1)} %get-tuple-element.29), channel_id=1, source_target_pairs={{0,192},{64,0},{128,64},{192,128},{1,193},{65,1},{129,65},{193,129... | collective-permute-start | bytes 786440 | tf_op jit(solution)/shard_map/ppermute | solution.py:190
  91.5 8.8 %collective-permute-start.6 = (bf16[32,8,512]{2,1,0:T(8,128)(2,1)S(1)}, bf16[32,8,512]{2,1,0:T(8,128)(2,1)S(1)}, u32[]{:S(2)}, u32[]{:S(2)}) collective-permute-start(bf16[32,8,512]{2,1,0:T(8,128)(2,1)S(1)} %get-tuple-element.30), channel_id=1, source_target_pairs={{0,64},{64,128},{128,192},{192,0},{1,65},{65,129},{129,193},{193,1... | collective-permute-start | bytes 786440 | tf_op jit(solution)/shard_map/ppermute | solution.py:187
  92.5 13.1 %collective-permute-start.7 = (bf16[32,8,512]{2,1,0:T(8,128)(2,1)S(1)}, bf16[32,8,512]{2,1,0:T(8,128)(2,1)S(1)}, u32[]{:S(2)}, u32[]{:S(2)}) collective-permute-start(bf16[32,8,512]{2,1,0:T(8,128)(2,1)S(1)} %get-tuple-element.29), channel_id=1, source_target_pairs={{0,64},{64,128},{128,192},{192,0},{1,65},{65,129},{129,193},{193,1... | collective-permute-start | bytes 786440 | tf_op jit(solution)/shard_map/ppermute | solution.py:187
  92.5 13.1 %collective-permute-start.8 = (bf16[32,8,512]{2,1,0:T(8,128)(2,1)S(1)}, bf16[32,8,512]{2,1,0:T(8,128)(2,1)S(1)}, u32[]{:S(2)}, u32[]{:S(2)}) collective-permute-start(bf16[32,8,512]{2,1,0:T(8,128)(2,1)S(1)} %get-tuple-element.30), channel_id=1, source_target_pairs={{0,192},{64,0},{128,64},{192,128},{1,193},{65,1},{129,65},{193,129... | collective-permute-start | bytes 786440 | tf_op jit(solution)/shard_map/ppermute | solution.py:190
  98.6 11.2 %collective-permute-start.11 = (bf16[32,8,512]{2,1,0:T(8,128)(2,1)S(1)}, bf16[32,8,512]{2,1,0:T(8,128)(2,1)S(1)}, u32[]{:S(2)}, u32[]{:S(2)}) collective-permute-start(bf16[32,8,512]{2,1,0:T(8,128)(2,1)S(1)} %collective-permute-done.9.refs_4_), channel_id=1, source_target_pairs={{0,192},{64,0},{128,64},{192,128},{1,193},{65,1},{129,65},{193,129... | collective-permute-start | bytes 786440 | tf_op jit(solution)/shard_map/ppermute | solution.py:190
  100.3 10.9 %collective-permute-start.10 = (bf16[32,8,512]{2,1,0:T(8,128)(2,1)S(1)}, bf16[32,8,512]{2,1,0:T(8,128)(2,1)S(1)}, u32[]{:S(2)}, u32[]{:S(2)}) collective-permute-start(bf16[32,8,512]{2,1,0:T(8,128)(2,1)S(1)} %collective-permute-done.6.refs_1_), channel_id=1, source_target_pairs={{0,64},{64,128},{128,192},{192,0},{1,65},{65,129},{129,193},{193,1... | collective-permute-start | bytes 786440 | tf_op jit(solution)/shard_map/ppermute | solution.py:187

commit v3 on v2

v3 whole, which is shorter than its diff:
```python
import functools

import jax
import jax.numpy as jnp
from jax import lax
from jax.experimental import pallas as pl
from jax.experimental.pallas import tpu as pltpu
from jax.sharding import PartitionSpec as P

ITERS = 2
REFRESH_PERIOD = 16
N_DP = 4

VMEM = pltpu.VMEM
SMEM = pltpu.SMEM
HBM = pltpu.HBM


def bf16_dot(a, b, dims=((1,), (0,))):
    return lax.dot_general(
        a.astype(jnp.bfloat16),
        b.astype(jnp.bfloat16),
        (dims, ((), ())),
        preferred_element_type=jnp.float32,
    )


def piece_start(quarter, first, slots):
    return lax.rem(lax.axis_index("dp") + quarter, N_DP) * (slots // N_DP) + first


def copy_rows(index_smem, source_ref, out_ref, start):
    def body(slot, carry):
        out_ref[slot] = source_ref[index_smem[start + slot]]
        return carry

    lax.fori_loop(0, out_ref.shape[0], body, 0, unroll=8)


CHUNKS = 8


def order_first_kernel(pieces, index_ref, source_ref, held_ref, index_smem, *refs):
    outs, (index_sem, sems) = refs[: len(pieces)], refs[len(pieces) :]
    fetch = pltpu.make_async_copy(index_ref, index_smem, index_sem)
    fetch.start()
    count = source_ref.shape[0] // CHUNKS
    loads = [
        pltpu.make_async_copy(
            source_ref.at[pl.ds(i * count, count)], held_ref.at[pl.ds(i * count, count)], sems.at[i]
        )
        for i in range(CHUNKS)
    ]
    for load in loads:
        load.start()
    fetch.wait()
    for load in loads:
        load.wait()
    for (quarter, first), out_ref in zip(pieces, outs, strict=True):
        copy_rows(index_smem, held_ref, out_ref, piece_start(quarter, first, index_ref.shape[0]))


def order_rest_kernel(pieces, index_ref, refresh_ref, held_ref, refresh_smem, *outs):
    refresh_smem[0] = refresh_ref[0]
    for (quarter, first), out_ref in zip(pieces, outs, strict=True):
        copy_rows(index_ref, held_ref, out_ref, piece_start(quarter, first, index_ref.shape[0]))


def order_first(index, source, pieces, counts):
    tail = source.shape[1:]
    return pl.pallas_call(
        functools.partial(order_first_kernel, pieces),
        out_shape=[VMEM(source.shape, source.dtype), SMEM(index.shape, index.dtype)]
        + [VMEM((count, *tail), source.dtype) for count in counts],
        in_specs=[pl.BlockSpec(memory_space=HBM)] * 2,
        out_specs=[pl.BlockSpec(memory_space=VMEM), pl.BlockSpec(memory_space=SMEM)]
        + [pl.BlockSpec(memory_space=VMEM)] * len(pieces),
        scratch_shapes=[pltpu.SemaphoreType.DMA, pltpu.SemaphoreType.DMA((CHUNKS,))],
        compiler_params=pltpu.CompilerParams(vmem_limit_bytes=8 * 2**20),
        name="order_first",
    )(
        pltpu.with_memory_space_constraint(index, HBM),
        pltpu.with_memory_space_constraint(source, HBM),
    )


def order_rest(index, refresh, held, pieces, counts):
    return pl.pallas_call(
        functools.partial(order_rest_kernel, pieces),
        out_shape=[SMEM(refresh.shape, refresh.dtype)]
        + [VMEM((count, *held.shape[1:]), held.dtype) for count in counts],
        in_specs=[pl.BlockSpec(memory_space=space) for space in (SMEM, SMEM, VMEM)],
        out_specs=[pl.BlockSpec(memory_space=SMEM)]
        + [pl.BlockSpec(memory_space=VMEM)] * len(pieces),
        compiler_params=pltpu.CompilerParams(vmem_limit_bytes=8 * 2**20),
        name="order_rest",
    )(index, refresh, held)


def place_kernel(pieces, aliased, index_ref, *refs):
    sources = refs[: len(pieces)]
    out_ref, sems = refs[len(pieces) + aliased :]
    for number, ((quarter, first), source_ref) in enumerate(zip(pieces, sources, strict=True)):
        start = piece_start(quarter, first, index_ref.shape[0])

        def body(slot, carry, source_ref=source_ref, number=number, start=start):
            pltpu.make_async_copy(
                source_ref.at[slot], out_ref.at[index_ref[start + slot]], sems.at[number]
            ).start()
            return carry

        lax.fori_loop(0, source_ref.shape[0], body, 0, unroll=16)
    for number, source_ref in enumerate(sources):
        pltpu.make_async_copy(source_ref, source_ref, sems.at[number]).wait()


def place_blocks(index, sources, pieces, name, out=None):
    rows, columns = sources[0].shape[1:]
    aliased = 0 if out is None else 1
    return pl.pallas_call(
        functools.partial(place_kernel, pieces, aliased),
        out_shape=jax.ShapeDtypeStruct((index.shape[0], rows, columns), sources[0].dtype),
        in_specs=[pl.BlockSpec(memory_space=SMEM)]
        + [pl.BlockSpec(memory_space=pl.ANY)] * (len(sources) + aliased),
        out_specs=pl.BlockSpec(memory_space=pl.ANY),
        scratch_shapes=[pltpu.SemaphoreType.DMA((len(pieces),))],
        input_output_aliases={1 + len(sources): 0} if aliased else {},
        compiler_params=pltpu.CompilerParams(vmem_limit_bytes=4 * 2**20),
        cost_estimate=pl.CostEstimate(
            flops=0, bytes_accessed=64 * rows * columns * 64 * len(sources), transcendentals=0
        ),
        name=name,
    )(index, *sources, *(() if out is None else (out,)))


def add_kernel(first_ref, second_ref, out_ref):
    total = first_ref[...].astype(jnp.float32) + second_ref[...].astype(jnp.float32)
    out_ref[...] = total.astype(out_ref.dtype)


def add_pieces(first, second):
    return pl.pallas_call(
        add_kernel,
        out_shape=jax.ShapeDtypeStruct(first.shape, first.dtype),
        in_specs=[pl.BlockSpec(memory_space=VMEM)] * 2,
        out_specs=pl.BlockSpec(memory_space=VMEM),
        compiler_params=pltpu.CompilerParams(vmem_limit_bytes=4 * 2**20),
        name="add_pieces",
    )(first, second)


def partial_kernel(mine_ref, raw_a_ref, raw_b_ref, out_ref):
    half = raw_a_ref.shape[0]
    for start, raw_ref in ((0, raw_a_ref), (half, raw_b_ref)):
        part = pl.ds(start, half)
        out_ref[part] = mine_ref[part].astype(jnp.float32) + raw_ref[...].astype(jnp.float32)


def partial_sum(mine, raw_a, raw_b):
    return pl.pallas_call(
        partial_kernel,
        out_shape=VMEM(mine.shape, jnp.float32),
        in_specs=[pl.BlockSpec(memory_space=VMEM)] * 3,
        out_specs=pl.BlockSpec(memory_space=VMEM),
        compiler_params=pltpu.CompilerParams(vmem_limit_bytes=6 * 2**20),
        name="partial_sum",
    )(mine, raw_a, raw_b)


def total_kernel(tie_ref, partial_ref, comb_a_ref, comb_b_ref, out_ref):
    del tie_ref
    half = comb_a_ref.shape[0]
    for start, comb_ref in ((0, comb_a_ref), (half, comb_b_ref)):
        part = pl.ds(start, half)
        total = partial_ref[part] + comb_ref[...].astype(jnp.float32)
        out_ref[part] = total.astype(out_ref.dtype)


def total_sum(tie, partial, comb_a, comb_b):
    return pl.pallas_call(
        total_kernel,
        out_shape=VMEM(partial.shape, comb_a.dtype),
        in_specs=[pl.BlockSpec(memory_space=pl.ANY)] + [pl.BlockSpec(memory_space=VMEM)] * 3,
        out_specs=pl.BlockSpec(memory_space=VMEM),
        compiler_params=pltpu.CompilerParams(vmem_limit_bytes=6 * 2**20),
        name="total_sum",
    )(tie, partial, comb_a, comb_b)


def inverse_roots(factors):
    fifth = [1.25 ** (5 - k) * (-0.25) ** k * c for k, c in enumerate((1, 5, 10, 10, 5, 1))]
    coefficients = [1.5625, -0.3125, 0.0, 0.0, 0.0, 0.0, 0.0]
    for k, value in enumerate(fifth):
        coefficients[k + 1] -= value / 4
    order = factors[0].shape[0]
    rows = lax.broadcasted_iota(jnp.int32, (order, order), 0)
    cols = lax.broadcasted_iota(jnp.int32, (order, order), 1)
    norms = [jnp.sqrt(jnp.sum(factor * factor, keepdims=True)) for factor in factors]
    scalings = [2.5 / norm for norm in norms]
    once = [factor * scaling for factor, scaling in zip(factors, scalings)]
    twice = [bf16_dot(m, m) for m in once]
    thrice = [bf16_dot(m2, m) for m2, m in zip(twice, once)]
    p = coefficients
    roots = []
    for m, m2, m3, scaling in zip(once, twice, thrice, scalings):
        low = p[1] * m + p[2] * m2 + p[3] * m3
        high = p[4] * m + p[5] * m2 + p[6] * m3
        total = bf16_dot(high, m3) + low
        total = jnp.where(rows == cols, total + p[0], total)
        roots.append(total * jnp.sqrt(jnp.sqrt(scaling)))
    return roots


def refreshing(refresh_ref):
    mine = lax.axis_index("dp") * lax.axis_size("fsdp") + lax.axis_index("fsdp")
    return lax.rem(mine, REFRESH_PERIOD) == refresh_ref[0]


def load_kernel(tie_ref, *refs):
    del tie_ref
    count = len(refs) // 2
    loads = [
        pltpu.make_async_copy(refs[i], refs[count + i], refs[-1].at[i]) for i in range(count)
    ]
    for load in loads:
        load.start()
    for load in loads:
        load.wait()


def load_matrices(tie, *matrices):
    return pl.pallas_call(
        load_kernel,
        out_shape=[VMEM(m.shape, m.dtype) for m in matrices],
        in_specs=[pl.BlockSpec(memory_space=pl.ANY)] + [pl.BlockSpec(memory_space=HBM)] * len(matrices),
        out_specs=[pl.BlockSpec(memory_space=VMEM)] * len(matrices),
        scratch_shapes=[pltpu.SemaphoreType.DMA((len(matrices),))],
        compiler_params=pltpu.CompilerParams(vmem_limit_bytes=8 * 2**20),
        name="load_matrices",
    )(tie, *[pltpu.with_memory_space_constraint(m, HBM) for m in matrices])


def gram_rows(grad):
    return bf16_dot(grad, grad, ((1,), (1,))) * (1.0 / grad.shape[0])


def gram_columns(grad):
    return bf16_dot(grad, grad, ((0,), (0,))) * (1.0 / grad.shape[0])


def update_kernel(
    refresh_ref, grad_ref, left_ref, right_ref, lroot_ref, rroot_ref,
    new_lroot_ref, new_rroot_ref, update_ref, roots, sems,
):
    grad = grad_ref[...]
    refreshed = refreshing(refresh_ref)

    @pl.when(refreshed)
    def _():
        new_left = left_ref[...] + gram_rows(grad)
        new_right = right_ref[...] + gram_columns(grad)
        new_roots = inverse_roots((new_left, new_right))
        writes = []
        for i, (root, out_ref) in enumerate(zip(new_roots, (new_lroot_ref, new_rroot_ref))):
            roots[i] = root
            write = pltpu.make_async_copy(roots.at[i], out_ref, sems.at[i])
            write.start()
            writes.append(write)
        mixed = bf16_dot(roots[0], grad)
        update_ref[...] = bf16_dot(mixed, roots[1]).astype(update_ref.dtype)
        for write in writes:
            write.wait()

    @pl.when(jnp.logical_not(refreshed))
    def _():
        loads = [
            pltpu.make_async_copy(source, roots.at[i], sems.at[i])
            for i, source in enumerate((lroot_ref, rroot_ref))
        ]
        for load in loads:
            load.start()
        loads[0].wait()
        mixed = bf16_dot(roots[0], grad)
        loads[1].wait()
        update_ref[...] = bf16_dot(mixed, roots[1]).astype(update_ref.dtype)


def owner_update(refresh, grad, left, right, lroot, rroot):
    order = grad.shape[0]
    return pl.pallas_call(
        update_kernel,
        out_shape=(
            HBM((order, order), jnp.float32),
            HBM((order, order), jnp.float32),
            VMEM((order, order), jnp.bfloat16),
        ),
        in_specs=[pl.BlockSpec(memory_space=SMEM)]
        + [pl.BlockSpec(memory_space=VMEM)] * 3
        + [pl.BlockSpec(memory_space=HBM)] * 2,
        out_specs=(pl.BlockSpec(memory_space=HBM),) * 2 + (pl.BlockSpec(memory_space=VMEM),),
        scratch_shapes=[
            pltpu.VMEM((2, order, order), jnp.float32),
            pltpu.SemaphoreType.DMA((2,)),
        ],
        compiler_params=pltpu.CompilerParams(vmem_limit_bytes=24 * 2**20),
        name="owner_update",
    )(refresh, grad, left, right, lroot, rroot)


def factors_kernel(
    tie_ref, refresh_ref, grad_ref, left_ref, right_ref, lroot_ref, rroot_ref, old_l_ref, old_r_ref,
    new_left_ref, new_right_ref, new_lroot_ref, new_rroot_ref,
    left, right, roots, sems,
):
    del tie_ref, old_l_ref, old_r_ref
    kept = jnp.logical_not(refreshing(refresh_ref))
    loads = [
        pltpu.make_async_copy(source, roots.at[i], sems.at[2 + i])
        for i, source in enumerate((lroot_ref, rroot_ref))
    ]
    keeps = [
        pltpu.make_async_copy(roots.at[i], target, sems.at[2 + i])
        for i, target in enumerate((new_lroot_ref, new_rroot_ref))
    ]

    @pl.when(kept)
    def _():
        for load in loads:
            load.start()

    grad = grad_ref[...]
    left[...] = left_ref[...] + gram_rows(grad)
    write_left = pltpu.make_async_copy(left, new_left_ref, sems.at[0])
    write_left.start()
    right[...] = right_ref[...] + gram_columns(grad)
    write_right = pltpu.make_async_copy(right, new_right_ref, sems.at[1])
    write_right.start()

    @pl.when(kept)
    def _():
        for load, keep in zip(loads, keeps, strict=True):
            load.wait()
            keep.start()
        for keep in keeps:
            keep.wait()

    write_left.wait()
    write_right.wait()


def owner_factors(tie, refresh, grad, left, right, lroot, rroot, new_lroot, new_rroot):
    order = grad.shape[0]
    return pl.pallas_call(
        factors_kernel,
        out_shape=(HBM((order, order), jnp.float32),) * 4,
        in_specs=[pl.BlockSpec(memory_space=pl.ANY), pl.BlockSpec(memory_space=SMEM)]
        + [pl.BlockSpec(memory_space=VMEM)] * 3
        + [pl.BlockSpec(memory_space=HBM)] * 4,
        out_specs=(pl.BlockSpec(memory_space=HBM),) * 4,
        scratch_shapes=[pltpu.VMEM((order, order), jnp.float32)] * 2
        + [pltpu.VMEM((2, order, order), jnp.float32), pltpu.SemaphoreType.DMA((4,))],
        input_output_aliases={7: 2, 8: 3},
        compiler_params=pltpu.CompilerParams(vmem_limit_bytes=16 * 2**20),
        name="owner_factors",
    )(
        tie,
        refresh,
        grad, left, right, lroot, rroot, new_lroot, new_rroot,
    )


def per_device(grads, left_factor, right_factor, left_root, right_root, block_of_slot, refresh):
    shard_count = lax.axis_size("fsdp")
    local = grads[0]
    blocks, piece_rows, order = local.shape
    quarter, half = blocks // N_DP, blocks // N_DP // 2

    def to_next(piece):
        return lax.ppermute(piece, "dp", [(i, (i + 1) % N_DP) for i in range(N_DP)])

    def to_prev(piece):
        return lax.ppermute(piece, "dp", [(i, (i - 1) % N_DP) for i in range(N_DP)])

    held, index, relay_a, relay_b = order_first(
        block_of_slot, local, ((2, 0), (2, half)), (half, half)
    )
    relayed_a, relayed_b = to_next(relay_a), to_prev(relay_b)
    refresh, raw_a, raw_b, own_a, own_b, mine = order_rest(
        index,
        refresh,
        held,
        ((3, 0), (1, half), (1, 0), (3, half), (0, 0)),
        (half, half, half, half, quarter),
    )
    raw_a, raw_b = to_prev(raw_a), to_next(raw_b)
    sum_a, sum_b = add_pieces(own_a, relayed_a), add_pieces(own_b, relayed_b)
    comb_a, comb_b = to_next(sum_a), to_prev(sum_b)
    left, right = load_matrices(sum_b, left_factor[0], right_factor[0])
    lroot, rroot = (
        pltpu.with_memory_space_constraint(root[0], HBM) for root in (left_root, right_root)
    )
    summed = total_sum(left, partial_sum(mine, raw_a, raw_b), comb_a, comb_b)

    grad = lax.all_to_all(summed, "fsdp", split_axis=0, concat_axis=0, tiled=True)
    grad = grad.reshape(order, order)

    new_lroot, new_rroot, update = owner_update(refresh, grad, left, right, lroot, rroot)

    rows = update.reshape(shard_count, piece_rows, order)
    rows = lax.all_to_all(rows, "fsdp", split_axis=0, concat_axis=0, tiled=True)
    rows_a, rows_b = rows[:half], rows[half:]
    prev_a, next_b = to_next(rows_a), to_prev(rows_b)
    prev_b, next_a = to_next(rows_b), to_prev(rows_a)
    new_left, new_right, new_lroot, new_rroot = owner_factors(
        rows_a, refresh, grad, left, right, lroot, rroot, new_lroot, new_rroot
    )
    over_a, over_b = to_next(prev_a), to_prev(next_b)
    updates = place_blocks(
        index,
        (rows, prev_a, next_b, prev_b, next_a),
        ((0, 0), (3, 0), (1, half), (3, half), (1, 0)),
        "place_early",
    )
    updates = place_blocks(
        index, (over_a, over_b), ((2, 0), (2, half)), "place_late", updates
    )
    return new_left[None], new_right[None], new_lroot[None], new_rroot[None], updates


def solution(mesh):
    owned = P(("dp", "fsdp"), None, None)
    return jax.shard_map(
        per_device,
        mesh=mesh,
        in_specs=(P("dp", None, "fsdp", None), owned, owned, owned, owned, P(), P()),
        out_specs=(owned, owned, owned, owned, P(None, "fsdp", None)),
        check_vma=False,
    )
```

time: 114 us -> 104 us (0.912)
  blocking collectives: 26.7 us -> 54.8 us
  waiting for transfers between devices: 38.5 us -> 20.7 us
  starting transfers between devices: 28.2 us -> 15.4 us
  local copies, waits for them, and re-layouts: 5.35 us -> 0.03 us
  between operations: 3.33 us -> 1.54 us
    all_to_all x0 -> x1, blocking collectives: none -> 30.5 us  [per_device(): lax.all_to_all(summed, 'fsdp', split_axis=0, concat_axis=0, tiled=True)]
    all_to_all x1 -> x0, waiting for transfers between devices: 14.1 us -> none  [per_device(): lax.all_to_all(summed, 'fsdp', split_axis=0, concat_axis=0, tiled=True)]
    all_to_all x1 -> x0, starting transfers between devices: 13.9 us -> none  [per_device(): lax.all_to_all(summed, 'fsdp', split_axis=0, concat_axis=0, tiled=True)]
    unnamed x14 -> x0, local copies, waits for them, and re-layouts: 4.73 us -> none
    ppermute x6, waiting for transfers between devices: 14 us -> 10.6 us  [to_next(): return lax.ppermute(piece, 'dp', [(i, (i + 1) % N_DP) for i in range(N_DP)])]
    ppermute x6, starting transfers between devices: 10.6 us -> 13.8 us  [to_prev(): return lax.ppermute(piece, 'dp', [(i, (i - 1) % N_DP) for i in range(N_DP)])]
    all_to_all x1, blocking collectives: 26.7 us -> 24.3 us  [per_device(): rows = lax.all_to_all(rows, 'fsdp', split_axis=0, concat_axis=0, tiled=True)]
    ppermute x6, starting transfers between devices: 3.62 us -> 1.58 us  [to_next(): return lax.ppermute(piece, 'dp', [(i, (i + 1) % N_DP) for i in range(N_DP)])]
  transfers between devices with their start and end apart: 13 -> 12, of which waited for: 8 -> 10; matrix products, arithmetic and copies ran while one was open for 1% -> 0% of each run, Pallas kernels for 3% -> 6%
where the time goes in v3:
time: 104 us
  blocking collectives  54.8 us (53%)
  waiting for transfers between devices  20.7 us (20%)
  starting transfers between devices  15.4 us (15%)
  Pallas kernels  11.2 us (11%)
  between operations  1.54 us (1%)
    all_to_all x1, blocking collectives, per_device(): lax.all_to_all(summed, 'fsdp', split_axis=0, concat_axis=0, tiled=True)  30.5 us
    all_to_all x1, blocking collectives, per_device(): rows = lax.all_to_all(rows, 'fsdp', split_axis=0, concat_axis=0, tiled=True)  24.3 us
    ppermute x6, starting transfers between devices, to_prev(): return lax.ppermute(piece, 'dp', [(i, (i - 1) % N_DP) for i in range(N_DP)])  13.8 us
    ppermute x6, waiting for transfers between devices, to_next(): return lax.ppermute(piece, 'dp', [(i, (i + 1) % N_DP) for i in range(N_DP)])  10.6 us
    ppermute x6, waiting for transfers between devices, to_prev(): return lax.ppermute(piece, 'dp', [(i, (i - 1) % N_DP) for i in range(N_DP)])  10.1 us
    pallas_call x1, Pallas kernels, owner_factors(): pl.pallas_call(factors_kernel, out_shape=(HBM((order, order), jnp.float32...  2.92 us
    pallas_call x2, Pallas kernels, place_blocks(): pl.pallas_call(functools.partial(place_kernel, pieces, aliased), out_shap...  2.19 us
    pallas_call x1, Pallas kernels, owner_update(): pl.pallas_call(update_kernel, out_shape=(HBM((order, order), jnp.float32)...  2.16 us
  transfers between devices with their start and end apart: 12, of which 10 were waited for; matrix products, arithmetic and copies ran while one was open for 0% of the time, Pallas kernels for 6%

profile of v3, /device:TPU:1, one launch (start us, length us, event | category | flops | bytes accessed | tf_op | source)
XLA Modules:
  0.0 103.7 jit_solution(11667171027420161489)
XLA Ops:
  0.6 1.7 %order_first.1 = (bf16[256,8,512]{2,1,0:T(8,128)(2,1)S(1)}, s32[256]{0:T(256)S(4)}, bf16[32,8,512]{2,1,0:T(8,128)(2,1)S(1)}, bf16[32,8,512]{2,1,0:T(8,128)(2,1)S(1)}) custom-call(s32[256]{0:T(256)} %index_ref.1, bf16[256,8,512]{2,1,0:T(8,128)(2,1)} %bitcast.18), custom_call_target="tpu_custom_call" | custom-call | tf_op jit(solution)/shard_map/order_first/pallas_call | solution.py:71
  2.3 3.6 %collective-permute-start = (bf16[32,8,512]{2,1,0:T(8,128)(2,1)S(1)}, bf16[32,8,512]{2,1,0:T(8,128)(2,1)S(1)}, u32[]{:S(2)}, u32[]{:S(2)}) collective-permute-start(bf16[32,8,512]{2,1,0:T(8,128)(2,1)S(1)} %get-tuple-element.28), channel_id=1, source_target_pairs={{0,192},{64,0},{128,64},{192,128},{1,193},{65,1},{129,65},{193,129... | collective-permute-start | bytes 786440 | tf_op jit(solution)/shard_map/ppermute | solution.py:382
  6.0 0.0 collective-permute-start.3
  6.6 0.4 order_rest.1
  7.0 2.8 %collective-permute-start.1 = (bf16[32,8,512]{2,1,0:T(8,128)(2,1)S(1)}, bf16[32,8,512]{2,1,0:T(8,128)(2,1)S(1)}, u32[]{:S(2)}, u32[]{:S(2)}) collective-permute-start(bf16[32,8,512]{2,1,0:T(8,128)(2,1)S(1)} %get-tuple-element.31), channel_id=1, source_target_pairs={{0,192},{64,0},{128,64},{192,128},{1,193},{65,1},{129,65},{193,129... | collective-permute-start | bytes 786440 | tf_op jit(solution)/shard_map/ppermute | solution.py:382
  9.8 0.0 collective-permute-start.2
  9.8 1.2 %collective-permute-done.second_ref = bf16[32,8,512]{2,1,0:T(8,128)(2,1)S(1)} collective-permute-done((bf16[32,8,512]{2,1,0:T(8,128)(2,1)S(1)}, bf16[32,8,512]{2,1,0:T(8,128)(2,1)S(1)}, u32[]{:S(2)}, u32[]{:S(2)}) %collective-permute-start) | collective-permute-done | bytes 262176 | tf_op jit(solution)/shard_map/ppermute | solution.py:382
  10.9 0.1 add_pieces.2.tie_ref
  11.0 3.5 %collective-permute-start.5 = (bf16[32,8,512]{2,1,0:T(8,128)(2,1)S(1)}, bf16[32,8,512]{2,1,0:T(8,128)(2,1)S(1)}, u32[]{:S(2)}, u32[]{:S(2)}) collective-permute-start(bf16[32,8,512]{2,1,0:T(8,128)(2,1)S(1)} %add_pieces.2.tie_ref), channel_id=1, source_target_pairs={{0,192},{64,0},{128,64},{192,128},{1,193},{65,1},{129,65},{193,129... | collective-permute-start | bytes 786440 | tf_op jit(solution)/shard_map/ppermute | solution.py:382
  14.5 0.0 collective-permute-done.3.second_ref
  14.5 0.1 add_pieces.3
  14.6 0.1 collective-permute-start.4
  14.7 1.6 %load_matrices.1 = (f32[512,512]{1,0:T(8,128)S(1)}, f32[512,512]{1,0:T(8,128)S(1)}) custom-call(bf16[32,8,512]{2,1,0:T(8,128)(2,1)S(1)} %add_pieces.2.tie_ref, f32[512,512]{1,0:T(8,128)} %bitcast.21, f32[512,512]{1,0:T(8,128)} %bitcast.22), custom_call_target="tpu_custom_call" | custom-call | tf_op jit(solution)/shard_map/load_matrices/pallas_call | solution.py:232
  16.2 0.3 collective-permute-done.1.raw_a_ref
  16.6 3.1 %collective-permute-done.2.raw_b_ref = bf16[32,8,512]{2,1,0:T(8,128)(2,1)S(1)} collective-permute-done((bf16[32,8,512]{2,1,0:T(8,128)(2,1)S(1)}, bf16[32,8,512]{2,1,0:T(8,128)(2,1)S(1)}, u32[]{:S(2)}, u32[]{:S(2)}) %collective-permute-start.2) | collective-permute-done | bytes 262176 | tf_op jit(solution)/shard_map/ppermute | solution.py:379
  19.7 0.1 partial_sum.1.partial_ref
  19.8 2.4 %collective-permute-done.5.comb_b_ref = bf16[32,8,512]{2,1,0:T(8,128)(2,1)S(1)} collective-permute-done((bf16[32,8,512]{2,1,0:T(8,128)(2,1)S(1)}, bf16[32,8,512]{2,1,0:T(8,128)(2,1)S(1)}, u32[]{:S(2)}, u32[]{:S(2)}) %collective-permute-start.5) | collective-permute-done | bytes 262176 | tf_op jit(solution)/shard_map/ppermute | solution.py:382
  22.2 3.1 %collective-permute-done.4.comb_a_ref = bf16[32,8,512]{2,1,0:T(8,128)(2,1)S(1)} collective-permute-done((bf16[32,8,512]{2,1,0:T(8,128)(2,1)S(1)}, bf16[32,8,512]{2,1,0:T(8,128)(2,1)S(1)}, u32[]{:S(2)}, u32[]{:S(2)}) %collective-permute-start.4) | collective-permute-done | bytes 262176 | tf_op jit(solution)/shard_map/ppermute | solution.py:379
  25.3 0.1 total_sum.1
  25.4 30.5 %all_to_all.10 = bf16[64,8,512]{2,1,0:T(8,128)(2,1)S(1)} all-to-all(bf16[64,8,512]{2,1,0:T(8,128)(2,1)S(1)} %total_sum.1), channel_id=1, replica_groups=mesh['dp'=4,'fsdp'=64] {'fsdp'}, dimensions={0} | all-to-all | bytes 1048576 | tf_op jit(solution)/shard_map/all_to_all | solution.py:404
  55.8 2.2 %owner_update.1 = (f32[512,512]{1,0:T(8,128)}, f32[512,512]{1,0:T(8,128)}, bf16[512,512]{1,0:T(8,128)(2,1)S(1)}) custom-call(s32[1]{0:T(128)S(4)} %get-tuple-element.26.refresh_ref, bf16[512,512]{1,0:T(8,128)(2,1)S(1)} %bitcast.11, f32[512,512]{1,0:T(8,128)S(1)} %get-tuple-element.29.tie_ref.left_ref, f32[512,512]{1,0:T(8,128)S(1)} %get-tuple-element.35.right_ref, ...), custom_call_target="tpu_custom_call" | custom-call | tf_op jit(solution)/shard_map/owner_update/pallas_call | solution.py:290
  58.0 24.3 %all_to_all.11.refs_0_ = bf16[64,8,512]{2,1,0:T(8,128)(2,1)S(1)} all-to-all(bf16[64,8,512]{2,1,0:T(8,128)(2,1)S(1)} %bitcast.13), channel_id=1, replica_groups=mesh['dp'=4,'fsdp'=64] {'fsdp'}, dimensions={0} | all-to-all | bytes 1048576 | tf_op jit(solution)/shard_map/all_to_all | solution.py:410
  82.3 0.1 collective-permute-start.8
  82.4 1.5 %collective-permute-start.6 = (bf16[32,8,512]{2,1,0:T(8,128)(2,1)S(1)}, bf16[32,8,512]{2,1,0:T(8,128)(2,1)S(1)}, u32[]{:S(2)}, u32[]{:S(2)}) collective-permute-start(bf16[32,8,512]{2,1,0:T(8,128)(2,1)S(1)} %get-tuple-element.44.tie_ref), channel_id=1, source_target_pairs={{0,64},{64,128},{128,192},{192,0},{1,65},{65,129},{129,193},{193,1... | collective-permute-start | bytes 786440 | tf_op jit(solution)/shard_map/ppermute | solution.py:379
  83.9 0.0 collective-permute-start.10
  83.9 2.6 %collective-permute-start.11 = (bf16[32,8,512]{2,1,0:T(8,128)(2,1)S(1)}, bf16[32,8,512]{2,1,0:T(8,128)(2,1)S(1)}, u32[]{:S(2)}, u32[]{:S(2)}) collective-permute-start(bf16[32,8,512]{2,1,0:T(8,128)(2,1)S(1)} %get-tuple-element.44.tie_ref), channel_id=1, source_target_pairs={{0,192},{64,0},{128,64},{192,128},{1,193},{65,1},{129,65},{193,129... | collective-permute-start | bytes 786440 | tf_op jit(solution)/shard_map/ppermute | solution.py:382
  86.6 3.4 %collective-permute-done.8.refs_2_ = bf16[32,8,512]{2,1,0:T(8,128)(2,1)S(1)} collective-permute-done((bf16[32,8,512]{2,1,0:T(8,128)(2,1)S(1)}, bf16[32,8,512]{2,1,0:T(8,128)(2,1)S(1)}, u32[]{:S(2)}, u32[]{:S(2)}) %collective-permute-start.8) | collective-permute-done | bytes 262176 | tf_op jit(solution)/shard_map/ppermute | solution.py:382
  90.0 1.2 %collective-permute-start.9 = (bf16[32,8,512]{2,1,0:T(8,128)(2,1)S(1)}, bf16[32,8,512]{2,1,0:T(8,128)(2,1)S(1)}, u32[]{:S(2)}, u32[]{:S(2)}) collective-permute-start(bf16[32,8,512]{2,1,0:T(8,128)(2,1)S(1)} %collective-permute-done.8.refs_2_), channel_id=1, source_target_pairs={{0,192},{64,0},{128,64},{192,128},{1,193},{65,1},{129,65},{193,129... | collective-permute-start | bytes 786440 | tf_op jit(solution)/shard_map/ppermute | solution.py:382
  91.2 0.2 collective-permute-done.6.refs_1_
  91.5 0.0 collective-permute-start.7
  91.5 2.9 %owner_factors.1 = (f32[512,512]{1,0:T(8,128)}, f32[512,512]{1,0:T(8,128)}, f32[512,512]{1,0:T(8,128)}, f32[512,512]{1,0:T(8,128)}) custom-call(bf16[32,8,512]{2,1,0:T(8,128)(2,1)S(1)} %get-tuple-element.44.tie_ref, s32[1]{0:T(128)S(4)} %get-tuple-element.26.refresh_ref, ...), custom_call_target="tpu_custom_call", output_to_operand_aliasing={{2}: (7, {}), {3}: (8, {})} | custom-call | tf_op jit(solution)/shard_map/owner_factors/pallas_call | solution.py:353
  94.4 2.7 %collective-permute-done.10.refs_3_ = bf16[32,8,512]{2,1,0:T(8,128)(2,1)S(1)} collective-permute-done((bf16[32,8,512]{2,1,0:T(8,128)(2,1)S(1)}, bf16[32,8,512]{2,1,0:T(8,128)(2,1)S(1)}, u32[]{:S(2)}, u32[]{:S(2)}) %collective-permute-start.10) | collective-permute-done | bytes 262176 | tf_op jit(solution)/shard_map/ppermute | solution.py:379
  97.1 0.0 collective-permute-done.11.refs_4_
  97.1 1.3 %place_early.1.refs_2_ = bf16[256,8,512]{2,1,0:T(8,128)(2,1)} custom-call(s32[256]{0:T(256)S(4)} %get-tuple-element.24.index_ref, bf16[64,8,512]{2,1,0:T(8,128)(2,1)S(1)} %all_to_all.11.refs_0_, bf16[32,8,512]{2,1,0:T(8,128)(2,1)S(1)} %collective-permute-done.6.refs_1_, bf16[32,8,512]{2,1,0:T(8,128)(2,1)S(1)} %collective-permute-done.8.refs_2_, ...), custom_call_target="tpu_custom_call" | custom-call | bytes 83886080 | tf_op jit(solution)/shard_map/place_early/pallas_call | solution.py:120
  98.4 2.8 %collective-permute-done.9.refs_1_ = bf16[32,8,512]{2,1,0:T(8,128)(2,1)S(1)} collective-permute-done((bf16[32,8,512]{2,1,0:T(8,128)(2,1)S(1)}, bf16[32,8,512]{2,1,0:T(8,128)(2,1)S(1)}, u32[]{:S(2)}, u32[]{:S(2)}) %collective-permute-start.9) | collective-permute-done | bytes 262176 | tf_op jit(solution)/shard_map/ppermute | solution.py:382
  101.2 1.5 %collective-permute-done.7.refs_0_ = bf16[32,8,512]{2,1,0:T(8,128)(2,1)S(1)} collective-permute-done((bf16[32,8,512]{2,1,0:T(8,128)(2,1)S(1)}, bf16[32,8,512]{2,1,0:T(8,128)(2,1)S(1)}, u32[]{:S(2)}, u32[]{:S(2)}) %collective-permute-start.7) | collective-permute-done | bytes 262176 | tf_op jit(solution)/shard_map/ppermute | solution.py:379
  102.7 0.8 place_late.1
  (1 shorter events, 0.0 us)
Async XLA Ops:
  2.3 8.6 %collective-permute-start = (bf16[32,8,512]{2,1,0:T(8,128)(2,1)S(1)}, bf16[32,8,512]{2,1,0:T(8,128)(2,1)S(1)}, u32[]{:S(2)}, u32[]{:S(2)}) collective-permute-start(bf16[32,8,512]{2,1,0:T(8,128)(2,1)S(1)} %get-tuple-element.28), channel_id=1, source_target_pairs={{0,192},{64,0},{128,64},{192,128},{1,193},{65,1},{129,65},{193,129... | collective-permute-start | bytes 786440 | tf_op jit(solution)/shard_map/ppermute | solution.py:382
  6.0 8.5 %collective-permute-start.3 = (bf16[32,8,512]{2,1,0:T(8,128)(2,1)S(1)}, bf16[32,8,512]{2,1,0:T(8,128)(2,1)S(1)}, u32[]{:S(2)}, u32[]{:S(2)}) collective-permute-start(bf16[32,8,512]{2,1,0:T(8,128)(2,1)S(1)} %get-tuple-element.34), channel_id=1, source_target_pairs={{0,64},{64,128},{128,192},{192,0},{1,65},{65,129},{129,193},{193,1... | collective-permute-start | bytes 786440 | tf_op jit(solution)/shard_map/ppermute | solution.py:379
  7.0 9.5 %collective-permute-start.1 = (bf16[32,8,512]{2,1,0:T(8,128)(2,1)S(1)}, bf16[32,8,512]{2,1,0:T(8,128)(2,1)S(1)}, u32[]{:S(2)}, u32[]{:S(2)}) collective-permute-start(bf16[32,8,512]{2,1,0:T(8,128)(2,1)S(1)} %get-tuple-element.31), channel_id=1, source_target_pairs={{0,192},{64,0},{128,64},{192,128},{1,193},{65,1},{129,65},{193,129... | collective-permute-start | bytes 786440 | tf_op jit(solution)/shard_map/ppermute | solution.py:382
  9.8 9.9 %collective-permute-start.2 = (bf16[32,8,512]{2,1,0:T(8,128)(2,1)S(1)}, bf16[32,8,512]{2,1,0:T(8,128)(2,1)S(1)}, u32[]{:S(2)}, u32[]{:S(2)}) collective-permute-start(bf16[32,8,512]{2,1,0:T(8,128)(2,1)S(1)} %get-tuple-element.32), channel_id=1, source_target_pairs={{0,64},{64,128},{128,192},{192,0},{1,65},{65,129},{129,193},{193,1... | collective-permute-start | bytes 786440 | tf_op jit(solution)/shard_map/ppermute | solution.py:379
  11.0 11.2 %collective-permute-start.5 = (bf16[32,8,512]{2,1,0:T(8,128)(2,1)S(1)}, bf16[32,8,512]{2,1,0:T(8,128)(2,1)S(1)}, u32[]{:S(2)}, u32[]{:S(2)}) collective-permute-start(bf16[32,8,512]{2,1,0:T(8,128)(2,1)S(1)} %add_pieces.2.tie_ref), channel_id=1, source_target_pairs={{0,192},{64,0},{128,64},{192,128},{1,193},{65,1},{129,65},{193,129... | collective-permute-start | bytes 786440 | tf_op jit(solution)/shard_map/ppermute | solution.py:382
  14.6 10.7 %collective-permute-start.4 = (bf16[32,8,512]{2,1,0:T(8,128)(2,1)S(1)}, bf16[32,8,512]{2,1,0:T(8,128)(2,1)S(1)}, u32[]{:S(2)}, u32[]{:S(2)}) collective-permute-start(bf16[32,8,512]{2,1,0:T(8,128)(2,1)S(1)} %add_pieces.3), channel_id=1, source_target_pairs={{0,64},{64,128},{128,192},{192,0},{1,65},{65,129},{129,193},{193,1... | collective-permute-start | bytes 786440 | tf_op jit(solution)/shard_map/ppermute | solution.py:379
  82.3 7.7 %collective-permute-start.8 = (bf16[32,8,512]{2,1,0:T(8,128)(2,1)S(1)}, bf16[32,8,512]{2,1,0:T(8,128)(2,1)S(1)}, u32[]{:S(2)}, u32[]{:S(2)}) collective-permute-start(bf16[32,8,512]{2,1,0:T(8,128)(2,1)S(1)} %get-tuple-element.43), channel_id=1, source_target_pairs={{0,192},{64,0},{128,64},{192,128},{1,193},{65,1},{129,65},{193,129... | collective-permute-start | bytes 786440 | tf_op jit(solution)/shard_map/ppermute | solution.py:382
  82.4 9.0 %collective-permute-start.6 = (bf16[32,8,512]{2,1,0:T(8,128)(2,1)S(1)}, bf16[32,8,512]{2,1,0:T(8,128)(2,1)S(1)}, u32[]{:S(2)}, u32[]{:S(2)}) collective-permute-start(bf16[32,8,512]{2,1,0:T(8,128)(2,1)S(1)} %get-tuple-element.44.tie_ref), channel_id=1, source_target_pairs={{0,64},{64,128},{128,192},{192,0},{1,65},{65,129},{129,193},{193,1... | collective-permute-start | bytes 786440 | tf_op jit(solution)/shard_map/ppermute | solution.py:379
  83.9 13.2 %collective-permute-start.10 = (bf16[32,8,512]{2,1,0:T(8,128)(2,1)S(1)}, bf16[32,8,512]{2,1,0:T(8,128)(2,1)S(1)}, u32[]{:S(2)}, u32[]{:S(2)}) collective-permute-start(bf16[32,8,512]{2,1,0:T(8,128)(2,1)S(1)} %get-tuple-element.43), channel_id=1, source_target_pairs={{0,64},{64,128},{128,192},{192,0},{1,65},{65,129},{129,193},{193,1... | collective-permute-start | bytes 786440 | tf_op jit(solution)/shard_map/ppermute | solution.py:379
  83.9 13.2 %collective-permute-start.11 = (bf16[32,8,512]{2,1,0:T(8,128)(2,1)S(1)}, bf16[32,8,512]{2,1,0:T(8,128)(2,1)S(1)}, u32[]{:S(2)}, u32[]{:S(2)}) collective-permute-start(bf16[32,8,512]{2,1,0:T(8,128)(2,1)S(1)} %get-tuple-element.44.tie_ref), channel_id=1, source_target_pairs={{0,192},{64,0},{128,64},{192,128},{1,193},{65,1},{129,65},{193,129... | collective-permute-start | bytes 786440 | tf_op jit(solution)/shard_map/ppermute | solution.py:382
  90.0 11.2 %collective-permute-start.9 = (bf16[32,8,512]{2,1,0:T(8,128)(2,1)S(1)}, bf16[32,8,512]{2,1,0:T(8,128)(2,1)S(1)}, u32[]{:S(2)}, u32[]{:S(2)}) collective-permute-start(bf16[32,8,512]{2,1,0:T(8,128)(2,1)S(1)} %collective-permute-done.8.refs_2_), channel_id=1, source_target_pairs={{0,192},{64,0},{128,64},{192,128},{1,193},{65,1},{129,65},{193,129... | collective-permute-start | bytes 786440 | tf_op jit(solution)/shard_map/ppermute | solution.py:382
  91.5 11.2 %collective-permute-start.7 = (bf16[32,8,512]{2,1,0:T(8,128)(2,1)S(1)}, bf16[32,8,512]{2,1,0:T(8,128)(2,1)S(1)}, u32[]{:S(2)}, u32[]{:S(2)}) collective-permute-start(bf16[32,8,512]{2,1,0:T(8,128)(2,1)S(1)} %collective-permute-done.6.refs_1_), channel_id=1, source_target_pairs={{0,64},{64,128},{128,192},{192,0},{1,65},{65,129},{129,193},{193,1... | collective-permute-start | bytes 786440 | tf_op jit(solution)/shard_map/ppermute | solution.py:379

commit v4 on v3

--- a/solution.py
+++ b/solution.py
@@ -25,13 +25,18 @@
     )
 
 
-def piece_start(quarter, first, slots):
-    return lax.rem(lax.axis_index("dp") + quarter, N_DP) * (slots // N_DP) + first
+def core_index():
+    return lax.rem(lax.axis_index("fsdp"), 2)
+
+
+def piece_slots(quarter, parity, slots):
+    start = lax.rem(lax.axis_index("dp") + quarter, N_DP) * (slots // N_DP)
+    return start + lax.rem(core_index() + parity, 2)
 
 
 def copy_rows(index_smem, source_ref, out_ref, start):
     def body(slot, carry):
-        out_ref[slot] = source_ref[index_smem[start + slot]]
+        out_ref[slot] = source_ref[index_smem[start + 2 * slot]]
         return carry
 
     lax.fori_loop(0, out_ref.shape[0], body, 0, unroll=8)
@@ -56,22 +61,22 @@
     fetch.wait()
     for load in loads:
         load.wait()
-    for (quarter, first), out_ref in zip(pieces, outs, strict=True):
-        copy_rows(index_smem, held_ref, out_ref, piece_start(quarter, first, index_ref.shape[0]))
+    for (quarter, parity), out_ref in zip(pieces, outs, strict=True):
+        copy_rows(index_smem, held_ref, out_ref, piece_slots(quarter, parity, index_ref.shape[0]))
 
 
 def order_rest_kernel(pieces, index_ref, refresh_ref, held_ref, refresh_smem, *outs):
     refresh_smem[0] = refresh_ref[0]
-    for (quarter, first), out_ref in zip(pieces, outs, strict=True):
-        copy_rows(index_ref, held_ref, out_ref, piece_start(quarter, first, index_ref.shape[0]))
-
-
-def order_first(index, source, pieces, counts):
-    tail = source.shape[1:]
+    for (quarter, parity), out_ref in zip(pieces, outs, strict=True):
+        copy_rows(index_ref, held_ref, out_ref, piece_slots(quarter, parity, index_ref.shape[0]))
+
+
+def order_first(index, source, pieces):
+    piece = (source.shape[0] // N_DP // 2, *source.shape[1:])
     return pl.pallas_call(
         functools.partial(order_first_kernel, pieces),
         out_shape=[VMEM(source.shape, source.dtype), SMEM(index.shape, index.dtype)]
-        + [VMEM((count, *tail), source.dtype) for count in counts],
+        + [VMEM(piece, source.dtype) for _ in pieces],
         in_specs=[pl.BlockSpec(memory_space=HBM)] * 2,
         out_specs=[pl.BlockSpec(memory_space=VMEM), pl.BlockSpec(memory_space=SMEM)]
         + [pl.BlockSpec(memory_space=VMEM)] * len(pieces),
@@ -84,11 +89,12 @@
     )
 
 
-def order_rest(index, refresh, held, pieces, counts):
+def order_rest(index, refresh, held, pieces):
+    piece = (held.shape[0] // N_DP // 2, *held.shape[1:])
     return pl.pallas_call(
         functools.partial(order_rest_kernel, pieces),
         out_shape=[SMEM(refresh.shape, refresh.dtype)]
-        + [VMEM((count, *held.shape[1:]), held.dtype) for count in counts],
+        + [VMEM(piece, held.dtype) for _ in pieces],
         in_specs=[pl.BlockSpec(memory_space=space) for space in (SMEM, SMEM, VMEM)],
         out_specs=[pl.BlockSpec(memory_space=SMEM)]
         + [pl.BlockSpec(memory_space=VMEM)] * len(pieces),
@@ -100,12 +106,12 @@
 def place_kernel(pieces, aliased, index_ref, *refs):
     sources = refs[: len(pieces)]
     out_ref, sems = refs[len(pieces) + aliased :]
-    for number, ((quarter, first), source_ref) in enumerate(zip(pieces, sources, strict=True)):
-        start = piece_start(quarter, first, index_ref.shape[0])
+    for number, ((quarter, parity), source_ref) in enumerate(zip(pieces, sources, strict=True)):
+        start = piece_slots(quarter, parity, index_ref.shape[0])
 
         def body(slot, carry, source_ref=source_ref, number=number, start=start):
             pltpu.make_async_copy(
-                source_ref.at[slot], out_ref.at[index_ref[start + slot]], sems.at[number]
+                source_ref.at[slot], out_ref.at[index_ref[start + 2 * slot]], sems.at[number]
             ).start()
             return carry
 
@@ -133,58 +139,59 @@
     )(index, *sources, *(() if out is None else (out,)))
 
 
-def add_kernel(first_ref, second_ref, out_ref):
-    total = first_ref[...].astype(jnp.float32) + second_ref[...].astype(jnp.float32)
-    out_ref[...] = total.astype(out_ref.dtype)
-
-
-def add_pieces(first, second):
+def add_kernel(*refs):
+    total = refs[0][...].astype(jnp.float32) + refs[1][...].astype(jnp.float32)
+    refs[-1][...] = total.astype(refs[-1].dtype)
+
+
+def add_pieces(first, second, dtype, name, tie=None):
+    ties = () if tie is None else (tie,)
     return pl.pallas_call(
         add_kernel,
-        out_shape=jax.ShapeDtypeStruct(first.shape, first.dtype),
-        in_specs=[pl.BlockSpec(memory_space=VMEM)] * 2,
+        out_shape=VMEM(first.shape, dtype),
+        in_specs=[pl.BlockSpec(memory_space=VMEM)] * 2
+        + [pl.BlockSpec(memory_space=pl.ANY)] * len(ties),
         out_specs=pl.BlockSpec(memory_space=VMEM),
-        compiler_params=pltpu.CompilerParams(vmem_limit_bytes=4 * 2**20),
-        name="add_pieces",
-    )(first, second)
-
-
-def partial_kernel(mine_ref, raw_a_ref, raw_b_ref, out_ref):
-    half = raw_a_ref.shape[0]
-    for start, raw_ref in ((0, raw_a_ref), (half, raw_b_ref)):
-        part = pl.ds(start, half)
-        out_ref[part] = mine_ref[part].astype(jnp.float32) + raw_ref[...].astype(jnp.float32)
-
-
-def partial_sum(mine, raw_a, raw_b):
-    return pl.pallas_call(
-        partial_kernel,
-        out_shape=VMEM(mine.shape, jnp.float32),
+        compiler_params=pltpu.CompilerParams(vmem_limit_bytes=6 * 2**20),
+        name=name,
+    )(first, second, *ties)
+
+
+def join_kernel(partial_ref, comb_ref, other_ref, out_ref):
+    me = core_index()
+    total = partial_ref[...] + comb_ref[...].astype(jnp.float32)
+    out_ref[:, me] = total.astype(out_ref.dtype)
+    out_ref[:, 1 - me] = other_ref[...]
+
+
+def join_cores(partial, comb, other):
+    slots, rows, columns = comb.shape
+    return pl.pallas_call(
+        join_kernel,
+        out_shape=VMEM((slots, 2, rows, columns), comb.dtype),
         in_specs=[pl.BlockSpec(memory_space=VMEM)] * 3,
         out_specs=pl.BlockSpec(memory_space=VMEM),
         compiler_params=pltpu.CompilerParams(vmem_limit_bytes=6 * 2**20),
-        name="partial_sum",
-    )(mine, raw_a, raw_b)
-
-
-def total_kernel(tie_ref, partial_ref, comb_a_ref, comb_b_ref, out_ref):
-    del tie_ref
-    half = comb_a_ref.shape[0]
-    for start, comb_ref in ((0, comb_a_ref), (half, comb_b_ref)):
-        part = pl.ds(start, half)
-        total = partial_ref[part] + comb_ref[...].astype(jnp.float32)
-        out_ref[part] = total.astype(out_ref.dtype)
-
-
-def total_sum(tie, partial, comb_a, comb_b):
-    return pl.pallas_call(
-        total_kernel,
-        out_shape=VMEM(partial.shape, comb_a.dtype),
-        in_specs=[pl.BlockSpec(memory_space=pl.ANY)] + [pl.BlockSpec(memory_space=VMEM)] * 3,
-        out_specs=pl.BlockSpec(memory_space=VMEM),
+        name="join_cores",
+    )(partial, comb, other)
+
+
+def split_kernel(rows_ref, mine_ref, other_ref):
+    me = core_index()
+    mine_ref[...] = rows_ref[:, me]
+    other_ref[...] = rows_ref[:, 1 - me]
+
+
+def split_cores(rows):
+    slots, _, count, columns = rows.shape
+    return pl.pallas_call(
+        split_kernel,
+        out_shape=[VMEM((slots, count, columns), rows.dtype)] * 2,
+        in_specs=[pl.BlockSpec(memory_space=VMEM)],
+        out_specs=[pl.BlockSpec(memory_space=VMEM)] * 2,
         compiler_params=pltpu.CompilerParams(vmem_limit_bytes=6 * 2**20),
-        name="total_sum",
-    )(tie, partial, comb_a, comb_b)
+        name="split_cores",
+    )(rows)
 
 
 def inverse_roots(factors):
@@ -373,7 +380,7 @@
     shard_count = lax.axis_size("fsdp")
     local = grads[0]
     blocks, piece_rows, order = local.shape
-    quarter, half = blocks // N_DP, blocks // N_DP // 2
+    chips = shard_count // 2
 
     def to_next(piece):
         return lax.ppermute(piece, "dp", [(i, (i + 1) % N_DP) for i in range(N_DP)])
@@ -381,49 +388,54 @@
     def to_prev(piece):
         return lax.ppermute(piece, "dp", [(i, (i - 1) % N_DP) for i in range(N_DP)])
 
-    held, index, relay_a, relay_b = order_first(
-        block_of_slot, local, ((2, 0), (2, half)), (half, half)
-    )
-    relayed_a, relayed_b = to_next(relay_a), to_prev(relay_b)
-    refresh, raw_a, raw_b, own_a, own_b, mine = order_rest(
-        index,
-        refresh,
-        held,
-        ((3, 0), (1, half), (1, 0), (3, half), (0, 0)),
-        (half, half, half, half, quarter),
-    )
-    raw_a, raw_b = to_prev(raw_a), to_next(raw_b)
-    sum_a, sum_b = add_pieces(own_a, relayed_a), add_pieces(own_b, relayed_b)
-    comb_a, comb_b = to_next(sum_a), to_prev(sum_b)
-    left, right = load_matrices(sum_b, left_factor[0], right_factor[0])
+    def to_core(piece):
+        return lax.ppermute(piece, "fsdp", [(i, i ^ 1) for i in range(shard_count)])
+
+    def over_chips(rows):
+        groups = [list(range(core, shard_count, 2)) for core in range(2)]
+        return lax.all_to_all(
+            rows, "fsdp", split_axis=0, concat_axis=0, axis_index_groups=groups, tiled=True
+        )
+
+    held, index, relay_b, relay_a = order_first(block_of_slot, local, ((2, 1), (2, 0)))
+    relayed_b, relayed_a = to_prev(relay_b), to_next(relay_a)
+    refresh, raw_b, raw_a, own_b, own_a, mine_b, mine_a = order_rest(
+        index, refresh, held, ((1, 1), (3, 0), (3, 1), (1, 0), (0, 1), (0, 0))
+    )
+    raw_b, raw_a = to_next(raw_b), to_prev(raw_a)
+    sum_b = add_pieces(own_b, relayed_b, own_b.dtype, "add_relay")
+    sum_a = add_pieces(own_a, relayed_a, own_a.dtype, "add_relay")
+    comb_b, comb_a = to_prev(sum_b), to_next(sum_a)
+    left, right = load_matrices(sum_a, left_factor[0], right_factor[0])
     lroot, rroot = (
         pltpu.with_memory_space_constraint(root[0], HBM) for root in (left_root, right_root)
     )
-    summed = total_sum(left, partial_sum(mine, raw_a, raw_b), comb_a, comb_b)
-
-    grad = lax.all_to_all(summed, "fsdp", split_axis=0, concat_axis=0, tiled=True)
-    grad = grad.reshape(order, order)
+    partial_b = add_pieces(mine_b, raw_b, jnp.float32, "add_raw", left)
+    partial_a = add_pieces(mine_a, raw_a, jnp.float32, "add_raw")
+    other = to_core(add_pieces(partial_b, comb_b, comb_b.dtype, "add_comb"))
+    grad = over_chips(join_cores(partial_a, comb_a, other)).reshape(order, order)
 
     new_lroot, new_rroot, update = owner_update(refresh, grad, left, right, lroot, rroot)
 
-    rows = update.reshape(shard_count, piece_rows, order)
-    rows = lax.all_to_all(rows, "fsdp", split_axis=0, concat_axis=0, tiled=True)
-    rows_a, rows_b = rows[:half], rows[half:]
-    prev_a, next_b = to_next(rows_a), to_prev(rows_b)
+    rows = over_chips(update.reshape(chips, 2, piece_rows, order))
+    rows_a, other = split_cores(rows)
+    prev_a = to_next(rows_a)
+    rows_b = to_core(other)
+    next_b = to_prev(rows_b)
     prev_b, next_a = to_next(rows_b), to_prev(rows_a)
+    over_a, over_b = to_next(prev_a), to_prev(next_b)
     new_left, new_right, new_lroot, new_rroot = owner_factors(
         rows_a, refresh, grad, left, right, lroot, rroot, new_lroot, new_rroot
     )
     over_a, over_b = to_next(prev_a), to_prev(next_b)
     updates = place_blocks(
         index,
-        (rows, prev_a, next_b, prev_b, next_a),
-        ((0, 0), (3, 0), (1, half), (3, half), (1, 0)),
+        (rows_a, rows_b, prev_a, next_b, prev_b, next_a),
+        ((0, 0), (0, 1), (3, 0), (1, 1), (3, 1), (1, 0)),
         "place_early",
     )
-    updates = place_blocks(
-        index, (over_a, over_b), ((2, 0), (2, half)), "place_late", updates
-    )
+    updates = place_blocks(index, (over_a,), ((2, 0),), "place_over", updates)
+    updates = place_blocks(index, (over_b,), ((2, 1),), "place_last", updates)
     return new_left[None], new_right[None], new_lroot[None], new_rroot[None], updates
 
 

time: 104 us -> 99.2 us (0.954)
  blocking collectives: 54.8 us -> 42.6 us
  starting transfers between devices: 15.4 us -> 25.9 us
  waiting for transfers between devices: 20.7 us -> 16.8 us
    all_to_all x2, blocking collectives: 54.8 us -> 42.6 us  [over_chips(): lax.all_to_all(rows, 'fsdp', split_axis=0, concat_axis=0, axis_index_grou...]
    ppermute x0 -> x2, starting transfers between devices: none -> 10.2 us  [to_core(): return lax.ppermute(piece, 'fsdp', [(i, i ^ 1) for i in range(shard_count)])]
    ppermute x6, waiting for transfers between devices: 10.1 us -> 4.77 us  [to_prev(): return lax.ppermute(piece, 'dp', [(i, (i - 1) % N_DP) for i in range(N_DP)])]
    ppermute x0 -> x2, waiting for transfers between devices: none -> 1.16 us  [to_core(): return lax.ppermute(piece, 'fsdp', [(i, i ^ 1) for i in range(shard_count)])]
    ppermute x6, starting transfers between devices: 1.58 us -> 2.71 us  [to_next(): return lax.ppermute(piece, 'dp', [(i, (i + 1) % N_DP) for i in range(N_DP)])]
    pallas_call x2 -> x3, Pallas kernels: 2.19 us -> 2.84 us  [place_blocks(): pl.pallas_call(functools.partial(place_kernel, pieces, aliased), out_shap...]
  transfers between devices with their start and end apart: 12 -> 14, of which waited for: 10 -> 7; matrix products, arithmetic and copies ran while one was open for 0% -> 0% of each run, Pallas kernels for 6% -> 7%
where the time goes in v4:
time: 99.2 us; the launch traced here: 98.8 us
  blocking collectives  42.6 us (43%)
  starting transfers between devices  25.9 us (26%)
  waiting for transfers between devices  16.8 us (17%)
  Pallas kernels  12 us (12%)
  between operations  1.57 us (2%)
    all_to_all x2, blocking collectives, over_chips(): lax.all_to_all(rows, 'fsdp', split_axis=0, concat_axis=0, axis_index_grou...  42.6 us
    ppermute x6, starting transfers between devices, to_prev(): return lax.ppermute(piece, 'dp', [(i, (i - 1) % N_DP) for i in range(N_DP)])  13 us
    ppermute x6, waiting for transfers between devices, to_next(): return lax.ppermute(piece, 'dp', [(i, (i + 1) % N_DP) for i in range(N_DP)])  10.9 us
    ppermute x2, starting transfers between devices, to_core(): return lax.ppermute(piece, 'fsdp', [(i, i ^ 1) for i in range(shard_count)])  10.2 us
    ppermute x6, waiting for transfers between devices, to_prev(): return lax.ppermute(piece, 'dp', [(i, (i - 1) % N_DP) for i in range(N_DP)])  4.77 us
    pallas_call x1, Pallas kernels, owner_factors(): pl.pallas_call(factors_kernel, out_shape=(HBM((order, order), jnp.float32...  2.96 us
    pallas_call x3, Pallas kernels, place_blocks(): pl.pallas_call(functools.partial(place_kernel, pieces, aliased), out_shap...  2.84 us
    ppermute x6, starting transfers between devices, to_next(): return lax.ppermute(piece, 'dp', [(i, (i + 1) % N_DP) for i in range(N_DP)])  2.71 us
  transfers between devices with their start and end apart: 14, of which 7 were waited for; matrix products, arithmetic and copies ran while one was open for 0% of the time, Pallas kernels for 7%

profile of v4, /device:TPU:1, one launch (start us, length us, event | category | flops | bytes accessed | tf_op | source)
XLA Modules:
  0.0 98.8 jit_solution(15234155642036222491)
XLA Ops:
  0.6 1.7 %order_first.1 = (bf16[256,8,512]{2,1,0:T(8,128)(2,1)S(1)}, s32[256]{0:T(256)S(4)}, bf16[32,8,512]{2,1,0:T(8,128)(2,1)S(1)}, bf16[32,8,512]{2,1,0:T(8,128)(2,1)S(1)}) custom-call(s32[256]{0:T(256)} %index_ref.1, bf16[256,8,512]{2,1,0:T(8,128)(2,1)} %bitcast.18), custom_call_target="tpu_custom_call" | custom-call | tf_op jit(solution)/shard_map/order_first/pallas_call | solution.py:76
  2.3 3.6 %collective-permute-start.4 = (bf16[32,8,512]{2,1,0:T(8,128)(2,1)S(1)}, bf16[32,8,512]{2,1,0:T(8,128)(2,1)S(1)}, u32[]{:S(2)}, u32[]{:S(2)}) collective-permute-start(bf16[32,8,512]{2,1,0:T(8,128)(2,1)S(1)} %get-tuple-element.38), channel_id=1, source_target_pairs={{0,192},{64,0},{128,64},{192,128},{1,193},{65,1},{129,65},{193,129... | collective-permute-start | bytes 786440 | tf_op jit(solution)/shard_map/ppermute | solution.py:389
  6.0 0.0 collective-permute-start.1
  6.6 0.4 order_rest.1
  7.0 0.1 collective-permute-start.3
  7.1 3.8 %collective-permute-done.4.refs_1_ = bf16[32,8,512]{2,1,0:T(8,128)(2,1)S(1)} collective-permute-done((bf16[32,8,512]{2,1,0:T(8,128)(2,1)S(1)}, bf16[32,8,512]{2,1,0:T(8,128)(2,1)S(1)}, u32[]{:S(2)}, u32[]{:S(2)}) %collective-permute-start.4) | collective-permute-done | bytes 262176 | tf_op jit(solution)/shard_map/ppermute | solution.py:389
  10.9 0.1 add_relay.3
  11.0 3.5 %collective-permute-start.5 = (bf16[32,8,512]{2,1,0:T(8,128)(2,1)S(1)}, bf16[32,8,512]{2,1,0:T(8,128)(2,1)S(1)}, u32[]{:S(2)}, u32[]{:S(2)}) collective-permute-start(bf16[32,8,512]{2,1,0:T(8,128)(2,1)S(1)} %add_relay.3), channel_id=1, source_target_pairs={{0,192},{64,0},{128,64},{192,128},{1,193},{65,1},{129,65},{193,129... | collective-permute-start | bytes 786440 | tf_op jit(solution)/shard_map/ppermute | solution.py:389
  14.5 0.1 collective-permute-start
  14.6 0.0 collective-permute-done.1.refs_1_
  14.6 0.1 add_relay.2.tie_ref
  14.7 1.5 %collective-permute-start.2 = (bf16[32,8,512]{2,1,0:T(8,128)(2,1)S(1)}, bf16[32,8,512]{2,1,0:T(8,128)(2,1)S(1)}, u32[]{:S(2)}, u32[]{:S(2)}) collective-permute-start(bf16[32,8,512]{2,1,0:T(8,128)(2,1)S(1)} %add_relay.2.tie_ref), channel_id=1, source_target_pairs={{0,64},{64,128},{128,192},{192,0},{1,65},{65,129},{129,193},{193,1... | collective-permute-start | bytes 786440 | tf_op jit(solution)/shard_map/ppermute | solution.py:386
  16.1 1.6 %load_matrices.1 = (f32[512,512]{1,0:T(8,128)S(1)}, f32[512,512]{1,0:T(8,128)S(1)}) custom-call(bf16[32,8,512]{2,1,0:T(8,128)(2,1)S(1)} %add_relay.2.tie_ref, f32[512,512]{1,0:T(8,128)} %bitcast.21, f32[512,512]{1,0:T(8,128)} %bitcast.22), custom_call_target="tpu_custom_call" | custom-call | tf_op jit(solution)/shard_map/load_matrices/pallas_call | solution.py:239
  17.7 2.0 %collective-permute-done.3.refs_1_ = bf16[32,8,512]{2,1,0:T(8,128)(2,1)S(1)} collective-permute-done((bf16[32,8,512]{2,1,0:T(8,128)(2,1)S(1)}, bf16[32,8,512]{2,1,0:T(8,128)(2,1)S(1)}, u32[]{:S(2)}, u32[]{:S(2)}) %collective-permute-start.3) | collective-permute-done | bytes 262176 | tf_op jit(solution)/shard_map/ppermute | solution.py:386
  19.7 0.1 add_raw.3.refs_0_
  19.7 0.0 collective-permute-done.5.refs_1_
  19.8 3.4 %collective-permute-start.6 = (bf16[32,8,512]{2,1,0:T(8,128)(2,1)S(1)}, bf16[32,8,512]{2,1,0:T(8,128)(2,1)S(1)}, u32[]{:S(2)}, u32[]{:S(2)}) collective-permute-start(bf16[32,8,512]{2,1,0:T(8,128)(2,1)S(1)} %add_comb.1), channel_id=1, source_target_pairs={{0,1},{1,0},{2,3},{3,2},{4,5},{5,4},{6,7},{7,6},{8,9},{9,8},{10,11... | collective-permute-start | bytes 786440 | tf_op jit(solution)/shard_map/ppermute | solution.py:392
  23.2 0.9 collective-permute-done.refs_1_
  24.2 0.1 add_raw.2.partial_ref
  24.2 1.0 %collective-permute-done.2.comb_ref = bf16[32,8,512]{2,1,0:T(8,128)(2,1)S(1)} collective-permute-done((bf16[32,8,512]{2,1,0:T(8,128)(2,1)S(1)}, bf16[32,8,512]{2,1,0:T(8,128)(2,1)S(1)}, u32[]{:S(2)}, u32[]{:S(2)}) %collective-permute-start.2) | collective-permute-done | bytes 262176 | tf_op jit(solution)/shard_map/ppermute | solution.py:386
  25.3 0.0 collective-permute-done.6.other_ref
  25.3 0.1 join_cores.1
  25.3 23.8 %all_to_all.10 = bf16[32,2,8,512]{3,2,1,0:T(8,128)(2,1)S(1)} all-to-all(bf16[32,2,8,512]{3,2,1,0:T(8,128)(2,1)S(1)} %join_cores.1), channel_id=1, replica_groups={{0,2,4,6,8,10,12,14,16,18,20,22,24,26,28,30,32,34,36,38,40,42,44,46,48,..., dimensions={0} | all-to-all | bytes 1048576 | tf_op jit(solution)/shard_map/all_to_all | solution.py:396
  49.1 2.2 %owner_update.1 = (f32[512,512]{1,0:T(8,128)}, f32[512,512]{1,0:T(8,128)}, bf16[512,512]{1,0:T(8,128)(2,1)S(1)}) custom-call(s32[1]{0:T(128)S(4)} %get-tuple-element.29.refresh_ref, bf16[512,512]{1,0:T(8,128)(2,1)S(1)} %bitcast.11, f32[512,512]{1,0:T(8,128)S(1)} %get-tuple-element.36.refs_2_.left_ref, f32[512,512]{1,0:T(8,128)S(1)} %get-tuple-element.39.right_ref, ...), custom_call_target="tpu_custom_call" | custom-call | tf_op jit(solution)/shard_map/owner_update/pallas_call | solution.py:297
  51.3 18.8 %all_to_all.11.rows_ref = bf16[32,2,8,512]{3,2,1,0:T(8,128)(2,1)S(1)} all-to-all(bf16[32,2,8,512]{3,2,1,0:T(8,128)(2,1)S(1)} %bitcast.13), channel_id=1, replica_groups={{0,2,4,6,8,10,12,14,16,18,20,22,24,26,28,30,32,34,36,38,40,42,44,46,48,..., dimensions={0} | all-to-all | bytes 1048576 | tf_op jit(solution)/shard_map/all_to_all | solution.py:396
  70.1 6.7 %collective-permute-start.7 = (bf16[32,8,512]{2,1,0:T(8,128)(2,1)S(1)}, bf16[32,8,512]{2,1,0:T(8,128)(2,1)S(1)}, u32[]{:S(2)}, u32[]{:S(2)}) collective-permute-start(bf16[32,8,512]{2,1,0:T(8,128)(2,1)S(1)} %get-tuple-element.48), channel_id=1, source_target_pairs={{0,1},{1,0},{2,3},{3,2},{4,5},{5,4},{6,7},{7,6},{8,9},{9,8},{10,11... | collective-permute-start | bytes 786440 | tf_op jit(solution)/shard_map/ppermute | solution.py:392
  76.9 0.0 collective-permute-start.10
  76.9 1.2 %collective-permute-done.7.refs_1_ = bf16[32,8,512]{2,1,0:T(8,128)(2,1)S(1)} collective-permute-done((bf16[32,8,512]{2,1,0:T(8,128)(2,1)S(1)}, bf16[32,8,512]{2,1,0:T(8,128)(2,1)S(1)}, u32[]{:S(2)}, u32[]{:S(2)}) %collective-permute-start.7) | collective-permute-done | bytes 262176 | tf_op jit(solution)/shard_map/ppermute | solution.py:392
  78.0 2.3 %collective-permute-start.8 = (bf16[32,8,512]{2,1,0:T(8,128)(2,1)S(1)}, bf16[32,8,512]{2,1,0:T(8,128)(2,1)S(1)}, u32[]{:S(2)}, u32[]{:S(2)}) collective-permute-start(bf16[32,8,512]{2,1,0:T(8,128)(2,1)S(1)} %collective-permute-done.7.refs_1_), channel_id=1, source_target_pairs={{0,192},{64,0},{128,64},{192,128},{1,193},{65,1},{129,65},{193,129... | collective-permute-start | bytes 786440 | tf_op jit(solution)/shard_map/ppermute | solution.py:389
  80.3 0.3 collective-permute-start.13
  80.7 1.1 %collective-permute-start.12 = (bf16[32,8,512]{2,1,0:T(8,128)(2,1)S(1)}, bf16[32,8,512]{2,1,0:T(8,128)(2,1)S(1)}, u32[]{:S(2)}, u32[]{:S(2)}) collective-permute-start(bf16[32,8,512]{2,1,0:T(8,128)(2,1)S(1)} %collective-permute-done.7.refs_1_), channel_id=1, source_target_pairs={{0,64},{64,128},{128,192},{192,0},{1,65},{65,129},{129,193},{193,1... | collective-permute-start | bytes 786440 | tf_op jit(solution)/shard_map/ppermute | solution.py:386
  81.8 4.1 %collective-permute-done.10.refs_2_ = bf16[32,8,512]{2,1,0:T(8,128)(2,1)S(1)} collective-permute-done((bf16[32,8,512]{2,1,0:T(8,128)(2,1)S(1)}, bf16[32,8,512]{2,1,0:T(8,128)(2,1)S(1)}, u32[]{:S(2)}, u32[]{:S(2)}) %collective-permute-start.10) | collective-permute-done | bytes 262176 | tf_op jit(solution)/shard_map/ppermute | solution.py:386
  85.9 0.0 collective-permute-start.11
  85.9 0.0 collective-permute-done.8.refs_3_
  85.9 3.1 %collective-permute-start.9 = (bf16[32,8,512]{2,1,0:T(8,128)(2,1)S(1)}, bf16[32,8,512]{2,1,0:T(8,128)(2,1)S(1)}, u32[]{:S(2)}, u32[]{:S(2)}) collective-permute-start(bf16[32,8,512]{2,1,0:T(8,128)(2,1)S(1)} %collective-permute-done.8.refs_3_), channel_id=1, source_target_pairs={{0,192},{64,0},{128,64},{192,128},{1,193},{65,1},{129,65},{193,129... | collective-permute-start | bytes 786440 | tf_op jit(solution)/shard_map/ppermute | solution.py:389
  89.1 3.0 %owner_factors.1 = (f32[512,512]{1,0:T(8,128)}, f32[512,512]{1,0:T(8,128)}, f32[512,512]{1,0:T(8,128)}, f32[512,512]{1,0:T(8,128)}) custom-call(bf16[32,8,512]{2,1,0:T(8,128)(2,1)S(1)} %get-tuple-element.41.tie_ref.refs_0_, s32[1]{0:T(128)S(4)} %get-tuple-element.29.refresh_ref, ...), custom_call_target="tpu_custom_call", output_to_operand_aliasing={{2}: (7, {}), {3}: (8, {})} | custom-call | tf_op jit(solution)/shard_map/owner_factors/pallas_call | solution.py:360
  92.0 0.0 collective-permute-done.13.refs_5_
  92.0 0.0 collective-permute-done.12.refs_4_
  92.1 1.4 %place_early.1.refs_1_ = bf16[256,8,512]{2,1,0:T(8,128)(2,1)} custom-call(s32[256]{0:T(256)S(4)} %get-tuple-element.27.index_ref, bf16[32,8,512]{2,1,0:T(8,128)(2,1)S(1)} %get-tuple-element.41.tie_ref.refs_0_, bf16[32,8,512]{2,1,0:T(8,128)(2,1)S(1)} %collective-permute-done.7.refs_1_, bf16[32,8,512]{2,1,0:T(8,128)(2,1)S(1)} %collective-permute-done.10.refs_2_, ...), custom_call_target="tpu_custom_call" | custom-call | bytes 100663296 | tf_op jit(solution)/shard_map/place_early/pallas_call | solution.py:126
  93.4 3.7 %collective-permute-done.11.refs_0_ = bf16[32,8,512]{2,1,0:T(8,128)(2,1)S(1)} collective-permute-done((bf16[32,8,512]{2,1,0:T(8,128)(2,1)S(1)}, bf16[32,8,512]{2,1,0:T(8,128)(2,1)S(1)}, u32[]{:S(2)}, u32[]{:S(2)}) %collective-permute-start.11) | collective-permute-done | bytes 262176 | tf_op jit(solution)/shard_map/ppermute | solution.py:386
  97.2 0.7 place_over.1.refs_1_
  97.9 0.0 collective-permute-done.9.refs_0_
  97.9 0.7 place_last.1
  (2 shorter events, 0.1 us)
Async XLA Ops:
  2.3 8.6 %collective-permute-start.4 = (bf16[32,8,512]{2,1,0:T(8,128)(2,1)S(1)}, bf16[32,8,512]{2,1,0:T(8,128)(2,1)S(1)}, u32[]{:S(2)}, u32[]{:S(2)}) collective-permute-start(bf16[32,8,512]{2,1,0:T(8,128)(2,1)S(1)} %get-tuple-element.38), channel_id=1, source_target_pairs={{0,192},{64,0},{128,64},{192,128},{1,193},{65,1},{129,65},{193,129... | collective-permute-start | bytes 786440 | tf_op jit(solution)/shard_map/ppermute | solution.py:389
  6.0 8.6 %collective-permute-start.1 = (bf16[32,8,512]{2,1,0:T(8,128)(2,1)S(1)}, bf16[32,8,512]{2,1,0:T(8,128)(2,1)S(1)}, u32[]{:S(2)}, u32[]{:S(2)}) collective-permute-start(bf16[32,8,512]{2,1,0:T(8,128)(2,1)S(1)} %get-tuple-element.33), channel_id=1, source_target_pairs={{0,64},{64,128},{128,192},{192,0},{1,65},{65,129},{129,193},{193,1... | collective-permute-start | bytes 786440 | tf_op jit(solution)/shard_map/ppermute | solution.py:386
  7.0 12.6 %collective-permute-start.3 = (bf16[32,8,512]{2,1,0:T(8,128)(2,1)S(1)}, bf16[32,8,512]{2,1,0:T(8,128)(2,1)S(1)}, u32[]{:S(2)}, u32[]{:S(2)}) collective-permute-start(bf16[32,8,512]{2,1,0:T(8,128)(2,1)S(1)} %get-tuple-element.35), channel_id=1, source_target_pairs={{0,64},{64,128},{128,192},{192,0},{1,65},{65,129},{129,193},{193,1... | collective-permute-start | bytes 786440 | tf_op jit(solution)/shard_map/ppermute | solution.py:386
  11.0 8.7 %collective-permute-start.5 = (bf16[32,8,512]{2,1,0:T(8,128)(2,1)S(1)}, bf16[32,8,512]{2,1,0:T(8,128)(2,1)S(1)}, u32[]{:S(2)}, u32[]{:S(2)}) collective-permute-start(bf16[32,8,512]{2,1,0:T(8,128)(2,1)S(1)} %add_relay.3), channel_id=1, source_target_pairs={{0,192},{64,0},{128,64},{192,128},{1,193},{65,1},{129,65},{193,129... | collective-permute-start | bytes 786440 | tf_op jit(solution)/shard_map/ppermute | solution.py:389
  14.5 9.7 %collective-permute-start = (bf16[32,8,512]{2,1,0:T(8,128)(2,1)S(1)}, bf16[32,8,512]{2,1,0:T(8,128)(2,1)S(1)}, u32[]{:S(2)}, u32[]{:S(2)}) collective-permute-start(bf16[32,8,512]{2,1,0:T(8,128)(2,1)S(1)} %get-tuple-element.31), channel_id=1, source_target_pairs={{0,192},{64,0},{128,64},{192,128},{1,193},{65,1},{129,65},{193,129... | collective-permute-start | bytes 786440 | tf_op jit(solution)/shard_map/ppermute | solution.py:389
  14.7 10.6 %collective-permute-start.2 = (bf16[32,8,512]{2,1,0:T(8,128)(2,1)S(1)}, bf16[32,8,512]{2,1,0:T(8,128)(2,1)S(1)}, u32[]{:S(2)}, u32[]{:S(2)}) collective-permute-start(bf16[32,8,512]{2,1,0:T(8,128)(2,1)S(1)} %add_relay.2.tie_ref), channel_id=1, source_target_pairs={{0,64},{64,128},{128,192},{192,0},{1,65},{65,129},{129,193},{193,1... | collective-permute-start | bytes 786440 | tf_op jit(solution)/shard_map/ppermute | solution.py:386
  19.8 5.5 %collective-permute-start.6 = (bf16[32,8,512]{2,1,0:T(8,128)(2,1)S(1)}, bf16[32,8,512]{2,1,0:T(8,128)(2,1)S(1)}, u32[]{:S(2)}, u32[]{:S(2)}) collective-permute-start(bf16[32,8,512]{2,1,0:T(8,128)(2,1)S(1)} %add_comb.1), channel_id=1, source_target_pairs={{0,1},{1,0},{2,3},{3,2},{4,5},{5,4},{6,7},{7,6},{8,9},{9,8},{10,11... | collective-permute-start | bytes 786440 | tf_op jit(solution)/shard_map/ppermute | solution.py:392
  70.1 7.9 %collective-permute-start.7 = (bf16[32,8,512]{2,1,0:T(8,128)(2,1)S(1)}, bf16[32,8,512]{2,1,0:T(8,128)(2,1)S(1)}, u32[]{:S(2)}, u32[]{:S(2)}) collective-permute-start(bf16[32,8,512]{2,1,0:T(8,128)(2,1)S(1)} %get-tuple-element.48), channel_id=1, source_target_pairs={{0,1},{1,0},{2,3},{3,2},{4,5},{5,4},{6,7},{7,6},{8,9},{9,8},{10,11... | collective-permute-start | bytes 786440 | tf_op jit(solution)/shard_map/ppermute | solution.py:392
  76.9 9.1 %collective-permute-start.10 = (bf16[32,8,512]{2,1,0:T(8,128)(2,1)S(1)}, bf16[32,8,512]{2,1,0:T(8,128)(2,1)S(1)}, u32[]{:S(2)}, u32[]{:S(2)}) collective-permute-start(bf16[32,8,512]{2,1,0:T(8,128)(2,1)S(1)} %get-tuple-element.41.tie_ref.refs_0_), channel_id=1, source_target_pairs={{0,64},{64,128},{128,192},{192,0},{1,65},{65,129},{129,193},{193,1... | collective-permute-start | bytes 786440 | tf_op jit(solution)/shard_map/ppermute | solution.py:386
  78.0 7.9 %collective-permute-start.8 = (bf16[32,8,512]{2,1,0:T(8,128)(2,1)S(1)}, bf16[32,8,512]{2,1,0:T(8,128)(2,1)S(1)}, u32[]{:S(2)}, u32[]{:S(2)}) collective-permute-start(bf16[32,8,512]{2,1,0:T(8,128)(2,1)S(1)} %collective-permute-done.7.refs_1_), channel_id=1, source_target_pairs={{0,192},{64,0},{128,64},{192,128},{1,193},{65,1},{129,65},{193,129... | collective-permute-start | bytes 786440 | tf_op jit(solution)/shard_map/ppermute | solution.py:389
  80.3 11.7 %collective-permute-start.13 = (bf16[32,8,512]{2,1,0:T(8,128)(2,1)S(1)}, bf16[32,8,512]{2,1,0:T(8,128)(2,1)S(1)}, u32[]{:S(2)}, u32[]{:S(2)}) collective-permute-start(bf16[32,8,512]{2,1,0:T(8,128)(2,1)S(1)} %get-tuple-element.41.tie_ref.refs_0_), channel_id=1, source_target_pairs={{0,192},{64,0},{128,64},{192,128},{1,193},{65,1},{129,65},{193,129... | collective-permute-start | bytes 786440 | tf_op jit(solution)/shard_map/ppermute | solution.py:389
  80.7 11.4 %collective-permute-start.12 = (bf16[32,8,512]{2,1,0:T(8,128)(2,1)S(1)}, bf16[32,8,512]{2,1,0:T(8,128)(2,1)S(1)}, u32[]{:S(2)}, u32[]{:S(2)}) collective-permute-start(bf16[32,8,512]{2,1,0:T(8,128)(2,1)S(1)} %collective-permute-done.7.refs_1_), channel_id=1, source_target_pairs={{0,64},{64,128},{128,192},{192,0},{1,65},{65,129},{129,193},{193,1... | collective-permute-start | bytes 786440 | tf_op jit(solution)/shard_map/ppermute | solution.py:386
  85.9 11.2 %collective-permute-start.11 = (bf16[32,8,512]{2,1,0:T(8,128)(2,1)S(1)}, bf16[32,8,512]{2,1,0:T(8,128)(2,1)S(1)}, u32[]{:S(2)}, u32[]{:S(2)}) collective-permute-start(bf16[32,8,512]{2,1,0:T(8,128)(2,1)S(1)} %collective-permute-done.10.refs_2_), channel_id=1, source_target_pairs={{0,64},{64,128},{128,192},{192,0},{1,65},{65,129},{129,193},{193,1... | collective-permute-start | bytes 786440 | tf_op jit(solution)/shard_map/ppermute | solution.py:386
  85.9 12.0 %collective-permute-start.9 = (bf16[32,8,512]{2,1,0:T(8,128)(2,1)S(1)}, bf16[32,8,512]{2,1,0:T(8,128)(2,1)S(1)}, u32[]{:S(2)}, u32[]{:S(2)}) collective-permute-start(bf16[32,8,512]{2,1,0:T(8,128)(2,1)S(1)} %collective-permute-done.8.refs_3_), channel_id=1, source_target_pairs={{0,192},{64,0},{128,64},{192,128},{1,193},{65,1},{129,65},{193,129... | collective-permute-start | bytes 786440 | tf_op jit(solution)/shard_map/ppermute | solution.py:389

commit v5 on v4

--- a/solution.py
+++ b/solution.py
@@ -256,8 +256,7 @@
 
 
 def update_kernel(
-    refresh_ref, grad_ref, left_ref, right_ref, lroot_ref, rroot_ref,
-    new_lroot_ref, new_rroot_ref, update_ref, roots, sems,
+    refresh_ref, grad_ref, left_ref, right_ref, lroot_ref, rroot_ref, update_ref, roots, sems
 ):
     grad = grad_ref[...]
     refreshed = refreshing(refresh_ref)
@@ -266,17 +265,9 @@
     def _():
         new_left = left_ref[...] + gram_rows(grad)
         new_right = right_ref[...] + gram_columns(grad)
-        new_roots = inverse_roots((new_left, new_right))
-        writes = []
-        for i, (root, out_ref) in enumerate(zip(new_roots, (new_lroot_ref, new_rroot_ref))):
-            roots[i] = root
-            write = pltpu.make_async_copy(roots.at[i], out_ref, sems.at[i])
-            write.start()
-            writes.append(write)
-        mixed = bf16_dot(roots[0], grad)
-        update_ref[...] = bf16_dot(mixed, roots[1]).astype(update_ref.dtype)
-        for write in writes:
-            write.wait()
+        new_lroot, new_rroot = inverse_roots((new_left, new_right))
+        mixed = bf16_dot(new_lroot, grad)
+        update_ref[...] = bf16_dot(mixed, new_rroot).astype(update_ref.dtype)
 
     @pl.when(jnp.logical_not(refreshed))
     def _():
@@ -296,15 +287,11 @@
     order = grad.shape[0]
     return pl.pallas_call(
         update_kernel,
-        out_shape=(
-            HBM((order, order), jnp.float32),
-            HBM((order, order), jnp.float32),
-            VMEM((order, order), jnp.bfloat16),
-        ),
+        out_shape=VMEM((order, order), jnp.bfloat16),
         in_specs=[pl.BlockSpec(memory_space=SMEM)]
         + [pl.BlockSpec(memory_space=VMEM)] * 3
         + [pl.BlockSpec(memory_space=HBM)] * 2,
-        out_specs=(pl.BlockSpec(memory_space=HBM),) * 2 + (pl.BlockSpec(memory_space=VMEM),),
+        out_specs=pl.BlockSpec(memory_space=VMEM),
         scratch_shapes=[
             pltpu.VMEM((2, order, order), jnp.float32),
             pltpu.SemaphoreType.DMA((2,)),
@@ -315,65 +302,53 @@
 
 
 def factors_kernel(
-    tie_ref, refresh_ref, grad_ref, left_ref, right_ref, lroot_ref, rroot_ref, old_l_ref, old_r_ref,
-    new_left_ref, new_right_ref, new_lroot_ref, new_rroot_ref,
-    left, right, roots, sems,
+    tie_ref, refresh_ref, grad_ref, left_ref, right_ref, lroot_ref, rroot_ref,
+    new_left_ref, new_right_ref, new_lroot_ref, new_rroot_ref, factors, roots, sems,
 ):
-    del tie_ref, old_l_ref, old_r_ref
-    kept = jnp.logical_not(refreshing(refresh_ref))
+    del tie_ref
+    refreshed = refreshing(refresh_ref)
     loads = [
         pltpu.make_async_copy(source, roots.at[i], sems.at[2 + i])
         for i, source in enumerate((lroot_ref, rroot_ref))
     ]
-    keeps = [
-        pltpu.make_async_copy(roots.at[i], target, sems.at[2 + i])
-        for i, target in enumerate((new_lroot_ref, new_rroot_ref))
-    ]
-
-    @pl.when(kept)
+    targets = (new_left_ref, new_right_ref)
+    writes = [pltpu.make_async_copy(factors.at[i], t, sems.at[i]) for i, t in enumerate(targets)]
+    targets = (new_lroot_ref, new_rroot_ref)
+    writes += [pltpu.make_async_copy(roots.at[i], t, sems.at[2 + i]) for i, t in enumerate(targets)]
+    for load in loads:
+        load.start()
+    grad = grad_ref[...]
+    factors[0] = left_ref[...] + gram_rows(grad)
+    writes[0].start()
+    factors[1] = right_ref[...] + gram_columns(grad)
+    writes[1].start()
+    for load in loads:
+        load.wait()
+
+    @pl.when(refreshed)
     def _():
-        for load in loads:
-            load.start()
-
-    grad = grad_ref[...]
-    left[...] = left_ref[...] + gram_rows(grad)
-    write_left = pltpu.make_async_copy(left, new_left_ref, sems.at[0])
-    write_left.start()
-    right[...] = right_ref[...] + gram_columns(grad)
-    write_right = pltpu.make_async_copy(right, new_right_ref, sems.at[1])
-    write_right.start()
-
-    @pl.when(kept)
-    def _():
-        for load, keep in zip(loads, keeps, strict=True):
-            load.wait()
-            keep.start()
-        for keep in keeps:
-            keep.wait()
-
-    write_left.wait()
-    write_right.wait()
-
-
-def owner_factors(tie, refresh, grad, left, right, lroot, rroot, new_lroot, new_rroot):
+        roots[0], roots[1] = inverse_roots((factors[0], factors[1]))
+
+    for write in writes[2:]:
+        write.start()
+    for write in writes:
+        write.wait()
+
+
+def owner_factors(tie, refresh, grad, left, right, lroot, rroot):
     order = grad.shape[0]
     return pl.pallas_call(
         factors_kernel,
         out_shape=(HBM((order, order), jnp.float32),) * 4,
         in_specs=[pl.BlockSpec(memory_space=pl.ANY), pl.BlockSpec(memory_space=SMEM)]
         + [pl.BlockSpec(memory_space=VMEM)] * 3
-        + [pl.BlockSpec(memory_space=HBM)] * 4,
+        + [pl.BlockSpec(memory_space=HBM)] * 2,
         out_specs=(pl.BlockSpec(memory_space=HBM),) * 4,
-        scratch_shapes=[pltpu.VMEM((order, order), jnp.float32)] * 2
-        + [pltpu.VMEM((2, order, order), jnp.float32), pltpu.SemaphoreType.DMA((4,))],
-        input_output_aliases={7: 2, 8: 3},
-        compiler_params=pltpu.CompilerParams(vmem_limit_bytes=16 * 2**20),
+        scratch_shapes=[pltpu.VMEM((2, order, order), jnp.float32)] * 2
+        + [pltpu.SemaphoreType.DMA((4,))],
+        compiler_params=pltpu.CompilerParams(vmem_limit_bytes=24 * 2**20),
         name="owner_factors",
-    )(
-        tie,
-        refresh,
-        grad, left, right, lroot, rroot, new_lroot, new_rroot,
-    )
+    )(tie, refresh, grad, left, right, lroot, rroot)
 
 
 def per_device(grads, left_factor, right_factor, left_root, right_root, block_of_slot, refresh):
@@ -415,7 +390,7 @@
     other = to_core(add_pieces(partial_b, comb_b, comb_b.dtype, "add_comb"))
     grad = over_chips(join_cores(partial_a, comb_a, other)).reshape(order, order)
 
-    new_lroot, new_rroot, update = owner_update(refresh, grad, left, right, lroot, rroot)
+    update = owner_update(refresh, grad, left, right, lroot, rroot)
 
     rows = over_chips(update.reshape(chips, 2, piece_rows, order))
     rows_a, other = split_cores(rows)
@@ -425,7 +400,7 @@
     prev_b, next_a = to_next(rows_b), to_prev(rows_a)
     over_a, over_b = to_next(prev_a), to_prev(next_b)
     new_left, new_right, new_lroot, new_rroot = owner_factors(
-        rows_a, refresh, grad, left, right, lroot, rroot, new_lroot, new_rroot
+        rows_a, refresh, grad, left, right, lroot, rroot
     )
     over_a, over_b = to_next(prev_a), to_prev(next_b)
     updates = place_blocks(

time: 99.2 us -> 99.8 us (level)
  starting transfers between devices: 25.9 us -> 23.5 us
  blocking collectives: 42.6 us -> 44.5 us
  Pallas kernels: 12 us -> 13.1 us
    all_to_all x2, blocking collectives: 42.6 us -> 44.5 us  [over_chips(): lax.all_to_all(rows, 'fsdp', split_axis=0, concat_axis=0, axis_index_grou...]
    ppermute x2, starting transfers between devices: 10.2 us -> 8.67 us  [to_core(): return lax.ppermute(piece, 'fsdp', [(i, i ^ 1) for i in range(shard_count)])]
    pallas_call x1, Pallas kernels: 2.96 us -> 4.1 us  [owner_factors(): pl.pallas_call(factors_kernel, out_shape=(HBM((order, order), jnp.float32...]
  transfers between devices with their start and end apart: 14 -> 14, of which waited for: 7 -> 7; matrix products, arithmetic and copies ran while one was open for 0% -> 0% of each run, Pallas kernels for 7% -> 9%
where the time goes in v5:
time: 99.8 us; the launch traced here: 99.2 us
  blocking collectives  44.5 us (45%)
  starting transfers between devices  23.5 us (24%)
  waiting for transfers between devices  16.6 us (17%)
  Pallas kernels  13.1 us (13%)
  between operations  1.57 us (2%)
    all_to_all x2, blocking collectives, over_chips(): lax.all_to_all(rows, 'fsdp', split_axis=0, concat_axis=0, axis_index_grou...  44.5 us
    ppermute x6, starting transfers between devices, to_prev(): return lax.ppermute(piece, 'dp', [(i, (i - 1) % N_DP) for i in range(N_DP)])  12.1 us
    ppermute x6, waiting for transfers between devices, to_next(): return lax.ppermute(piece, 'dp', [(i, (i + 1) % N_DP) for i in range(N_DP)])  10.6 us
    ppermute x2, starting transfers between devices, to_core(): return lax.ppermute(piece, 'fsdp', [(i, i ^ 1) for i in range(shard_count)])  8.67 us
    ppermute x6, waiting for transfers between devices, to_prev(): return lax.ppermute(piece, 'dp', [(i, (i - 1) % N_DP) for i in range(N_DP)])  4.77 us
    pallas_call x1, Pallas kernels, owner_factors(): pl.pallas_call(factors_kernel, out_shape=(HBM((order, order), jnp.float32...  4.1 us
    pallas_call x3, Pallas kernels, place_blocks(): pl.pallas_call(functools.partial(place_kernel, pieces, aliased), out_shap...  2.84 us
    ppermute x6, starting transfers between devices, to_next(): return lax.ppermute(piece, 'dp', [(i, (i + 1) % N_DP) for i in range(N_DP)])  2.71 us
  transfers between devices with their start and end apart: 14, of which 7 were waited for; matrix products, arithmetic and copies ran while one was open for 0% of the time, Pallas kernels for 9%

profile of v5, /device:TPU:1, one launch (start us, length us, event | category | flops | bytes accessed | tf_op | source)
XLA Modules:
  0.0 99.2 jit_solution(8249914676253892237)
XLA Ops:
  0.6 1.7 %order_first.1 = (bf16[256,8,512]{2,1,0:T(8,128)(2,1)S(1)}, s32[256]{0:T(256)S(4)}, bf16[32,8,512]{2,1,0:T(8,128)(2,1)S(1)}, bf16[32,8,512]{2,1,0:T(8,128)(2,1)S(1)}) custom-call(s32[256]{0:T(256)} %index_ref.1, bf16[256,8,512]{2,1,0:T(8,128)(2,1)} %bitcast.18), custom_call_target="tpu_custom_call" | custom-call | tf_op jit(solution)/shard_map/order_first/pallas_call | solution.py:76
  2.3 3.6 %collective-permute-start.4 = (bf16[32,8,512]{2,1,0:T(8,128)(2,1)S(1)}, bf16[32,8,512]{2,1,0:T(8,128)(2,1)S(1)}, u32[]{:S(2)}, u32[]{:S(2)}) collective-permute-start(bf16[32,8,512]{2,1,0:T(8,128)(2,1)S(1)} %get-tuple-element.35), channel_id=1, source_target_pairs={{0,192},{64,0},{128,64},{192,128},{1,193},{65,1},{129,65},{193,129... | collective-permute-start | bytes 786440 | tf_op jit(solution)/shard_map/ppermute | solution.py:364
  6.0 0.0 collective-permute-start.1
  6.6 0.4 order_rest.1
  7.0 0.1 collective-permute-start.3
  7.1 3.8 %collective-permute-done.4.refs_1_ = bf16[32,8,512]{2,1,0:T(8,128)(2,1)S(1)} collective-permute-done((bf16[32,8,512]{2,1,0:T(8,128)(2,1)S(1)}, bf16[32,8,512]{2,1,0:T(8,128)(2,1)S(1)}, u32[]{:S(2)}, u32[]{:S(2)}) %collective-permute-start.4) | collective-permute-done | bytes 262176 | tf_op jit(solution)/shard_map/ppermute | solution.py:364
  10.9 0.1 add_relay.3
  11.0 3.5 %collective-permute-start.5 = (bf16[32,8,512]{2,1,0:T(8,128)(2,1)S(1)}, bf16[32,8,512]{2,1,0:T(8,128)(2,1)S(1)}, u32[]{:S(2)}, u32[]{:S(2)}) collective-permute-start(bf16[32,8,512]{2,1,0:T(8,128)(2,1)S(1)} %add_relay.3), channel_id=1, source_target_pairs={{0,192},{64,0},{128,64},{192,128},{1,193},{65,1},{129,65},{193,129... | collective-permute-start | bytes 786440 | tf_op jit(solution)/shard_map/ppermute | solution.py:364
  14.5 0.1 collective-permute-start
  14.6 0.0 collective-permute-done.1.refs_1_
  14.6 0.1 add_relay.2.tie_ref
  14.7 1.5 %collective-permute-start.2 = (bf16[32,8,512]{2,1,0:T(8,128)(2,1)S(1)}, bf16[32,8,512]{2,1,0:T(8,128)(2,1)S(1)}, u32[]{:S(2)}, u32[]{:S(2)}) collective-permute-start(bf16[32,8,512]{2,1,0:T(8,128)(2,1)S(1)} %add_relay.2.tie_ref), channel_id=1, source_target_pairs={{0,64},{64,128},{128,192},{192,0},{1,65},{65,129},{129,193},{193,1... | collective-permute-start | bytes 786440 | tf_op jit(solution)/shard_map/ppermute | solution.py:361
  16.1 1.6 %load_matrices.1 = (f32[512,512]{1,0:T(8,128)S(1)}, f32[512,512]{1,0:T(8,128)S(1)}) custom-call(bf16[32,8,512]{2,1,0:T(8,128)(2,1)S(1)} %add_relay.2.tie_ref, f32[512,512]{1,0:T(8,128)} %bitcast.19, f32[512,512]{1,0:T(8,128)} %bitcast.20), custom_call_target="tpu_custom_call" | custom-call | tf_op jit(solution)/shard_map/load_matrices/pallas_call | solution.py:239
  17.7 2.0 %collective-permute-done.3.refs_1_ = bf16[32,8,512]{2,1,0:T(8,128)(2,1)S(1)} collective-permute-done((bf16[32,8,512]{2,1,0:T(8,128)(2,1)S(1)}, bf16[32,8,512]{2,1,0:T(8,128)(2,1)S(1)}, u32[]{:S(2)}, u32[]{:S(2)}) %collective-permute-start.3) | collective-permute-done | bytes 262176 | tf_op jit(solution)/shard_map/ppermute | solution.py:361
  19.7 0.1 add_raw.3.refs_0_
  19.7 0.0 collective-permute-done.5.refs_1_
  19.8 3.4 %collective-permute-start.6 = (bf16[32,8,512]{2,1,0:T(8,128)(2,1)S(1)}, bf16[32,8,512]{2,1,0:T(8,128)(2,1)S(1)}, u32[]{:S(2)}, u32[]{:S(2)}) collective-permute-start(bf16[32,8,512]{2,1,0:T(8,128)(2,1)S(1)} %add_comb.1), channel_id=1, source_target_pairs={{0,1},{1,0},{2,3},{3,2},{4,5},{5,4},{6,7},{7,6},{8,9},{9,8},{10,11... | collective-permute-start | bytes 786440 | tf_op jit(solution)/shard_map/ppermute | solution.py:367
  23.2 0.9 collective-permute-done.refs_1_
  24.2 0.1 add_raw.2.partial_ref
  24.2 1.0 %collective-permute-done.2.comb_ref = bf16[32,8,512]{2,1,0:T(8,128)(2,1)S(1)} collective-permute-done((bf16[32,8,512]{2,1,0:T(8,128)(2,1)S(1)}, bf16[32,8,512]{2,1,0:T(8,128)(2,1)S(1)}, u32[]{:S(2)}, u32[]{:S(2)}) %collective-permute-start.2) | collective-permute-done | bytes 262176 | tf_op jit(solution)/shard_map/ppermute | solution.py:361
  25.3 0.0 collective-permute-done.6.other_ref
  25.3 0.1 join_cores.1
  25.3 23.8 %all_to_all.10 = bf16[32,2,8,512]{3,2,1,0:T(8,128)(2,1)S(1)} all-to-all(bf16[32,2,8,512]{3,2,1,0:T(8,128)(2,1)S(1)} %join_cores.1), channel_id=1, replica_groups={{0,2,4,6,8,10,12,14,16,18,20,22,24,26,28,30,32,34,36,38,40,42,44,46,48,..., dimensions={0} | all-to-all | bytes 1048576 | tf_op jit(solution)/shard_map/all_to_all | solution.py:371
  49.1 2.2 %owner_update.1 = bf16[512,512]{1,0:T(8,128)(2,1)S(1)} custom-call(s32[1]{0:T(128)S(4)} %get-tuple-element.26.refresh_ref, bf16[512,512]{1,0:T(8,128)(2,1)S(1)} %bitcast.11, f32[512,512]{1,0:T(8,128)S(1)} %get-tuple-element.33.refs_2_.left_ref, f32[512,512]{1,0:T(8,128)S(1)} %get-tuple-element.36.right_ref, f32[512,512]{1,0:T(8,128)} %bitcast.14, ...), custom_call_target="tpu_custom_call" | custom-call | tf_op jit(solution)/shard_map/owner_update/pallas_call | solution.py:288
  51.3 20.7 %all_to_all.11.rows_ref = bf16[32,2,8,512]{3,2,1,0:T(8,128)(2,1)S(1)} all-to-all(bf16[32,2,8,512]{3,2,1,0:T(8,128)(2,1)S(1)} %bitcast.13), channel_id=1, replica_groups={{0,2,4,6,8,10,12,14,16,18,20,22,24,26,28,30,32,34,36,38,40,42,44,46,48,..., dimensions={0} | all-to-all | bytes 1048576 | tf_op jit(solution)/shard_map/all_to_all | solution.py:371
  72.0 5.2 %collective-permute-start.7 = (bf16[32,8,512]{2,1,0:T(8,128)(2,1)S(1)}, bf16[32,8,512]{2,1,0:T(8,128)(2,1)S(1)}, u32[]{:S(2)}, u32[]{:S(2)}) collective-permute-start(bf16[32,8,512]{2,1,0:T(8,128)(2,1)S(1)} %get-tuple-element.42), channel_id=1, source_target_pairs={{0,1},{1,0},{2,3},{3,2},{4,5},{5,4},{6,7},{7,6},{8,9},{9,8},{10,11... | collective-permute-start | bytes 786440 | tf_op jit(solution)/shard_map/ppermute | solution.py:367
  77.3 0.0 collective-permute-start.10
  77.3 1.2 %collective-permute-done.7.refs_1_ = bf16[32,8,512]{2,1,0:T(8,128)(2,1)S(1)} collective-permute-done((bf16[32,8,512]{2,1,0:T(8,128)(2,1)S(1)}, bf16[32,8,512]{2,1,0:T(8,128)(2,1)S(1)}, u32[]{:S(2)}, u32[]{:S(2)}) %collective-permute-start.7) | collective-permute-done | bytes 262176 | tf_op jit(solution)/shard_map/ppermute | solution.py:367
  78.4 1.9 %collective-permute-start.8 = (bf16[32,8,512]{2,1,0:T(8,128)(2,1)S(1)}, bf16[32,8,512]{2,1,0:T(8,128)(2,1)S(1)}, u32[]{:S(2)}, u32[]{:S(2)}) collective-permute-start(bf16[32,8,512]{2,1,0:T(8,128)(2,1)S(1)} %collective-permute-done.7.refs_1_), channel_id=1, source_target_pairs={{0,192},{64,0},{128,64},{192,128},{1,193},{65,1},{129,65},{193,129... | collective-permute-start | bytes 786440 | tf_op jit(solution)/shard_map/ppermute | solution.py:364
  80.3 0.3 collective-permute-start.13
  80.6 1.1 %collective-permute-start.12 = (bf16[32,8,512]{2,1,0:T(8,128)(2,1)S(1)}, bf16[32,8,512]{2,1,0:T(8,128)(2,1)S(1)}, u32[]{:S(2)}, u32[]{:S(2)}) collective-permute-start(bf16[32,8,512]{2,1,0:T(8,128)(2,1)S(1)} %collective-permute-done.7.refs_1_), channel_id=1, source_target_pairs={{0,64},{64,128},{128,192},{192,0},{1,65},{65,129},{129,193},{193,1... | collective-permute-start | bytes 786440 | tf_op jit(solution)/shard_map/ppermute | solution.py:361
  81.8 4.6 %collective-permute-done.10.refs_2_ = bf16[32,8,512]{2,1,0:T(8,128)(2,1)S(1)} collective-permute-done((bf16[32,8,512]{2,1,0:T(8,128)(2,1)S(1)}, bf16[32,8,512]{2,1,0:T(8,128)(2,1)S(1)}, u32[]{:S(2)}, u32[]{:S(2)}) %collective-permute-start.10) | collective-permute-done | bytes 262176 | tf_op jit(solution)/shard_map/ppermute | solution.py:361
  86.3 0.0 collective-permute-start.11
  86.3 0.0 collective-permute-done.8.refs_3_
  86.3 2.7 %collective-permute-start.9 = (bf16[32,8,512]{2,1,0:T(8,128)(2,1)S(1)}, bf16[32,8,512]{2,1,0:T(8,128)(2,1)S(1)}, u32[]{:S(2)}, u32[]{:S(2)}) collective-permute-start(bf16[32,8,512]{2,1,0:T(8,128)(2,1)S(1)} %collective-permute-done.8.refs_3_), channel_id=1, source_target_pairs={{0,192},{64,0},{128,64},{192,128},{1,193},{65,1},{129,65},{193,129... | collective-permute-start | bytes 786440 | tf_op jit(solution)/shard_map/ppermute | solution.py:364
  89.0 4.1 %owner_factors.1 = (f32[512,512]{1,0:T(8,128)}, f32[512,512]{1,0:T(8,128)}, f32[512,512]{1,0:T(8,128)}, f32[512,512]{1,0:T(8,128)}) custom-call(bf16[32,8,512]{2,1,0:T(8,128)(2,1)S(1)} %get-tuple-element.37.tie_ref.refs_0_, s32[1]{0:T(128)S(4)} %get-tuple-element.26.refresh_ref, bf16[512,512]{1,0:T(8,128)(2,1)S(1)} %bitcast.12, ...), custom_call_target="tpu_custom_call" | custom-call | tf_op jit(solution)/shard_map/owner_factors/pallas_call | solution.py:340
  93.1 0.0 collective-permute-done.13.refs_5_
  93.2 0.0 collective-permute-done.12.refs_4_
  93.2 1.4 %place_early.1.refs_1_ = bf16[256,8,512]{2,1,0:T(8,128)(2,1)} custom-call(s32[256]{0:T(256)S(4)} %get-tuple-element.24.index_ref, bf16[32,8,512]{2,1,0:T(8,128)(2,1)S(1)} %get-tuple-element.37.tie_ref.refs_0_, bf16[32,8,512]{2,1,0:T(8,128)(2,1)S(1)} %collective-permute-done.7.refs_1_, bf16[32,8,512]{2,1,0:T(8,128)(2,1)S(1)} %collective-permute-done.10.refs_2_, ...), custom_call_target="tpu_custom_call" | custom-call | bytes 100663296 | tf_op jit(solution)/shard_map/place_early/pallas_call | solution.py:126
  94.5 3.0 %collective-permute-done.11.refs_0_ = bf16[32,8,512]{2,1,0:T(8,128)(2,1)S(1)} collective-permute-done((bf16[32,8,512]{2,1,0:T(8,128)(2,1)S(1)}, bf16[32,8,512]{2,1,0:T(8,128)(2,1)S(1)}, u32[]{:S(2)}, u32[]{:S(2)}) %collective-permute-start.11) | collective-permute-done | bytes 262176 | tf_op jit(solution)/shard_map/ppermute | solution.py:361
  97.6 0.7 place_over.1.refs_1_
  98.3 0.0 collective-permute-done.9.refs_0_
  98.3 0.7 place_last.1
  (2 shorter events, 0.1 us)
Async XLA Ops:
  2.3 8.6 %collective-permute-start.4 = (bf16[32,8,512]{2,1,0:T(8,128)(2,1)S(1)}, bf16[32,8,512]{2,1,0:T(8,128)(2,1)S(1)}, u32[]{:S(2)}, u32[]{:S(2)}) collective-permute-start(bf16[32,8,512]{2,1,0:T(8,128)(2,1)S(1)} %get-tuple-element.35), channel_id=1, source_target_pairs={{0,192},{64,0},{128,64},{192,128},{1,193},{65,1},{129,65},{193,129... | collective-permute-start | bytes 786440 | tf_op jit(solution)/shard_map/ppermute | solution.py:364
  6.0 8.6 %collective-permute-start.1 = (bf16[32,8,512]{2,1,0:T(8,128)(2,1)S(1)}, bf16[32,8,512]{2,1,0:T(8,128)(2,1)S(1)}, u32[]{:S(2)}, u32[]{:S(2)}) collective-permute-start(bf16[32,8,512]{2,1,0:T(8,128)(2,1)S(1)} %get-tuple-element.30), channel_id=1, source_target_pairs={{0,64},{64,128},{128,192},{192,0},{1,65},{65,129},{129,193},{193,1... | collective-permute-start | bytes 786440 | tf_op jit(solution)/shard_map/ppermute | solution.py:361
  7.0 12.6 %collective-permute-start.3 = (bf16[32,8,512]{2,1,0:T(8,128)(2,1)S(1)}, bf16[32,8,512]{2,1,0:T(8,128)(2,1)S(1)}, u32[]{:S(2)}, u32[]{:S(2)}) collective-permute-start(bf16[32,8,512]{2,1,0:T(8,128)(2,1)S(1)} %get-tuple-element.32), channel_id=1, source_target_pairs={{0,64},{64,128},{128,192},{192,0},{1,65},{65,129},{129,193},{193,1... | collective-permute-start | bytes 786440 | tf_op jit(solution)/shard_map/ppermute | solution.py:361
  11.0 8.7 %collective-permute-start.5 = (bf16[32,8,512]{2,1,0:T(8,128)(2,1)S(1)}, bf16[32,8,512]{2,1,0:T(8,128)(2,1)S(1)}, u32[]{:S(2)}, u32[]{:S(2)}) collective-permute-start(bf16[32,8,512]{2,1,0:T(8,128)(2,1)S(1)} %add_relay.3), channel_id=1, source_target_pairs={{0,192},{64,0},{128,64},{192,128},{1,193},{65,1},{129,65},{193,129... | collective-permute-start | bytes 786440 | tf_op jit(solution)/shard_map/ppermute | solution.py:364
  14.5 9.7 %collective-permute-start = (bf16[32,8,512]{2,1,0:T(8,128)(2,1)S(1)}, bf16[32,8,512]{2,1,0:T(8,128)(2,1)S(1)}, u32[]{:S(2)}, u32[]{:S(2)}) collective-permute-start(bf16[32,8,512]{2,1,0:T(8,128)(2,1)S(1)} %get-tuple-element.28), channel_id=1, source_target_pairs={{0,192},{64,0},{128,64},{192,128},{1,193},{65,1},{129,65},{193,129... | collective-permute-start | bytes 786440 | tf_op jit(solution)/shard_map/ppermute | solution.py:364
  14.7 10.6 %collective-permute-start.2 = (bf16[32,8,512]{2,1,0:T(8,128)(2,1)S(1)}, bf16[32,8,512]{2,1,0:T(8,128)(2,1)S(1)}, u32[]{:S(2)}, u32[]{:S(2)}) collective-permute-start(bf16[32,8,512]{2,1,0:T(8,128)(2,1)S(1)} %add_relay.2.tie_ref), channel_id=1, source_target_pairs={{0,64},{64,128},{128,192},{192,0},{1,65},{65,129},{129,193},{193,1... | collective-permute-start | bytes 786440 | tf_op jit(solution)/shard_map/ppermute | solution.py:361
  19.8 5.5 %collective-permute-start.6 = (bf16[32,8,512]{2,1,0:T(8,128)(2,1)S(1)}, bf16[32,8,512]{2,1,0:T(8,128)(2,1)S(1)}, u32[]{:S(2)}, u32[]{:S(2)}) collective-permute-start(bf16[32,8,512]{2,1,0:T(8,128)(2,1)S(1)} %add_comb.1), channel_id=1, source_target_pairs={{0,1},{1,0},{2,3},{3,2},{4,5},{5,4},{6,7},{7,6},{8,9},{9,8},{10,11... | collective-permute-start | bytes 786440 | tf_op jit(solution)/shard_map/ppermute | solution.py:367
  72.0 6.4 %collective-permute-start.7 = (bf16[32,8,512]{2,1,0:T(8,128)(2,1)S(1)}, bf16[32,8,512]{2,1,0:T(8,128)(2,1)S(1)}, u32[]{:S(2)}, u32[]{:S(2)}) collective-permute-start(bf16[32,8,512]{2,1,0:T(8,128)(2,1)S(1)} %get-tuple-element.42), channel_id=1, source_target_pairs={{0,1},{1,0},{2,3},{3,2},{4,5},{5,4},{6,7},{7,6},{8,9},{9,8},{10,11... | collective-permute-start | bytes 786440 | tf_op jit(solution)/shard_map/ppermute | solution.py:367
  77.3 9.1 %collective-permute-start.10 = (bf16[32,8,512]{2,1,0:T(8,128)(2,1)S(1)}, bf16[32,8,512]{2,1,0:T(8,128)(2,1)S(1)}, u32[]{:S(2)}, u32[]{:S(2)}) collective-permute-start(bf16[32,8,512]{2,1,0:T(8,128)(2,1)S(1)} %get-tuple-element.37.tie_ref.refs_0_), channel_id=1, source_target_pairs={{0,64},{64,128},{128,192},{192,0},{1,65},{65,129},{129,193},{193,1... | collective-permute-start | bytes 786440 | tf_op jit(solution)/shard_map/ppermute | solution.py:361
  78.4 7.9 %collective-permute-start.8 = (bf16[32,8,512]{2,1,0:T(8,128)(2,1)S(1)}, bf16[32,8,512]{2,1,0:T(8,128)(2,1)S(1)}, u32[]{:S(2)}, u32[]{:S(2)}) collective-permute-start(bf16[32,8,512]{2,1,0:T(8,128)(2,1)S(1)} %collective-permute-done.7.refs_1_), channel_id=1, source_target_pairs={{0,192},{64,0},{128,64},{192,128},{1,193},{65,1},{129,65},{193,129... | collective-permute-start | bytes 786440 | tf_op jit(solution)/shard_map/ppermute | solution.py:364
  80.3 12.8 %collective-permute-start.13 = (bf16[32,8,512]{2,1,0:T(8,128)(2,1)S(1)}, bf16[32,8,512]{2,1,0:T(8,128)(2,1)S(1)}, u32[]{:S(2)}, u32[]{:S(2)}) collective-permute-start(bf16[32,8,512]{2,1,0:T(8,128)(2,1)S(1)} %get-tuple-element.37.tie_ref.refs_0_), channel_id=1, source_target_pairs={{0,192},{64,0},{128,64},{192,128},{1,193},{65,1},{129,65},{193,129... | collective-permute-start | bytes 786440 | tf_op jit(solution)/shard_map/ppermute | solution.py:364
  80.6 12.5 %collective-permute-start.12 = (bf16[32,8,512]{2,1,0:T(8,128)(2,1)S(1)}, bf16[32,8,512]{2,1,0:T(8,128)(2,1)S(1)}, u32[]{:S(2)}, u32[]{:S(2)}) collective-permute-start(bf16[32,8,512]{2,1,0:T(8,128)(2,1)S(1)} %collective-permute-done.7.refs_1_), channel_id=1, source_target_pairs={{0,64},{64,128},{128,192},{192,0},{1,65},{65,129},{129,193},{193,1... | collective-permute-start | bytes 786440 | tf_op jit(solution)/shard_map/ppermute | solution.py:361
  86.3 11.2 %collective-permute-start.11 = (bf16[32,8,512]{2,1,0:T(8,128)(2,1)S(1)}, bf16[32,8,512]{2,1,0:T(8,128)(2,1)S(1)}, u32[]{:S(2)}, u32[]{:S(2)}) collective-permute-start(bf16[32,8,512]{2,1,0:T(8,128)(2,1)S(1)} %collective-permute-done.10.refs_2_), channel_id=1, source_target_pairs={{0,64},{64,128},{128,192},{192,0},{1,65},{65,129},{129,193},{193,1... | collective-permute-start | bytes 786440 | tf_op jit(solution)/shard_map/ppermute | solution.py:361
  86.3 12.0 %collective-permute-start.9 = (bf16[32,8,512]{2,1,0:T(8,128)(2,1)S(1)}, bf16[32,8,512]{2,1,0:T(8,128)(2,1)S(1)}, u32[]{:S(2)}, u32[]{:S(2)}) collective-permute-start(bf16[32,8,512]{2,1,0:T(8,128)(2,1)S(1)} %collective-permute-done.8.refs_3_), channel_id=1, source_target_pairs={{0,192},{64,0},{128,64},{192,128},{1,193},{65,1},{129,65},{193,129... | collective-permute-start | bytes 786440 | tf_op jit(solution)/shard_map/ppermute | solution.py:364

commit v6 on v5

--- a/solution.py
+++ b/solution.py
@@ -176,22 +176,21 @@
     )(partial, comb, other)
 
 
-def split_kernel(rows_ref, mine_ref, other_ref):
-    me = core_index()
-    mine_ref[...] = rows_ref[:, me]
-    other_ref[...] = rows_ref[:, 1 - me]
-
-
-def split_cores(rows):
+def pick_kernel(core, rows_ref, tie_ref, out_ref):
+    del tie_ref
+    out_ref[...] = rows_ref[:, lax.rem(core_index() + core, 2)]
+
+
+def pick_core(rows, core, tie):
     slots, _, count, columns = rows.shape
     return pl.pallas_call(
-        split_kernel,
-        out_shape=[VMEM((slots, count, columns), rows.dtype)] * 2,
-        in_specs=[pl.BlockSpec(memory_space=VMEM)],
-        out_specs=[pl.BlockSpec(memory_space=VMEM)] * 2,
+        functools.partial(pick_kernel, core),
+        out_shape=VMEM((slots, count, columns), rows.dtype),
+        in_specs=[pl.BlockSpec(memory_space=VMEM), pl.BlockSpec(memory_space=pl.ANY)],
+        out_specs=pl.BlockSpec(memory_space=VMEM),
         compiler_params=pltpu.CompilerParams(vmem_limit_bytes=6 * 2**20),
-        name="split_cores",
-    )(rows)
+        name="pick_core",
+    )(rows, tie)
 
 
 def inverse_roots(factors):
@@ -393,7 +392,8 @@
     update = owner_update(refresh, grad, left, right, lroot, rroot)
 
     rows = over_chips(update.reshape(chips, 2, piece_rows, order))
-    rows_a, other = split_cores(rows)
+    rows_a = pick_core(rows, 0, update)
+    other = pick_core(rows, 1, rows_a)
     prev_a = to_next(rows_a)
     rows_b = to_core(other)
     next_b = to_prev(rows_b)

time: 99.8 us -> 99.2 us (level)
  starting transfers between devices: 23.5 us -> 25.9 us
  blocking collectives: 44.5 us -> 42.6 us
  waiting for transfers between devices: 16.6 us -> 15.6 us
    all_to_all x2, blocking collectives: 44.5 us -> 42.6 us  [over_chips(): lax.all_to_all(rows, 'fsdp', split_axis=0, concat_axis=0, axis_index_grou...]
    ppermute x2, starting transfers between devices: 8.67 us -> 10.2 us  [to_core(): return lax.ppermute(piece, 'fsdp', [(i, i ^ 1) for i in range(shard_count)])]
where the time goes in v6:
time: 99.2 us; the launch traced here: 98.8 us
  blocking collectives  42.6 us (43%)
  starting transfers between devices  25.9 us (26%)
  waiting for transfers between devices  15.6 us (16%)
  Pallas kernels  13.1 us (13%)
  between operations  1.58 us (2%)
    all_to_all x2, blocking collectives, over_chips(): lax.all_to_all(rows, 'fsdp', split_axis=0, concat_axis=0, axis_index_grou...  42.6 us
    ppermute x6, starting transfers between devices, to_prev(): return lax.ppermute(piece, 'dp', [(i, (i - 1) % N_DP) for i in range(N_DP)])  13 us
    ppermute x2, starting transfers between devices, to_core(): return lax.ppermute(piece, 'fsdp', [(i, i ^ 1) for i in range(shard_count)])  10.2 us
    ppermute x6, waiting for transfers between devices, to_next(): return lax.ppermute(piece, 'dp', [(i, (i + 1) % N_DP) for i in range(N_DP)])  9.72 us
    ppermute x6, waiting for transfers between devices, to_prev(): return lax.ppermute(piece, 'dp', [(i, (i - 1) % N_DP) for i in range(N_DP)])  4.77 us
    pallas_call x1, Pallas kernels, owner_factors(): pl.pallas_call(factors_kernel, out_shape=(HBM((order, order), jnp.float32...  4.11 us
    pallas_call x3, Pallas kernels, place_blocks(): pl.pallas_call(functools.partial(place_kernel, pieces, aliased), out_shap...  2.84 us
    ppermute x6, starting transfers between devices, to_next(): return lax.ppermute(piece, 'dp', [(i, (i + 1) % N_DP) for i in range(N_DP)])  2.71 us
  transfers between devices with their start and end apart: 14, of which 7 were waited for; matrix products, arithmetic and copies ran while one was open for 0% of the time, Pallas kernels for 9%

profile of v6, /device:TPU:1, one launch (start us, length us, event | category | flops | bytes accessed | tf_op | source)
XLA Modules:
  0.0 98.8 jit_solution(5626931783714446542)
XLA Ops:
  0.6 1.7 %order_first.1 = (bf16[256,8,512]{2,1,0:T(8,128)(2,1)S(1)}, s32[256]{0:T(256)S(4)}, bf16[32,8,512]{2,1,0:T(8,128)(2,1)S(1)}, bf16[32,8,512]{2,1,0:T(8,128)(2,1)S(1)}) custom-call(s32[256]{0:T(256)} %index_ref.1, bf16[256,8,512]{2,1,0:T(8,128)(2,1)} %bitcast.18), custom_call_target="tpu_custom_call" | custom-call | tf_op jit(solution)/shard_map/order_first/pallas_call | solution.py:76
  2.3 3.6 %collective-permute-start.4 = (bf16[32,8,512]{2,1,0:T(8,128)(2,1)S(1)}, bf16[32,8,512]{2,1,0:T(8,128)(2,1)S(1)}, u32[]{:S(2)}, u32[]{:S(2)}) collective-permute-start(bf16[32,8,512]{2,1,0:T(8,128)(2,1)S(1)} %get-tuple-element.33), channel_id=1, source_target_pairs={{0,192},{64,0},{128,64},{192,128},{1,193},{65,1},{129,65},{193,129... | collective-permute-start | bytes 786440 | tf_op jit(solution)/shard_map/ppermute | solution.py:363
  6.0 0.0 collective-permute-start.1
  6.6 0.4 order_rest.1
  7.0 0.1 collective-permute-start.3
  7.1 3.8 %collective-permute-done.4.refs_1_ = bf16[32,8,512]{2,1,0:T(8,128)(2,1)S(1)} collective-permute-done((bf16[32,8,512]{2,1,0:T(8,128)(2,1)S(1)}, bf16[32,8,512]{2,1,0:T(8,128)(2,1)S(1)}, u32[]{:S(2)}, u32[]{:S(2)}) %collective-permute-start.4) | collective-permute-done | bytes 262176 | tf_op jit(solution)/shard_map/ppermute | solution.py:363
  10.9 0.1 add_relay.3
  11.0 3.5 %collective-permute-start.5 = (bf16[32,8,512]{2,1,0:T(8,128)(2,1)S(1)}, bf16[32,8,512]{2,1,0:T(8,128)(2,1)S(1)}, u32[]{:S(2)}, u32[]{:S(2)}) collective-permute-start(bf16[32,8,512]{2,1,0:T(8,128)(2,1)S(1)} %add_relay.3), channel_id=1, source_target_pairs={{0,192},{64,0},{128,64},{192,128},{1,193},{65,1},{129,65},{193,129... | collective-permute-start | bytes 786440 | tf_op jit(solution)/shard_map/ppermute | solution.py:363
  14.5 0.1 collective-permute-start
  14.6 0.0 collective-permute-done.1.refs_1_
  14.6 0.1 add_relay.2.tie_ref
  14.7 1.5 %collective-permute-start.2 = (bf16[32,8,512]{2,1,0:T(8,128)(2,1)S(1)}, bf16[32,8,512]{2,1,0:T(8,128)(2,1)S(1)}, u32[]{:S(2)}, u32[]{:S(2)}) collective-permute-start(bf16[32,8,512]{2,1,0:T(8,128)(2,1)S(1)} %add_relay.2.tie_ref), channel_id=1, source_target_pairs={{0,64},{64,128},{128,192},{192,0},{1,65},{65,129},{129,193},{193,1... | collective-permute-start | bytes 786440 | tf_op jit(solution)/shard_map/ppermute | solution.py:360
  16.1 1.6 %load_matrices.1 = (f32[512,512]{1,0:T(8,128)S(1)}, f32[512,512]{1,0:T(8,128)S(1)}) custom-call(bf16[32,8,512]{2,1,0:T(8,128)(2,1)S(1)} %add_relay.2.tie_ref, f32[512,512]{1,0:T(8,128)} %bitcast.19, f32[512,512]{1,0:T(8,128)} %bitcast.20), custom_call_target="tpu_custom_call" | custom-call | tf_op jit(solution)/shard_map/load_matrices/pallas_call | solution.py:238
  17.7 2.0 %collective-permute-done.3.refs_1_ = bf16[32,8,512]{2,1,0:T(8,128)(2,1)S(1)} collective-permute-done((bf16[32,8,512]{2,1,0:T(8,128)(2,1)S(1)}, bf16[32,8,512]{2,1,0:T(8,128)(2,1)S(1)}, u32[]{:S(2)}, u32[]{:S(2)}) %collective-permute-start.3) | collective-permute-done | bytes 262176 | tf_op jit(solution)/shard_map/ppermute | solution.py:360
  19.7 0.1 add_raw.3.refs_0_
  19.7 0.0 collective-permute-done.5.refs_1_
  19.8 3.4 %collective-permute-start.6 = (bf16[32,8,512]{2,1,0:T(8,128)(2,1)S(1)}, bf16[32,8,512]{2,1,0:T(8,128)(2,1)S(1)}, u32[]{:S(2)}, u32[]{:S(2)}) collective-permute-start(bf16[32,8,512]{2,1,0:T(8,128)(2,1)S(1)} %add_comb.1), channel_id=1, source_target_pairs={{0,1},{1,0},{2,3},{3,2},{4,5},{5,4},{6,7},{7,6},{8,9},{9,8},{10,11... | collective-permute-start | bytes 786440 | tf_op jit(solution)/shard_map/ppermute | solution.py:366
  23.2 0.9 collective-permute-done.refs_1_
  24.2 0.1 add_raw.2.partial_ref
  24.2 1.0 %collective-permute-done.2.comb_ref = bf16[32,8,512]{2,1,0:T(8,128)(2,1)S(1)} collective-permute-done((bf16[32,8,512]{2,1,0:T(8,128)(2,1)S(1)}, bf16[32,8,512]{2,1,0:T(8,128)(2,1)S(1)}, u32[]{:S(2)}, u32[]{:S(2)}) %collective-permute-start.2) | collective-permute-done | bytes 262176 | tf_op jit(solution)/shard_map/ppermute | solution.py:360
  25.3 0.0 collective-permute-done.6.other_ref
  25.3 0.1 join_cores.1
  25.3 23.8 %all_to_all.10 = bf16[32,2,8,512]{3,2,1,0:T(8,128)(2,1)S(1)} all-to-all(bf16[32,2,8,512]{3,2,1,0:T(8,128)(2,1)S(1)} %join_cores.1), channel_id=1, replica_groups={{0,2,4,6,8,10,12,14,16,18,20,22,24,26,28,30,32,34,36,38,40,42,44,46,48,..., dimensions={0} | all-to-all | bytes 1048576 | tf_op jit(solution)/shard_map/all_to_all | solution.py:370
  49.1 2.2 %owner_update.1.tie_ref = bf16[512,512]{1,0:T(8,128)(2,1)S(1)} custom-call(s32[1]{0:T(128)S(4)} %get-tuple-element.24.refresh_ref, bf16[512,512]{1,0:T(8,128)(2,1)S(1)} %bitcast.11, f32[512,512]{1,0:T(8,128)S(1)} %get-tuple-element.31.refs_2_.left_ref, f32[512,512]{1,0:T(8,128)S(1)} %get-tuple-element.34.right_ref, f32[512,512]{1,0:T(8,128)} %bitcast.14, ...), custom_call_target="tpu_custom_call" | custom-call | tf_op jit(solution)/shard_map/owner_update/pallas_call | solution.py:287
  51.3 18.8 %all_to_all.11.rows_ref = bf16[32,2,8,512]{3,2,1,0:T(8,128)(2,1)S(1)} all-to-all(bf16[32,2,8,512]{3,2,1,0:T(8,128)(2,1)S(1)} %bitcast.13), channel_id=1, replica_groups={{0,2,4,6,8,10,12,14,16,18,20,22,24,26,28,30,32,34,36,38,40,42,44,46,48,..., dimensions={0} | all-to-all | bytes 1048576 | tf_op jit(solution)/shard_map/all_to_all | solution.py:370
  70.1 6.7 %collective-permute-start.7 = (bf16[32,8,512]{2,1,0:T(8,128)(2,1)S(1)}, bf16[32,8,512]{2,1,0:T(8,128)(2,1)S(1)}, u32[]{:S(2)}, u32[]{:S(2)}) collective-permute-start(bf16[32,8,512]{2,1,0:T(8,128)(2,1)S(1)} %pick_core.3), channel_id=1, source_target_pairs={{0,1},{1,0},{2,3},{3,2},{4,5},{5,4},{6,7},{7,6},{8,9},{9,8},{10,11... | collective-permute-start | bytes 786440 | tf_op jit(solution)/shard_map/ppermute | solution.py:366
  76.9 0.0 collective-permute-start.10
  76.9 1.2 %collective-permute-done.7.refs_1_ = bf16[32,8,512]{2,1,0:T(8,128)(2,1)S(1)} collective-permute-done((bf16[32,8,512]{2,1,0:T(8,128)(2,1)S(1)}, bf16[32,8,512]{2,1,0:T(8,128)(2,1)S(1)}, u32[]{:S(2)}, u32[]{:S(2)}) %collective-permute-start.7) | collective-permute-done | bytes 262176 | tf_op jit(solution)/shard_map/ppermute | solution.py:366
  78.0 2.3 %collective-permute-start.8 = (bf16[32,8,512]{2,1,0:T(8,128)(2,1)S(1)}, bf16[32,8,512]{2,1,0:T(8,128)(2,1)S(1)}, u32[]{:S(2)}, u32[]{:S(2)}) collective-permute-start(bf16[32,8,512]{2,1,0:T(8,128)(2,1)S(1)} %collective-permute-done.7.refs_1_), channel_id=1, source_target_pairs={{0,192},{64,0},{128,64},{192,128},{1,193},{65,1},{129,65},{193,129... | collective-permute-start | bytes 786440 | tf_op jit(solution)/shard_map/ppermute | solution.py:363
  80.3 0.3 collective-permute-start.13
  80.7 1.1 %collective-permute-start.12 = (bf16[32,8,512]{2,1,0:T(8,128)(2,1)S(1)}, bf16[32,8,512]{2,1,0:T(8,128)(2,1)S(1)}, u32[]{:S(2)}, u32[]{:S(2)}) collective-permute-start(bf16[32,8,512]{2,1,0:T(8,128)(2,1)S(1)} %collective-permute-done.7.refs_1_), channel_id=1, source_target_pairs={{0,64},{64,128},{128,192},{192,0},{1,65},{65,129},{129,193},{193,1... | collective-permute-start | bytes 786440 | tf_op jit(solution)/shard_map/ppermute | solution.py:360
  81.8 4.1 %collective-permute-done.10.refs_2_ = bf16[32,8,512]{2,1,0:T(8,128)(2,1)S(1)} collective-permute-done((bf16[32,8,512]{2,1,0:T(8,128)(2,1)S(1)}, bf16[32,8,512]{2,1,0:T(8,128)(2,1)S(1)}, u32[]{:S(2)}, u32[]{:S(2)}) %collective-permute-start.10) | collective-permute-done | bytes 262176 | tf_op jit(solution)/shard_map/ppermute | solution.py:360
  85.9 0.0 collective-permute-start.11
  85.9 0.0 collective-permute-done.8.refs_3_
  85.9 3.1 %collective-permute-start.9 = (bf16[32,8,512]{2,1,0:T(8,128)(2,1)S(1)}, bf16[32,8,512]{2,1,0:T(8,128)(2,1)S(1)}, u32[]{:S(2)}, u32[]{:S(2)}) collective-permute-start(bf16[32,8,512]{2,1,0:T(8,128)(2,1)S(1)} %collective-permute-done.8.refs_3_), channel_id=1, source_target_pairs={{0,192},{64,0},{128,64},{192,128},{1,193},{65,1},{129,65},{193,129... | collective-permute-start | bytes 786440 | tf_op jit(solution)/shard_map/ppermute | solution.py:363
  89.1 4.1 %owner_factors.1 = (f32[512,512]{1,0:T(8,128)}, f32[512,512]{1,0:T(8,128)}, f32[512,512]{1,0:T(8,128)}, f32[512,512]{1,0:T(8,128)}) custom-call(bf16[32,8,512]{2,1,0:T(8,128)(2,1)S(1)} %pick_core.2.tie_ref.refs_0_, s32[1]{0:T(128)S(4)} %get-tuple-element.24.refresh_ref, bf16[512,512]{1,0:T(8,128)(2,1)S(1)} %bitcast.12, ...), custom_call_target="tpu_custom_call" | custom-call | tf_op jit(solution)/shard_map/owner_factors/pallas_call | solution.py:339
  93.2 0.0 collective-permute-done.13.refs_5_
  93.2 0.0 collective-permute-done.12.refs_4_
  93.2 1.4 %place_early.1.refs_1_ = bf16[256,8,512]{2,1,0:T(8,128)(2,1)} custom-call(s32[256]{0:T(256)S(4)} %get-tuple-element.22.index_ref, bf16[32,8,512]{2,1,0:T(8,128)(2,1)S(1)} %pick_core.2.tie_ref.refs_0_, bf16[32,8,512]{2,1,0:T(8,128)(2,1)S(1)} %collective-permute-done.7.refs_1_, bf16[32,8,512]{2,1,0:T(8,128)(2,1)S(1)} %collective-permute-done.10.refs_2_, ...), custom_call_target="tpu_custom_call" | custom-call | bytes 100663296 | tf_op jit(solution)/shard_map/place_early/pallas_call | solution.py:126
  94.6 2.6 %collective-permute-done.11.refs_0_ = bf16[32,8,512]{2,1,0:T(8,128)(2,1)S(1)} collective-permute-done((bf16[32,8,512]{2,1,0:T(8,128)(2,1)S(1)}, bf16[32,8,512]{2,1,0:T(8,128)(2,1)S(1)}, u32[]{:S(2)}, u32[]{:S(2)}) %collective-permute-start.11) | collective-permute-done | bytes 262176 | tf_op jit(solution)/shard_map/ppermute | solution.py:360
  97.2 0.7 place_over.1.refs_1_
  97.9 0.0 collective-permute-done.9.refs_0_
  97.9 0.7 place_last.1
  (3 shorter events, 0.1 us)
Async XLA Ops:
  2.3 8.6 %collective-permute-start.4 = (bf16[32,8,512]{2,1,0:T(8,128)(2,1)S(1)}, bf16[32,8,512]{2,1,0:T(8,128)(2,1)S(1)}, u32[]{:S(2)}, u32[]{:S(2)}) collective-permute-start(bf16[32,8,512]{2,1,0:T(8,128)(2,1)S(1)} %get-tuple-element.33), channel_id=1, source_target_pairs={{0,192},{64,0},{128,64},{192,128},{1,193},{65,1},{129,65},{193,129... | collective-permute-start | bytes 786440 | tf_op jit(solution)/shard_map/ppermute | solution.py:363
  6.0 8.6 %collective-permute-start.1 = (bf16[32,8,512]{2,1,0:T(8,128)(2,1)S(1)}, bf16[32,8,512]{2,1,0:T(8,128)(2,1)S(1)}, u32[]{:S(2)}, u32[]{:S(2)}) collective-permute-start(bf16[32,8,512]{2,1,0:T(8,128)(2,1)S(1)} %get-tuple-element.28), channel_id=1, source_target_pairs={{0,64},{64,128},{128,192},{192,0},{1,65},{65,129},{129,193},{193,1... | collective-permute-start | bytes 786440 | tf_op jit(solution)/shard_map/ppermute | solution.py:360
  7.0 12.6 %collective-permute-start.3 = (bf16[32,8,512]{2,1,0:T(8,128)(2,1)S(1)}, bf16[32,8,512]{2,1,0:T(8,128)(2,1)S(1)}, u32[]{:S(2)}, u32[]{:S(2)}) collective-permute-start(bf16[32,8,512]{2,1,0:T(8,128)(2,1)S(1)} %get-tuple-element.30), channel_id=1, source_target_pairs={{0,64},{64,128},{128,192},{192,0},{1,65},{65,129},{129,193},{193,1... | collective-permute-start | bytes 786440 | tf_op jit(solution)/shard_map/ppermute | solution.py:360
  11.0 8.7 %collective-permute-start.5 = (bf16[32,8,512]{2,1,0:T(8,128)(2,1)S(1)}, bf16[32,8,512]{2,1,0:T(8,128)(2,1)S(1)}, u32[]{:S(2)}, u32[]{:S(2)}) collective-permute-start(bf16[32,8,512]{2,1,0:T(8,128)(2,1)S(1)} %add_relay.3), channel_id=1, source_target_pairs={{0,192},{64,0},{128,64},{192,128},{1,193},{65,1},{129,65},{193,129... | collective-permute-start | bytes 786440 | tf_op jit(solution)/shard_map/ppermute | solution.py:363
  14.5 9.7 %collective-permute-start = (bf16[32,8,512]{2,1,0:T(8,128)(2,1)S(1)}, bf16[32,8,512]{2,1,0:T(8,128)(2,1)S(1)}, u32[]{:S(2)}, u32[]{:S(2)}) collective-permute-start(bf16[32,8,512]{2,1,0:T(8,128)(2,1)S(1)} %get-tuple-element.26), channel_id=1, source_target_pairs={{0,192},{64,0},{128,64},{192,128},{1,193},{65,1},{129,65},{193,129... | collective-permute-start | bytes 786440 | tf_op jit(solution)/shard_map/ppermute | solution.py:363
  14.7 10.6 %collective-permute-start.2 = (bf16[32,8,512]{2,1,0:T(8,128)(2,1)S(1)}, bf16[32,8,512]{2,1,0:T(8,128)(2,1)S(1)}, u32[]{:S(2)}, u32[]{:S(2)}) collective-permute-start(bf16[32,8,512]{2,1,0:T(8,128)(2,1)S(1)} %add_relay.2.tie_ref), channel_id=1, source_target_pairs={{0,64},{64,128},{128,192},{192,0},{1,65},{65,129},{129,193},{193,1... | collective-permute-start | bytes 786440 | tf_op jit(solution)/shard_map/ppermute | solution.py:360
  19.8 5.5 %collective-permute-start.6 = (bf16[32,8,512]{2,1,0:T(8,128)(2,1)S(1)}, bf16[32,8,512]{2,1,0:T(8,128)(2,1)S(1)}, u32[]{:S(2)}, u32[]{:S(2)}) collective-permute-start(bf16[32,8,512]{2,1,0:T(8,128)(2,1)S(1)} %add_comb.1), channel_id=1, source_target_pairs={{0,1},{1,0},{2,3},{3,2},{4,5},{5,4},{6,7},{7,6},{8,9},{9,8},{10,11... | collective-permute-start | bytes 786440 | tf_op jit(solution)/shard_map/ppermute | solution.py:366
  70.1 7.9 %collective-permute-start.7 = (bf16[32,8,512]{2,1,0:T(8,128)(2,1)S(1)}, bf16[32,8,512]{2,1,0:T(8,128)(2,1)S(1)}, u32[]{:S(2)}, u32[]{:S(2)}) collective-permute-start(bf16[32,8,512]{2,1,0:T(8,128)(2,1)S(1)} %pick_core.3), channel_id=1, source_target_pairs={{0,1},{1,0},{2,3},{3,2},{4,5},{5,4},{6,7},{7,6},{8,9},{9,8},{10,11... | collective-permute-start | bytes 786440 | tf_op jit(solution)/shard_map/ppermute | solution.py:366
  76.9 9.1 %collective-permute-start.10 = (bf16[32,8,512]{2,1,0:T(8,128)(2,1)S(1)}, bf16[32,8,512]{2,1,0:T(8,128)(2,1)S(1)}, u32[]{:S(2)}, u32[]{:S(2)}) collective-permute-start(bf16[32,8,512]{2,1,0:T(8,128)(2,1)S(1)} %pick_core.2.tie_ref.refs_0_), channel_id=1, source_target_pairs={{0,64},{64,128},{128,192},{192,0},{1,65},{65,129},{129,193},{193,1... | collective-permute-start | bytes 786440 | tf_op jit(solution)/shard_map/ppermute | solution.py:360
  78.0 7.9 %collective-permute-start.8 = (bf16[32,8,512]{2,1,0:T(8,128)(2,1)S(1)}, bf16[32,8,512]{2,1,0:T(8,128)(2,1)S(1)}, u32[]{:S(2)}, u32[]{:S(2)}) collective-permute-start(bf16[32,8,512]{2,1,0:T(8,128)(2,1)S(1)} %collective-permute-done.7.refs_1_), channel_id=1, source_target_pairs={{0,192},{64,0},{128,64},{192,128},{1,193},{65,1},{129,65},{193,129... | collective-permute-start | bytes 786440 | tf_op jit(solution)/shard_map/ppermute | solution.py:363
  80.3 12.9 %collective-permute-start.13 = (bf16[32,8,512]{2,1,0:T(8,128)(2,1)S(1)}, bf16[32,8,512]{2,1,0:T(8,128)(2,1)S(1)}, u32[]{:S(2)}, u32[]{:S(2)}) collective-permute-start(bf16[32,8,512]{2,1,0:T(8,128)(2,1)S(1)} %pick_core.2.tie_ref.refs_0_), channel_id=1, source_target_pairs={{0,192},{64,0},{128,64},{192,128},{1,193},{65,1},{129,65},{193,129... | collective-permute-start | bytes 786440 | tf_op jit(solution)/shard_map/ppermute | solution.py:363
  80.7 12.5 %collective-permute-start.12 = (bf16[32,8,512]{2,1,0:T(8,128)(2,1)S(1)}, bf16[32,8,512]{2,1,0:T(8,128)(2,1)S(1)}, u32[]{:S(2)}, u32[]{:S(2)}) collective-permute-start(bf16[32,8,512]{2,1,0:T(8,128)(2,1)S(1)} %collective-permute-done.7.refs_1_), channel_id=1, source_target_pairs={{0,64},{64,128},{128,192},{192,0},{1,65},{65,129},{129,193},{193,1... | collective-permute-start | bytes 786440 | tf_op jit(solution)/shard_map/ppermute | solution.py:360
  85.9 11.2 %collective-permute-start.11 = (bf16[32,8,512]{2,1,0:T(8,128)(2,1)S(1)}, bf16[32,8,512]{2,1,0:T(8,128)(2,1)S(1)}, u32[]{:S(2)}, u32[]{:S(2)}) collective-permute-start(bf16[32,8,512]{2,1,0:T(8,128)(2,1)S(1)} %collective-permute-done.10.refs_2_), channel_id=1, source_target_pairs={{0,64},{64,128},{128,192},{192,0},{1,65},{65,129},{129,193},{193,1... | collective-permute-start | bytes 786440 | tf_op jit(solution)/shard_map/ppermute | solution.py:360
  85.9 12.0 %collective-permute-start.9 = (bf16[32,8,512]{2,1,0:T(8,128)(2,1)S(1)}, bf16[32,8,512]{2,1,0:T(8,128)(2,1)S(1)}, u32[]{:S(2)}, u32[]{:S(2)}) collective-permute-start(bf16[32,8,512]{2,1,0:T(8,128)(2,1)S(1)} %collective-permute-done.8.refs_3_), channel_id=1, source_target_pairs={{0,192},{64,0},{128,64},{192,128},{1,193},{65,1},{129,65},{193,129... | collective-permute-start | bytes 786440 | tf_op jit(solution)/shard_map/ppermute | solution.py:363
